TPU v7x, 256 devices: a whole 4x4x8 slice. The times are simulated.
256 devices in a mesh: src: 32 (over z, x), tgt: 8 (over y, core).
Axes of the slice: x: 4, y: 4, z: 8, core: 2. Of those that a mesh axis runs over, the one named last changes fastest.
Arguments:
- sources: bfloat16 [65536, 768], P('src'), may hold values from -24 to 24
- targets: bfloat16 [32768, 768], P('tgt'), may hold values from -24 to 24
- block_lists: int32 [256, 8, 4], P('src', 'tgt'), may hold values from 0 to 15, as said below
- live_counts: int32 [256, 8], P('src', 'tgt'), may hold values from 1 to 4, as said below
Outputs:
- mapped_rows: float32 [65536, 768], P(('src', 'tgt'))
- row_potential: float32 [65536], P('src')
- col_potential: float32 [32768], P('tgt')
Inputs may be any that keep to these rules, and one draw needn't show every extreme that they name: `block_lists`: entries of a list at one (b, t) are distinct block numbers within shard t; every target block of every shard is the first entry of the list of some source block. `live_counts`: some list is full in every draw.
All inputs are finite; a program needn't handle non-finite values.
Results may differ from a plain program's by a relative error of at most 0.007.
Values sent between devices are 32-bit elements; how exact they have to be, the bound alone decides.
No kernel may reach another device: no remote copies, remote signals or barrier semaphores. Data moves between devices by JAX's collectives and lax.ppermute only.
A program may use at most 128 MiB of HBM per device.

v0:
```python
import math

import jax
import jax.numpy as jnp
from jax import lax
from jax.sharding import PartitionSpec as P

BLK = 256
ITERS = 3


EPSILON = 0.1
NEGATIVE = -1e30


def row_logsum(tile_cost, col_tiles, live_mask):
    scores = jnp.where(live_mask, (col_tiles[:, :, None, :] - tile_cost) / EPSILON, NEGATIVE)
    local_peak = jnp.max(scores, axis=(1, 3))
    peak = lax.pmax(local_peak, "tgt")
    local_sum = jnp.sum(jnp.exp(scores - peak[:, None, :, None]), axis=(1, 3))
    summed = lax.psum(local_sum, "tgt")
    return (scores, peak + jnp.log(summed))


def col_logsum(tile_cost, row_potential, live_mask, onehot, slot_block):
    scores = jnp.where(live_mask, (row_potential[:, None, :, None] - tile_cost) / EPSILON, NEGATIVE)
    tile_max = jnp.max(scores, axis=2)
    local_peak = jnp.max(
        jnp.where(onehot[:, :, :, None], tile_max[:, :, None, :], NEGATIVE), axis=(0, 1)
    )
    peak = lax.pmax(local_peak, "src")
    shifted = peak[slot_block]
    tile_sum = jnp.sum(jnp.exp(scores - shifted[:, :, None, :]), axis=2)
    summed = lax.psum(
        jnp.sum(jnp.where(onehot[:, :, :, None], tile_sum[:, :, None, :], 0.0), axis=(0, 1)), "src"
    )
    return peak + jnp.log(summed)


def local(sources, targets, block_lists, live_counts):
    src_rows, features = sources.shape
    src_blocks = src_rows // BLK
    tgt_blocks = targets.shape[0] // BLK
    slot_count = block_lists.shape[2]
    slot_block = block_lists[:, 0, :]
    live_slot = jnp.arange(slot_count, dtype=jnp.int32)[None, :] < live_counts
    onehot = (
        slot_block[:, :, None] == jnp.arange(tgt_blocks, dtype=jnp.int32)[None, None, :]
    ) & live_slot[:, :, None]
    live_mask = live_slot[:, :, None, None]
    tgt_blocked = targets.reshape(tgt_blocks, BLK, features)
    tile_targets = tgt_blocked[slot_block]
    src_blocked = sources.reshape(src_blocks, BLK, features)
    src_square = jnp.sum(jnp.square(sources.astype(jnp.float32)), -1).reshape(src_blocks, BLK)
    tgt_square = jnp.sum(jnp.square(targets.astype(jnp.float32)), -1).reshape(tgt_blocks, BLK)[
        slot_block
    ]
    cross_term = jnp.einsum(
        "brd,bkcd->bkrc", src_blocked, tile_targets, preferred_element_type=jnp.float32
    )
    tile_cost = (
        src_square[:, None, :, None] + tgt_square[:, :, None, :] - 2.0 * cross_term
    ) / features
    log_src_mass = math.log(src_rows * lax.axis_size("src"))
    log_tgt_mass = math.log(targets.shape[0] * lax.axis_size("tgt"))
    col_potential = jnp.zeros((tgt_blocks, BLK), jnp.float32)
    row_potential = jnp.zeros((src_blocks, BLK), jnp.float32)
    for sweep in range(ITERS):
        scores, row_lse = row_logsum(tile_cost, col_potential[slot_block], live_mask)
        row_potential = -EPSILON * log_src_mass - EPSILON * row_lse
        col_lse = col_logsum(tile_cost, row_potential, live_mask, onehot, slot_block)
        col_potential = -EPSILON * log_tgt_mass - EPSILON * col_lse
    scores, final_lse = row_logsum(tile_cost, col_potential[slot_block], live_mask)
    weights = jnp.where(live_mask, jnp.exp(scores - final_lse[:, None, :, None]), 0.0).astype(
        jnp.bfloat16
    )
    numerator = jnp.einsum(
        "bkrc,bkcd->brd", weights, tile_targets, preferred_element_type=jnp.float32
    ).reshape(src_rows, features)
    summed_all = lax.psum(numerator, "tgt")
    row_share = src_rows // lax.axis_size("tgt")
    mapped = lax.dynamic_slice_in_dim(summed_all, lax.axis_index("tgt") * row_share, row_share, 0)
    return (mapped, row_potential.reshape(src_rows), col_potential.reshape(tgt_blocks * BLK))


def solution(mesh):
    in_specs = (P("src", None), P("tgt", None), P("src", "tgt", None), P("src", "tgt"))
    out_specs = (P(("src", "tgt"), None), P("src"), P("tgt"))
    return jax.shard_map(local, mesh=mesh, in_specs=in_specs, out_specs=out_specs, check_vma=False)
```

profile of v0, /device:TPU:1, one launch (start us, length us, event | category | flops | bytes accessed | tf_op | source)
XLA Modules:
  0.0 1140.3 jit_solution(17579513966267825080)
XLA Ops:
  7.2 0.7 iota_compare_fusion.1
  7.9 0.7 compare_select_fusion
  8.8 4.1 multiply_reduce_fusion
  12.9 9.6 gather_fusion.2
  22.5 0.6 gather_fusion
  23.2 0.6 gather_fusion.1
  23.8 0.7 multiply_reduce_fusion.1
  24.5 9.5 fusion.1
  34.1 15.2 %pmax.49 = f32[8,256]{1,0:T(8,128)S(1)} all-reduce(f32[8,256]{1,0:T(8,128)S(1)} %get-tuple-element.3), channel_id=1, replica_groups=mesh['src'=32,'tgt'=8] {'tgt'}, use_global_device_ids=true, to_apply=%region_3.4 | all-reduce | flops 2048 | bytes 16384 | tf_op jit(solution)/shard_map/pmax | solution.py:19
  49.3 4.6 exponential_reduce_fusion.6
  53.9 13.4 %psum.56 = f32[8,256]{1,0:T(8,128)S(1)} all-reduce(f32[8,256]{1,0:T(8,128)S(1)} %exponential_reduce_fusion.6), channel_id=1, replica_groups=mesh['src'=32,'tgt'=8] {'tgt'}, use_global_device_ids=true, to_apply=%region_5.6 | all-reduce | flops 2048 | bytes 16384 | tf_op jit(solution)/shard_map/psum | solution.py:21
  67.3 4.7 fusion.2
  72.1 0.1 select_reduce_fusion.5
  72.3 118.4 %pmax.50 = f32[16,256]{1,0:T(8,128)S(1)} all-reduce(f32[16,256]{1,0:T(8,128)S(1)} %select_reduce_fusion.5), channel_id=1, replica_groups=mesh['src'=32,'tgt'=8] {'src'}, use_global_device_ids=true, to_apply=%region_8.9 | all-reduce | flops 4096 | bytes 32768 | tf_op jit(solution)/shard_map/pmax | solution.py:31
  190.7 0.6 gather_fusion.3
  191.3 5.2 exponential_reduce_fusion.5
  196.6 109.9 %psum.57 = f32[16,256]{1,0:T(8,128)S(1)} all-reduce(f32[16,256]{1,0:T(8,128)S(1)} %select_reduce_fusion.4), channel_id=1, replica_groups=mesh['src'=32,'tgt'=8] {'src'}, use_global_device_ids=true, to_apply=%region_11.12 | all-reduce | flops 4096 | bytes 32768 | tf_op jit(solution)/shard_map/psum | solution.py:34
  306.6 0.6 gather_fusion.4
  307.2 4.1 fusion.3
  311.3 68.0 %pmax.51 = f32[8,256]{1,0:T(8,128)S(1)} all-reduce(f32[8,256]{1,0:T(8,128)S(1)} %fusion.3), channel_id=1, replica_groups=mesh['src'=32,'tgt'=8] {'tgt'}, use_global_device_ids=true, to_apply=%region_13.14 | all-reduce | flops 2048 | bytes 16384 | tf_op jit(solution)/shard_map/pmax | solution.py:19
  379.3 4.6 exponential_reduce_fusion.4
  384.0 12.7 %psum.58 = f32[8,256]{1,0:T(8,128)S(1)} all-reduce(f32[8,256]{1,0:T(8,128)S(1)} %exponential_reduce_fusion.4), channel_id=1, replica_groups=mesh['src'=32,'tgt'=8] {'tgt'}, use_global_device_ids=true, to_apply=%region_15.16 | all-reduce | flops 2048 | bytes 16384 | tf_op jit(solution)/shard_map/psum | solution.py:21
  396.6 4.7 fusion.4
  401.5 109.9 %pmax.52 = f32[16,256]{1,0:T(8,128)S(1)} all-reduce(f32[16,256]{1,0:T(8,128)S(1)} %select_reduce_fusion.3), channel_id=1, replica_groups=mesh['src'=32,'tgt'=8] {'src'}, use_global_device_ids=true, to_apply=%region_18.19 | all-reduce | flops 4096 | bytes 32768 | tf_op jit(solution)/shard_map/pmax | solution.py:31
  511.4 0.6 gather_fusion.5
  512.0 5.2 exponential_reduce_fusion.3
  517.2 0.1 select_reduce_fusion.2
  517.3 110.3 %psum.59 = f32[16,256]{1,0:T(8,128)S(1)} all-reduce(f32[16,256]{1,0:T(8,128)S(1)} %select_reduce_fusion.2), channel_id=1, replica_groups=mesh['src'=32,'tgt'=8] {'src'}, use_global_device_ids=true, to_apply=%region_21.22 | all-reduce | flops 4096 | bytes 32768 | tf_op jit(solution)/shard_map/psum | solution.py:34
  627.6 0.6 gather_fusion.6
  628.2 4.1 fusion.5
  632.4 67.8 %pmax.53 = f32[8,256]{1,0:T(8,128)S(1)} all-reduce(f32[8,256]{1,0:T(8,128)S(1)} %fusion.5), channel_id=1, replica_groups=mesh['src'=32,'tgt'=8] {'tgt'}, use_global_device_ids=true, to_apply=%region_23.24 | all-reduce | flops 2048 | bytes 16384 | tf_op jit(solution)/shard_map/pmax | solution.py:19
  700.2 4.6 exponential_reduce_fusion.2
  704.8 12.7 %psum.60 = f32[8,256]{1,0:T(8,128)S(1)} all-reduce(f32[8,256]{1,0:T(8,128)S(1)} %exponential_reduce_fusion.2), channel_id=1, replica_groups=mesh['src'=32,'tgt'=8] {'tgt'}, use_global_device_ids=true, to_apply=%region_25.26 | all-reduce | flops 2048 | bytes 16384 | tf_op jit(solution)/shard_map/psum | solution.py:21
  717.5 4.7 fusion.6
  722.3 109.9 %pmax.54 = f32[16,256]{1,0:T(8,128)S(1)} all-reduce(f32[16,256]{1,0:T(8,128)S(1)} %select_reduce_fusion.1), channel_id=1, replica_groups=mesh['src'=32,'tgt'=8] {'src'}, use_global_device_ids=true, to_apply=%region_28.29 | all-reduce | flops 4096 | bytes 32768 | tf_op jit(solution)/shard_map/pmax | solution.py:31
  832.3 0.6 gather_fusion.7
  832.9 5.2 exponential_reduce_fusion.1
  838.2 110.3 %psum.61 = f32[16,256]{1,0:T(8,128)S(1)} all-reduce(f32[16,256]{1,0:T(8,128)S(1)} %select_reduce_fusion), channel_id=1, replica_groups=mesh['src'=32,'tgt'=8] {'src'}, use_global_device_ids=true, to_apply=%region_31.32 | all-reduce | flops 4096 | bytes 32768 | tf_op jit(solution)/shard_map/psum | solution.py:34
  948.5 0.6 gather_fusion.8
  949.1 4.1 fusion.7
  953.3 68.0 %pmax.55 = f32[8,256]{1,0:T(8,128)S(1)} all-reduce(f32[8,256]{1,0:T(8,128)S(1)} %fusion.7), channel_id=1, replica_groups=mesh['src'=32,'tgt'=8] {'tgt'}, use_global_device_ids=true, to_apply=%region_33.34 | all-reduce | flops 2048 | bytes 16384 | tf_op jit(solution)/shard_map/pmax | solution.py:19
  1021.3 4.6 exponential_reduce_fusion
  1025.9 12.7 %psum.62 = f32[8,256]{1,0:T(8,128)S(1)} all-reduce(f32[8,256]{1,0:T(8,128)S(1)} %exponential_reduce_fusion), channel_id=1, replica_groups=mesh['src'=32,'tgt'=8] {'tgt'}, use_global_device_ids=true, to_apply=%region_35.36 | all-reduce | flops 2048 | bytes 16384 | tf_op jit(solution)/shard_map/psum | solution.py:21
  1038.6 11.1 fusion.8
  1049.7 0.6 copy.20
  1050.3 0.6 copy.19
  1050.9 80.5 %all-reduce.2.cloned.1.call-done = f32[2048,768]{1,0:T(8,128)} async-done(((f32[2048,768]{1,0:T(8,128)}), f32[2048,768]{1,0:T(8,128)}) %all-reduce.2.cloned.1.call-update) | async-done | bytes 6291472 | tf_op jit(solution)/shard_map/psum | solution.py:80
  1131.4 2.1 constant_dynamic-slice_fusion
  (33 shorter events, 1.1 us)
Async XLA Ops:
  7.2 1124.2 %all-reduce.2.cloned.1.call-start = ((), (), s32[]{:S(2)}) async-start(), calls=%async_computation | async-start | bytes 12582912 | tf_op jit(solution)/shard_map/psum | solution.py:80
  12.9 10.9 copy-start
  49.3 22.7 %copy-start.1 = (s32[8,1,4]{0,2,1:T(4,128)S(1)}, s32[8,1,4]{0,2,1:T(4,128)}, u32[]{:S(2)}) copy-start(s32[8,1,4]{0,2,1:T(4,128)} %param.6) | copy-start | bytes 388
Sparse Core Ops, SparseCore 0:
  1049.8 81.5 all-reduce.1
where the time goes:
time: 1140 us
  blocking collectives  939 us (82%)
  waiting for transfers between devices  80.5 us (7%)
  other arithmetic  67.5 us (6%)
  matrix products  20.6 us (2%)
  local copies, waits for them, and re-layouts  18.1 us (2%)
  between operations  14.4 us (1%)
    pmax x3, blocking collectives, col_logsum(): peak = lax.pmax(local_peak, 'src')  338 us
    psum x3, blocking collectives, col_logsum(): lax.psum(jnp.sum(jnp.where(onehot[:, :, :, None], tile_sum[:, :, None, :]...  331 us
    pmax x4, blocking collectives, row_logsum(): peak = lax.pmax(local_peak, 'tgt')  219 us
    psum x1, waiting for transfers between devices, local(): summed_all = lax.psum(numerator, 'tgt')  80.5 us
    psum x4, blocking collectives, row_logsum(): summed = lax.psum(local_sum, 'tgt')  51.4 us
  transfers between devices with their start and end apart: 1, of which 1 were waited for; matrix products, arithmetic and copies ran while one was open for 0% of the time, Pallas kernels for 0%

commit v1 on v0

v1 whole, which is shorter than its diff:
```python
import functools
import math

import jax
import jax.numpy as jnp
from jax import lax
from jax.experimental import pallas as pl
from jax.experimental.pallas import tpu as pltpu
from jax.sharding import PartitionSpec as P

BLK = 256
ITERS = 3
EPSILON = 0.1
NEGATIVE = -1e30
LOG2E = math.log2(math.e)
LN2 = math.log(2.0)
LANES = 128

VMEM = pl.BlockSpec(memory_space=pltpu.VMEM)
SMEM = pl.BlockSpec(memory_space=pltpu.SMEM)
ANY = pl.BlockSpec(memory_space=pl.ANY)
PARAMS = pltpu.CompilerParams(vmem_limit_bytes=40 * 1024 * 1024)


def eye():
    shape = (LANES, LANES)
    return lax.broadcasted_iota(jnp.int32, shape, 0) == lax.broadcasted_iota(jnp.int32, shape, 1)


def to_lanes(column):
    mask = eye()
    halves = [
        jnp.sum(jnp.where(mask, column[h * LANES : (h + 1) * LANES], 0.0), axis=0, keepdims=True)
        for h in range(BLK // LANES)
    ]
    return jnp.concatenate(halves, axis=1)


def to_sublanes(row):
    mask = eye()
    halves = [
        jnp.sum(jnp.where(mask, row[:, h * LANES : (h + 1) * LANES], 0.0), axis=1, keepdims=True)
        for h in range(BLK // LANES)
    ]
    return jnp.concatenate(halves, axis=0)


def fold_rows(tile, op):
    out = tile[0:8]
    for r in range(8, BLK, 8):
        out = op(out, tile[r : r + 8])
    return out


def merge_lse(ref):
    values = ref[...]
    peak = jnp.max(values, axis=0)
    return peak + jnp.log2(jnp.sum(jnp.exp2(values - peak[None]), axis=0))


def cost_kernel(lists, counts, src_hbm, tgt_hbm, tgt, z_ref, rows, src, bias, sems, *, features):
    tgt_blocks, src_blocks = tgt.shape[0], src.shape[0]
    src_copies = [
        pltpu.make_async_copy(src_hbm.at[b], src.at[b], sems.at[tgt_blocks + b])
        for b in range(src_blocks)
    ]
    tgt_copies = [
        pltpu.make_async_copy(tgt_hbm.at[t], tgt.at[t], sems.at[t]) for t in range(tgt_blocks)
    ]
    for copy in tgt_copies:
        copy.start()
    for copy in src_copies:
        copy.start()
    scale = LOG2E / (features * EPSILON)
    mask = eye()
    for t in range(tgt_blocks):
        tgt_copies[t].wait()
        for h in range(BLK // LANES):
            part = tgt[t, h * LANES : (h + 1) * LANES, :]
            gram = lax.dot_general(
                part, part, (((1,), (1,)), ((), ())), preferred_element_type=jnp.float32
            )
            square = jnp.sum(jnp.where(mask, gram, 0.0), axis=0, keepdims=True)
            bias[t : t + 1, h * LANES : (h + 1) * LANES] = -scale * square
    for b in range(src_blocks):
        src_copies[b].wait()

        def score(k, peak, b=b):
            t = lists[b, k]
            cross = lax.dot_general(
                src[b], tgt[t], (((1,), (1,)), ((), ())), preferred_element_type=jnp.float32
            )
            z = (2.0 * scale) * cross + bias[pl.ds(t, 1), :]
            z_ref[b, k] = z
            return jnp.maximum(peak, jnp.maximum(z[:, :LANES], z[:, LANES:]))

        count = counts[b]
        peak = lax.fori_loop(0, count, score, jnp.full((BLK, LANES), NEGATIVE, jnp.float32))
        peak = jnp.max(peak, axis=1, keepdims=True)

        def total(k, acc, b=b, peak=peak):
            e = jnp.exp2(z_ref[b, k] - peak)
            return acc + e[:, :LANES] + e[:, LANES:]

        acc = lax.fori_loop(0, count, total, jnp.zeros((BLK, LANES), jnp.float32))
        lse = peak + jnp.log2(jnp.sum(acc, axis=1, keepdims=True))
        rows[b : b + 1, :] = to_lanes(lse)


def first_col_kernel(lists, counts, z_ref, row_parts, w_ref, row_lse, cols, peaks, sums):
    src_blocks, tgt_blocks = z_ref.shape[0], cols.shape[0]
    row_lse[...] = merge_lse(row_parts)
    peaks[...] = jnp.full(peaks.shape, NEGATIVE, jnp.float32)
    sums[...] = jnp.zeros(sums.shape, jnp.float32)
    for b in range(src_blocks):
        shift = to_sublanes(row_lse[b : b + 1, :])

        def shifted(k, carry, b=b, shift=shift):
            t = lists[b, k]
            w = z_ref[b, k] - shift
            w_ref[b, k] = w
            peaks[t] = jnp.maximum(peaks[t], fold_rows(w, jnp.maximum))
            return carry

        lax.fori_loop(0, counts[b], shifted, 0)
    for t in range(tgt_blocks):
        peaks[t] = jnp.broadcast_to(jnp.max(peaks[t], axis=0, keepdims=True), (8, BLK))
    for b in range(src_blocks):

        def summed(k, carry, b=b):
            t = lists[b, k]
            e = jnp.exp2(w_ref[b, k] - peaks[t, 0:1, :])
            sums[t] += fold_rows(e, jnp.add)
            return carry

        lax.fori_loop(0, counts[b], summed, 0)
    for t in range(tgt_blocks):
        total = jnp.sum(sums[t], axis=0, keepdims=True)
        lse = peaks[t, 0:1, :] + jnp.log2(total)
        cols[t : t + 1, :] = jnp.where(total > 0.0, lse, NEGATIVE)


def row_totals(lists, counts, tile, rows, src_blocks):
    for b in range(src_blocks):

        def total(k, acc, b=b):
            q = tile(b, k, lists[b, k])
            return acc + q[:, :LANES] + q[:, LANES:]

        acc = lax.fori_loop(0, counts[b], total, jnp.zeros((BLK, LANES), jnp.float32))
        rows[b : b + 1, :] = to_lanes(jnp.sum(acc, axis=1, keepdims=True))


def first_row_kernel(lists, counts, w_ref, col_parts, q_ref, col_lse, rows):
    col_lse[...] = merge_lse(col_parts)

    def tile(b, k, t):
        q = jnp.exp2(w_ref[b, k] - col_lse[pl.ds(t, 1), :])
        q_ref[b, k] = q
        return q

    row_totals(lists, counts, tile, rows, w_ref.shape[0])


def col_kernel(lists, counts, q_ref, row_parts, row_scale, cols, sums, *, share):
    src_blocks, tgt_blocks = q_ref.shape[0], cols.shape[0]
    row_scale[...] = share / jnp.sum(row_parts[...], axis=0)
    sums[...] = jnp.zeros(sums.shape, jnp.float32)
    for b in range(src_blocks):
        scale = to_sublanes(row_scale[b : b + 1, :])

        def summed(k, carry, b=b, scale=scale):
            t = lists[b, k]
            sums[t] += fold_rows(q_ref[b, k] * scale, jnp.add)
            return carry

        lax.fori_loop(0, counts[b], summed, 0)
    for t in range(tgt_blocks):
        cols[t : t + 1, :] = jnp.sum(sums[t], axis=0, keepdims=True)


def row_kernel(lists, counts, q_ref, col_parts, col_scale, rows):
    col_scale[...] = 1.0 / jnp.sum(col_parts[...], axis=0)

    def tile(b, k, t):
        return q_ref[b, k] * col_scale[pl.ds(t, 1), :]

    row_totals(lists, counts, tile, rows, q_ref.shape[0])


def project_kernel(lists, counts, q_ref, col_parts, tgt, col_scale, out, rows):
    col_scale[...] = 1.0 / jnp.sum(col_parts[...], axis=0)
    for b in range(q_ref.shape[0]):

        def project(k, acc, b=b):
            t = lists[b, k]
            weights = q_ref[b, k] * col_scale[pl.ds(t, 1), :]
            part = jnp.dot(
                weights.astype(jnp.bfloat16), tgt[t], preferred_element_type=jnp.float32
            )

            @pl.when(k == 0)
            def _():
                out[b] = part

            @pl.when(k > 0)
            def _():
                out[b] += part

            return acc + weights[:, :LANES] + weights[:, LANES:]

        acc = lax.fori_loop(0, counts[b], project, jnp.zeros((BLK, LANES), jnp.float32))
        rows[b : b + 1, :] = to_lanes(jnp.sum(acc, axis=1, keepdims=True))


def in_vmem(x):
    return pltpu.with_memory_space_constraint(x, pltpu.VMEM)


def f32(*shape):
    return jax.ShapeDtypeStruct(shape, jnp.float32)


def gather(x, axis):
    n = lax.axis_size(axis)
    return lax.all_to_all(jnp.broadcast_to(x[None], (n, *x.shape)), axis, 0, 0)


def local(sources, targets, block_lists, live_counts):
    src_rows, features = sources.shape
    src_blocks = src_rows // BLK
    tgt_blocks = targets.shape[0] // BLK
    slots = block_lists.shape[2]
    lists = block_lists[:, 0, :]
    counts = live_counts[:, 0]
    total_src = src_rows * lax.axis_size("src")
    total_tgt = targets.shape[0] * lax.axis_size("tgt")
    src_blocked = sources.reshape(src_blocks, BLK, features)
    tgt_blocked = targets.reshape(tgt_blocks, BLK, features)
    tiles = pltpu.VMEM((src_blocks, slots, BLK, BLK), jnp.float32)
    row_shape, col_shape = f32(src_blocks, BLK), f32(tgt_blocks, BLK)
    col_scratch = pltpu.VMEM((tgt_blocks, 8, BLK), jnp.float32)

    tgt_vmem, z, rows = pl.pallas_call(
        functools.partial(cost_kernel, features=features),
        in_specs=[SMEM, SMEM, ANY, ANY],
        out_specs=[VMEM, VMEM, VMEM],
        out_shape=[pltpu.VMEM(tgt_blocked.shape, jnp.bfloat16), tiles, row_shape],
        scratch_shapes=[
            pltpu.VMEM(src_blocked.shape, jnp.bfloat16),
            pltpu.VMEM((tgt_blocks, BLK), jnp.float32),
            pltpu.SemaphoreType.DMA((tgt_blocks + src_blocks,)),
        ],
        compiler_params=PARAMS,
    )(lists, counts, src_blocked, tgt_blocked)

    w, row_lse, cols = pl.pallas_call(
        first_col_kernel,
        in_specs=[SMEM, SMEM, VMEM, VMEM],
        out_specs=[VMEM, VMEM, VMEM],
        out_shape=[tiles, row_shape, col_shape],
        scratch_shapes=[col_scratch, col_scratch],
        input_output_aliases={2: 0},
        compiler_params=PARAMS,
    )(lists, counts, in_vmem(z), gather(rows, "tgt"))

    q, col_lse, rows = pl.pallas_call(
        first_row_kernel,
        in_specs=[SMEM, SMEM, VMEM, VMEM],
        out_specs=[VMEM, VMEM, VMEM],
        out_shape=[tiles, col_shape, row_shape],
        input_output_aliases={2: 0},
        compiler_params=PARAMS,
    )(lists, counts, in_vmem(w), gather(cols, "src"))
    q = in_vmem(q)

    for sweep in range(1, ITERS):
        row_scale, cols = pl.pallas_call(
            functools.partial(col_kernel, share=total_tgt / total_src),
            in_specs=[SMEM, SMEM, VMEM, VMEM],
            out_specs=[VMEM, VMEM],
            out_shape=[row_shape, col_shape],
            scratch_shapes=[col_scratch],
            compiler_params=PARAMS,
        )(lists, counts, q, gather(rows, "tgt"))
        col_parts = gather(cols, "src")
        if sweep < ITERS - 1:
            col_scale, rows = pl.pallas_call(
                row_kernel,
                in_specs=[SMEM, SMEM, VMEM, VMEM],
                out_specs=[VMEM, VMEM],
                out_shape=[col_shape, row_shape],
                compiler_params=PARAMS,
            )(lists, counts, q, col_parts)

    col_scale, numerator, rows = pl.pallas_call(
        project_kernel,
        in_specs=[SMEM, SMEM, VMEM, VMEM, VMEM],
        out_specs=[VMEM, VMEM, VMEM],
        out_shape=[col_shape, f32(src_blocks, BLK, features), row_shape],
        compiler_params=PARAMS,
    )(lists, counts, q, col_parts, in_vmem(tgt_vmem))

    mass = lax.psum_scatter(rows, "tgt", scatter_dimension=0, tiled=True)
    share = lax.psum_scatter(numerator.reshape(src_rows, features), "tgt", tiled=True)
    mapped = share / mass.reshape(BLK, 1)

    src_square = jnp.sum(jnp.square(sources.astype(jnp.float32)), -1)
    row_potential = (
        EPSILON * (jnp.log(row_scale) - LN2 * row_lse - math.log(total_src))
    ).reshape(src_rows) + src_square / features
    col_potential = EPSILON * (
        jnp.log(col_scale) - LN2 * col_lse + (math.log(total_src) - math.log(total_tgt))
    )
    return (mapped, row_potential, col_potential.reshape(tgt_blocks * BLK))


def solution(mesh):
    in_specs = (P("src", None), P("tgt", None), P("src", "tgt", None), P("src", "tgt"))
    out_specs = (P(("src", "tgt"), None), P("src"), P("tgt"))
    return jax.shard_map(local, mesh=mesh, in_specs=in_specs, out_specs=out_specs, check_vma=False)
```

time: 1140 us -> 200 us (0.18)
  blocking collectives: 939 us -> 118 us
  other arithmetic: 67.5 us -> 3.44 us
  waiting for transfers between devices: 80.5 us -> 23.8 us
  Pallas kernels: 0 us -> 34.6 us
  matrix products: 20.6 us -> 0 us
  local copies, waits for them, and re-layouts: 18.1 us -> 5.26 us
    pmax x7 -> x0, blocking collectives: 557 us -> none  [the longest x3 338 us: col_logsum(): peak = lax.pmax(local_peak, 'src')]
    psum x7 -> x0, blocking collectives: 382 us -> none  [the longest x3 331 us: col_logsum(): lax.psum(jnp.sum(jnp.where(onehot[:, :, :, None], tile_sum[:, :, None, :]...]
    all_to_all x0 -> x6, blocking collectives: none -> 102 us  [gather(): return lax.all_to_all(jnp.broadcast_to(x[None], (n, *x.shape)), axis, 0, 0)]
    psum x1 -> x0, waiting for transfers between devices: 80.5 us -> none  [local(): summed_all = lax.psum(numerator, 'tgt')]
    reduce_sum x12 -> x1, other arithmetic: 39.1 us -> 0.68 us  [local(): src_square = jnp.sum(jnp.square(sources.astype(jnp.float32)), -1)]
    pallas_call x0 -> x7, Pallas kernels: none -> 34.6 us  [the longest x1 12.8 us: local(): pl.pallas_call(functools.partial(cost_kernel, features=features), in_spec...]
    reduce_max x9 -> x0, other arithmetic: 26.8 us -> none  [the longest x3 14 us: col_logsum(): tile_max = jnp.max(scores, axis=2)]
    reduce_scatter x0 -> x1, waiting for transfers between devices: none -> 23.8 us  [local(): lax.psum_scatter(numerator.reshape(src_rows, features), 'tgt', tiled=True)]
  transfers between devices with their start and end apart: 1 -> 1, of which waited for: 1 -> 1; matrix products, arithmetic and copies ran while one was open for 0% -> 2% of each run, Pallas kernels for 0% -> 0%
where the time goes in v1:
time: 200 us
  blocking collectives  118 us (59%)
  Pallas kernels  34.6 us (17%)
  waiting for transfers between devices  23.8 us (12%)
  between operations  14.2 us (7%)
  local copies, waits for them, and re-layouts  5.26 us (3%)
  other arithmetic  3.44 us (2%)
    all_to_all x6, blocking collectives, gather(): return lax.all_to_all(jnp.broadcast_to(x[None], (n, *x.shape)), axis, 0, 0)  102 us
    reduce_scatter x1, waiting for transfers between devices, local(): lax.psum_scatter(numerator.reshape(src_rows, features), 'tgt', tiled=True)  23.8 us
    unnamed x1, blocking collectives  16.6 us
    pallas_call x1, Pallas kernels, local(): pl.pallas_call(functools.partial(cost_kernel, features=features), in_spec...  12.8 us
    pallas_call x1, Pallas kernels, local(): pl.pallas_call(project_kernel, in_specs=[SMEM, SMEM, VMEM, VMEM, VMEM], o...  8.13 us
    pallas_call x2, Pallas kernels, local(): pl.pallas_call(functools.partial(col_kernel, share=total_tgt / total_src)...  5.72 us
  transfers between devices with their start and end apart: 1, of which 1 were waited for; matrix products, arithmetic and copies ran while one was open for 2% of the time, Pallas kernels for 0%

profile of v1, /device:TPU:1, one launch (start us, length us, event | category | flops | bytes accessed | tf_op | source)
XLA Modules:
  0.0 199.6 jit_solution(7268270820873008311)
XLA Ops:
  7.2 0.0 copy-start.1
  7.2 0.0 reduce-scatter.2.cloned.1.call-start
  7.2 1.3 copy.22.lists
  8.6 0.0 copy-start
  8.6 12.8 %shard_map.67 = (bf16[16,256,768]{2,1,0:T(8,128)(2,1)S(1)}, f32[8,4,256,256]{3,2,1,0:T(8,128)S(1)}, f32[8,256]{1,0:T(8,128)}) custom-call(s32[8,4]{1,0:T(8,128)} %copy.22.lists, s32[8]{0:T(128)} %bitcast.13, bf16[8,256,768]{2,1,0:T(8,128)(2,1)} %bitcast.20, bf16[16,256,768]{2,1,0:T(8,128)(2,1)} %bitcast.21), custom_call_target="tpu_custom_call" | custom-call | tf_op jit(solution)/shard_map/pallas_call | solution.py:244
  21.3 0.7 broadcast_in_dim.12
  22.0 13.2 %all_to_all.30.row_parts = f32[8,8,256]{2,1,0:T(8,128)S(1)} all-to-all(f32[8,8,256]{2,1,0:T(8,128)S(1)} %broadcast_in_dim.12), channel_id=1, replica_groups=mesh['src'=32,'tgt'=8] {'tgt'}, dimensions={0} | all-to-all | bytes 131072 | tf_op jit(solution)/shard_map/all_to_all | solution.py:226
  35.2 0.0 copy-done.1
  35.2 0.0 copy-done
  35.2 3.3 %shard_map.68 = (f32[8,4,256,256]{3,2,1,0:T(8,128)S(1)}, f32[8,256]{1,0:T(8,128)S(1)}, f32[16,256]{1,0:T(8,128)S(1)}) custom-call(s32[8,4]{1,0:T(8,128)S(1)} %copy-done, s32[8]{0:T(128)S(1)} %bitcast.15, f32[8,4,256,256]{3,2,1,0:T(8,128)S(1)} %get-tuple-element.19.z_ref, f32[8,8,256]{2,1,0:T(8,128)S(1)} %all_to_all.30.row_parts), custom_call_target="tpu_custom_call", output_to_operand_aliasing={{0}: (2, {})} | custom-call | tf_op jit(solution)/shard_map/pallas_call | solution.py:257
  38.5 0.1 broadcast_in_dim.13
  38.5 26.0 %all_to_all.31.col_parts = f32[32,16,256]{2,1,0:T(8,128)S(1)} all-to-all(f32[32,16,256]{2,1,0:T(8,128)S(1)} %broadcast_in_dim.13), channel_id=1, replica_groups=mesh['src'=32,'tgt'=8] {'src'}, dimensions={0} | all-to-all | bytes 1048576 | tf_op jit(solution)/shard_map/all_to_all | solution.py:226
  64.5 2.2 %shard_map.69 = (f32[8,4,256,256]{3,2,1,0:T(8,128)S(1)}, f32[16,256]{1,0:T(8,128)S(1)}, f32[8,256]{1,0:T(8,128)S(1)}) custom-call(s32[8,4]{1,0:T(8,128)S(1)} %copy-done, s32[8]{0:T(128)S(1)} %bitcast.16, f32[8,4,256,256]{3,2,1,0:T(8,128)S(1)} %get-tuple-element.21.w_ref, f32[32,16,256]{2,1,0:T(8,128)S(1)} %all_to_all.31.col_parts), custom_call_target="tpu_custom_call", output_to_operand_aliasing={{0}: (2, {})} | custom-call | tf_op jit(solution)/shard_map/pallas_call | solution.py:267
  66.8 11.8 %all_to_all.32.row_parts = f32[8,8,256]{2,1,0:T(8,128)S(1)} all-to-all(f32[8,8,256]{2,1,0:T(8,128)S(1)} %broadcast_in_dim.14), channel_id=1, replica_groups=mesh['src'=32,'tgt'=8] {'tgt'}, dimensions={0} | all-to-all | bytes 131072 | tf_op jit(solution)/shard_map/all_to_all | solution.py:226
  78.6 3.1 %shard_map.70 = (f32[8,256]{1,0:T(8,128)}, f32[16,256]{1,0:T(8,128)S(1)}) custom-call(s32[8,4]{1,0:T(8,128)S(1)} %copy-done, s32[8]{0:T(128)S(1)} %bitcast.17, f32[8,4,256,256]{3,2,1,0:T(8,128)S(1)} %get-tuple-element.23.q_ref, f32[8,8,256]{2,1,0:T(8,128)S(1)} %all_to_all.32.row_parts), custom_call_target="tpu_custom_call" | custom-call | tf_op jit(solution)/shard_map/pallas_call | solution.py:278
  81.8 19.9 %all_to_all.33.col_parts = f32[32,16,256]{2,1,0:T(8,128)S(1)} all-to-all(f32[32,16,256]{2,1,0:T(8,128)S(1)} %broadcast_in_dim.15), channel_id=1, replica_groups=mesh['src'=32,'tgt'=8] {'src'}, dimensions={0} | all-to-all | bytes 1048576 | tf_op jit(solution)/shard_map/all_to_all | solution.py:226
  101.7 2.5 %shard_map.71 = (f32[16,256]{1,0:T(8,128)}, f32[8,256]{1,0:T(8,128)S(1)}) custom-call(s32[8,4]{1,0:T(8,128)S(1)} %copy-done, s32[8]{0:T(128)S(1)} %bitcast.18, f32[8,4,256,256]{3,2,1,0:T(8,128)S(1)} %get-tuple-element.23.q_ref, f32[32,16,256]{2,1,0:T(8,128)S(1)} %all_to_all.33.col_parts), custom_call_target="tpu_custom_call" | custom-call | tf_op jit(solution)/shard_map/pallas_call | solution.py:288
  104.2 10.8 %all_to_all.34.row_parts = f32[8,8,256]{2,1,0:T(8,128)S(1)} all-to-all(f32[8,8,256]{2,1,0:T(8,128)S(1)} %broadcast_in_dim.16), channel_id=1, replica_groups=mesh['src'=32,'tgt'=8] {'tgt'}, dimensions={0} | all-to-all | bytes 131072 | tf_op jit(solution)/shard_map/all_to_all | solution.py:226
  115.0 2.6 %shard_map.72 = (f32[8,256]{1,0:T(8,128)S(1)}, f32[16,256]{1,0:T(8,128)S(1)}) custom-call(s32[8,4]{1,0:T(8,128)S(1)} %copy-done, s32[8]{0:T(128)S(1)} %bitcast.19, f32[8,4,256,256]{3,2,1,0:T(8,128)S(1)} %get-tuple-element.23.q_ref, f32[8,8,256]{2,1,0:T(8,128)S(1)} %all_to_all.34.row_parts), custom_call_target="tpu_custom_call" | custom-call | tf_op jit(solution)/shard_map/pallas_call | solution.py:278
  117.5 0.1 broadcast_in_dim.17
  117.6 20.0 %all_to_all.35.col_parts = f32[32,16,256]{2,1,0:T(8,128)} all-to-all(f32[32,16,256]{2,1,0:T(8,128)S(1)} %broadcast_in_dim.17), channel_id=1, replica_groups=mesh['src'=32,'tgt'=8] {'src'}, dimensions={0} | all-to-all | bytes 1048576 | tf_op jit(solution)/shard_map/all_to_all | solution.py:226
  137.6 8.1 %shard_map.73 = (f32[16,256]{1,0:T(8,128)}, f32[8,256,768]{2,1,0:T(8,128)}, f32[8,256]{1,0:T(8,128)}) custom-call(s32[8,4]{1,0:T(8,128)} %copy.22.lists, s32[8]{0:T(128)} %bitcast.14, f32[8,4,256,256]{3,2,1,0:T(8,128)S(1)} %get-tuple-element.23.q_ref, f32[32,16,256]{2,1,0:T(8,128)} %all_to_all.35.col_parts, bf16[16,256,768]{2,1,0:T(8,128)(2,1)S(1)} %get-tuple-element.28.tgt), custom_call_target="tpu_custom_call" | custom-call | tf_op jit(solution)/shard_map/pallas_call | solution.py:296
  145.7 0.0 copy-start.5
  145.7 0.0 copy-start.2
  145.7 0.0 copy-start.3
  145.7 0.0 copy-start.4
  145.7 0.0 reduce-scatter.2.cloned.1.call-update
  145.8 0.6 copy-done.5
  146.4 0.6 dynamic-slice
  147.0 0.7 copy-done.2
  147.6 0.7 multiply_reduce_fusion
  148.3 0.6 multiply_add_fusion
  149.0 0.0 copy-done.3
  149.0 0.6 copy.24
  149.6 0.0 copy-done.4
  149.6 16.6 %all-reduce = f32[8,256]{1,0:T(8,128)S(1)} all-reduce(f32[8,256]{1,0:T(8,128)S(1)} %copy-done.4), channel_id=3, replica_groups=mesh['src'=32,'tgt'=8] {'tgt'}, use_global_device_ids=true, to_apply=%region_1.0.clone | all-reduce | flops 2048 | bytes 16384
  166.2 0.6 constant_dynamic-slice_fusion
  166.8 23.8 %reduce-scatter.2.cloned.1.call-done = f32[256,768]{1,0:T(8,128)} async-done(((f32[2048,768]{1,0:T(8,128)}), f32[256,768]{1,0:T(8,128)}) %reduce-scatter.2.cloned.1.call-update) | async-done | bytes 786448 | tf_op jit(solution)/shard_map/reduce_scatter | solution.py:305
  190.6 2.1 %broadcast_divide_fusion = f32[256,768]{1,0:T(8,128)} fusion(f32[256,768]{1,0:T(8,128)} %reduce-scatter.2.cloned.1.call-done, f32[256]{0:T(256)S(1)} %bitcast.25), kind=kLoop, calls=%fused_computation.1 | loop fusion | flops 196608 | bytes 1573888 | tf_op jit(solution)/shard_map/div | solution.py:306
  (6 shorter events, 0.1 us)
Async XLA Ops:
  7.2 28.0 %copy-start.1 = (s32[8,1]{0,1:T(1,128)S(1)}, s32[8,1]{0,1:T(1,128)}, u32[]{:S(2)}) copy-start(s32[8,1]{0,1:T(1,128)} %param.7) | copy-start | bytes 100
  7.2 183.4 %reduce-scatter.2.cloned.1.call-start = ((), (), s32[]{:S(2)}) async-start(), calls=%async_computation.7 | async-start | bytes 7077888 | tf_op jit(solution)/shard_map/reduce_scatter | solution.py:305
  8.6 26.6 %copy-start = (s32[8,4]{1,0:T(8,128)S(1)}, s32[8,4]{1,0:T(8,128)}, u32[]{:S(2)}) copy-start(s32[8,4]{1,0:T(8,128)} %copy.22.lists) | copy-start | bytes 388
  145.7 0.7 copy-start.5
  145.7 1.9 copy-start.2
  145.7 3.2 %copy-start.3 = (f32[16,256]{1,0:T(8,128)S(1)}, f32[16,256]{1,0:T(8,128)}, u32[]{:S(2)}) copy-start(f32[16,256]{1,0:T(8,128)} %get-tuple-element.33) | copy-start | bytes 49156
  145.7 3.9 %copy-start.4 = (f32[8,256]{1,0:T(8,128)S(1)}, f32[8,256]{1,0:T(8,128)}, u32[]{:S(2)}) copy-start(f32[8,256]{1,0:T(8,128)} %get-tuple-element.30) | copy-start | bytes 24580
Sparse Core Ops, SparseCore 0:
  145.9 44.6 reduce-scatter.1

commit v2 on v1

v2 whole, which is shorter than its diff:
```python
import functools
import math

import jax
import jax.numpy as jnp
from jax import lax
from jax.experimental import pallas as pl
from jax.experimental.pallas import tpu as pltpu
from jax.sharding import PartitionSpec as P

BLK = 256
ITERS = 3
EPSILON = 0.1
NEGATIVE = -1e30
LOG2E = math.log2(math.e)
LN2 = math.log(2.0)
LANES = 128
SUB = 8

VMEM = pl.BlockSpec(memory_space=pltpu.VMEM)
SMEM = pl.BlockSpec(memory_space=pltpu.SMEM)
HBM = pl.BlockSpec(memory_space=pltpu.HBM)
PARAMS = pltpu.CompilerParams(vmem_limit_bytes=12 * 1024 * 1024)
NT_DIMS = (((1,), (1,)), ((), ()))


def eye():
    shape = (LANES, LANES)
    return lax.broadcasted_iota(jnp.int32, shape, 0) == lax.broadcasted_iota(jnp.int32, shape, 1)


def lane_halves(x):
    return [x[:, h : h + LANES] for h in range(0, x.shape[1], LANES)]


def to_lanes(column):
    mask = eye()
    halves = [
        jnp.sum(jnp.where(mask, column[h : h + LANES], 0.0), axis=0, keepdims=True)
        for h in range(0, BLK, LANES)
    ]
    return jnp.concatenate(halves, axis=1)


def to_sublanes(row):
    mask = eye()
    halves = [
        jnp.sum(jnp.where(mask, half, 0.0), axis=1, keepdims=True) for half in lane_halves(row)
    ]
    return jnp.concatenate(halves, axis=0)


def lane_total(x):
    halves = [
        jnp.sum(jnp.transpose(x[h : h + LANES]), axis=0, keepdims=True)
        for h in range(0, BLK, LANES)
    ]
    return jnp.concatenate(halves, axis=1)


def fold_rows(tile, op):
    parts = [tile[r : r + SUB] for r in range(0, BLK, SUB)]
    while len(parts) > 1:
        parts = [op(parts[i], parts[i + 1]) for i in range(0, len(parts), 2)]
    return parts[0]


def fold_lanes(tile, op):
    return functools.reduce(op, lane_halves(tile))


def merge_lse(values):
    peak = jnp.max(values, axis=0)
    return peak + jnp.log2(jnp.sum(jnp.exp2(values - peak[None]), axis=0))


def slot(lists, counts, b, k):
    live = k < counts[0, b]
    return jnp.where(live, lists[k, b], lists[0, b]), live


def spread(out, scratch, n):
    packed = jnp.concatenate([scratch[i, 0:1, :] for i in range(scratch.shape[0])], axis=0)
    for d in range(n):
        out[d] = packed


def cost_kernel(
    lists, counts, src_hbm, tgt_hbm, tgt, z_ref, rows, src, bias, totals, sems, *, features
):
    tgt_blocks, src_blocks, slots = tgt.shape[0], src.shape[0], z_ref.shape[1]

    def tgt_copy(t):
        return pltpu.make_async_copy(tgt_hbm.at[t], tgt.at[t], sems.at[t])

    def src_copy(b):
        return pltpu.make_async_copy(src_hbm.at[b], src.at[b], sems.at[tgt_blocks + b])

    for t in range(tgt_blocks):
        tgt_copy(t).start()
    for b in range(src_blocks):
        src_copy(b).start()
    scale = LOG2E / (features * EPSILON)

    @pl.loop(0, tgt_blocks)
    def _(t):
        tgt_copy(t).wait()
        y = tgt[t].astype(jnp.float32)
        square = fold_lanes(y * y, jnp.add)
        bias[t] = jnp.broadcast_to(-scale * lane_total(square), (SUB, BLK))

    @pl.loop(0, src_blocks)
    def _(b):
        src_copy(b).wait()
        peak = None
        for k in range(slots):
            t, live = slot(lists, counts, b, k)
            cross = lax.dot_general(src[b], tgt[t], NT_DIMS, preferred_element_type=jnp.float32)
            z = jnp.where(live, (2.0 * scale) * cross + bias[t, 0:1, :], NEGATIVE)
            z_ref[b, k] = z
            top = fold_lanes(z, jnp.maximum)
            peak = top if peak is None else jnp.maximum(peak, top)
        peak = jnp.max(peak, axis=1, keepdims=True)
        total = None
        for k in range(slots):
            part = fold_lanes(jnp.exp2(z_ref[b, k] - peak), jnp.add)
            total = part if total is None else total + part
        lse = to_lanes(peak) + jnp.log2(lane_total(total))
        totals[b] = jnp.broadcast_to(lse, (SUB, BLK))

    spread(rows, totals, rows.shape[0])


def first_col_kernel(lists, counts, z_ref, row_parts, w_ref, row_lse, cols, peaks, sums):
    src_blocks, slots, tgt_blocks = z_ref.shape[0], z_ref.shape[1], peaks.shape[0]
    row_lse[...] = merge_lse(row_parts[...])
    peaks[...] = jnp.full(peaks.shape, NEGATIVE, jnp.float32)
    sums[...] = jnp.zeros(sums.shape, jnp.float32)

    @pl.loop(0, src_blocks)
    def _(b):
        shift = to_sublanes(row_lse[pl.ds(b, 1), :])
        for k in range(slots):
            t, _ = slot(lists, counts, b, k)
            w = z_ref[b, k] - shift
            w_ref[b, k] = w
            peaks[t] = jnp.maximum(peaks[t], fold_rows(w, jnp.maximum))

    for t in range(tgt_blocks):
        peaks[t] = jnp.broadcast_to(jnp.max(peaks[t], axis=0, keepdims=True), (SUB, BLK))

    @pl.loop(0, src_blocks)
    def _(b):
        for k in range(slots):
            t, _ = slot(lists, counts, b, k)
            sums[t] += fold_rows(jnp.exp2(w_ref[b, k] - peaks[t, 0:1, :]), jnp.add)

    for t in range(tgt_blocks):
        total = jnp.sum(sums[t], axis=0, keepdims=True)
        lse = jnp.where(total > 0.0, peaks[t, 0:1, :] + jnp.log2(total), NEGATIVE)
        sums[t] = jnp.broadcast_to(lse, (SUB, BLK))
    spread(cols, sums, cols.shape[0])


def row_totals(lists, counts, tile, totals, src_blocks, slots):
    @pl.loop(0, src_blocks)
    def _(b):
        total = None
        for k in range(slots):
            t, _ = slot(lists, counts, b, k)
            part = fold_lanes(tile(b, k, t), jnp.add)
            total = part if total is None else total + part
        totals[b] = jnp.broadcast_to(lane_total(total), (SUB, BLK))


def first_row_kernel(lists, counts, w_ref, col_parts, q_ref, col_lse, rows, totals):
    col_lse[...] = merge_lse(col_parts[...])

    def tile(b, k, t):
        q = jnp.exp2(w_ref[b, k] - col_lse[pl.ds(t, 1), :])
        q_ref[b, k] = q
        return q

    row_totals(lists, counts, tile, totals, w_ref.shape[0], w_ref.shape[1])
    spread(rows, totals, rows.shape[0])


def col_kernel(lists, counts, q_ref, row_parts, row_scale, cols, sums, *, share):
    src_blocks, slots, tgt_blocks = q_ref.shape[0], q_ref.shape[1], sums.shape[0]
    row_scale[...] = share / jnp.sum(row_parts[...], axis=0)
    sums[...] = jnp.zeros(sums.shape, jnp.float32)

    @pl.loop(0, src_blocks)
    def _(b):
        scale = to_sublanes(row_scale[pl.ds(b, 1), :])
        for k in range(slots):
            t, _ = slot(lists, counts, b, k)
            sums[t] += fold_rows(q_ref[b, k] * scale, jnp.add)

    for t in range(tgt_blocks):
        sums[t] = jnp.broadcast_to(jnp.sum(sums[t], axis=0, keepdims=True), (SUB, BLK))
    spread(cols, sums, cols.shape[0])


def row_kernel(lists, counts, q_ref, col_parts, col_scale, rows, totals):
    col_scale[...] = 1.0 / jnp.sum(col_parts[...], axis=0)

    def tile(b, k, t):
        return q_ref[b, k] * col_scale[pl.ds(t, 1), :]

    row_totals(lists, counts, tile, totals, q_ref.shape[0], q_ref.shape[1])
    spread(rows, totals, rows.shape[0])


def position():
    return lax.div(lax.axis_index("tgt"), 2), lax.rem(lax.axis_index("tgt"), 2)


def block_at(step, sibling):
    chip, core = position()
    chips = lax.axis_size("tgt") // 2
    return 2 * lax.rem(chip + step + chips, chips) + (1 - core if sibling else core)


def weighted(lists, counts, q_ref, col_scale, b):
    slots = q_ref.shape[1]
    entries = [slot(lists, counts, b, k)[0] for k in range(slots)]
    return [(t, q_ref[b, k] * col_scale[pl.ds(t, 1), :]) for k, t in enumerate(entries)]


def project(weights, tgt, column, width):
    terms = [
        jnp.dot(
            w.astype(jnp.bfloat16),
            tgt[t, :, pl.ds(column, width)],
            preferred_element_type=jnp.float32,
        )
        for t, w in weights
    ]
    return functools.reduce(jnp.add, terms)


def first_project_kernel(lists, counts, q_ref, col_parts, tgt, col_scale, own, other):
    width = own.shape[2]
    col_scale[...] = 1.0 / jnp.sum(col_parts[...], axis=0)

    @pl.loop(0, 2)
    def _(i):
        column = pl.multiple_of(i * width, LANES)
        for sibling, out in ((True, other), (False, own)):
            weights = weighted(lists, counts, q_ref, col_scale, block_at(2 * i - 1, sibling))
            out[i] = project(weights, tgt, column, width)


def middle_project_kernel(lists, counts, q_ref, col_scale, tgt, own, other):
    width = own.shape[2]
    for sibling, out in ((True, other), (False, own)):
        weights = weighted(lists, counts, q_ref, col_scale, block_at(2, sibling))

        @pl.loop(0, 2)
        def _(i, out=out, weights=weights):
            out[i] = project(weights, tgt, pl.multiple_of(i * width, LANES), width)


def last_project_kernel(
    lists, counts, q_ref, col_scale, tgt, own_last, other_last, own_end, other_end, mass, totals
):
    width = own_last.shape[2]

    @pl.loop(0, 2)
    def _(i):
        column = pl.multiple_of((1 - i) * width, LANES)
        for sibling, out in ((True, other_last), (False, own_last)):
            weights = weighted(lists, counts, q_ref, col_scale, block_at(2 * i - 1, sibling))
            out[1 - i] = project(weights, tgt, column, width)

    for sibling, out in ((True, other_end), (False, own_end)):
        weights = weighted(lists, counts, q_ref, col_scale, block_at(0, sibling))

        @pl.loop(0, 2)
        def _(i, out=out, weights=weights):
            out[i] = project(weights, tgt, pl.multiple_of(i * width, LANES), width)

    def tile(b, k, t):
        return q_ref[b, k] * col_scale[pl.ds(t, 1), :]

    row_totals(lists, counts, tile, totals, q_ref.shape[0], q_ref.shape[1])
    for b in range(mass.shape[0]):
        mass[b] = totals[b, 0:1, :]


def finish_kernel(up, down, own, other, mass, out):
    width = up.shape[1]
    scale = to_sublanes(1.0 / jnp.sum(mass[...], axis=0))
    out[:, :width] = (up[...] + own[0] + other[0]) * scale
    out[:, width:] = (down[...] + own[1] + other[1]) * scale


def in_vmem(x):
    return pltpu.with_memory_space_constraint(x, pltpu.VMEM)


def in_hbm(x):
    return pltpu.with_memory_space_constraint(x, pltpu.HBM)


def f32(*shape):
    return jax.ShapeDtypeStruct(shape, jnp.float32)


def v32(*shape):
    return pltpu.VMEM(shape, jnp.float32)


def exchange(copies, axis):
    return in_vmem(lax.all_to_all(copies, axis, 0, 0))


def local(sources, targets, block_lists, live_counts):
    src_rows, features = sources.shape
    src_blocks = src_rows // BLK
    tgt_blocks = targets.shape[0] // BLK
    slots = block_lists.shape[2]
    n_src, n_tgt = lax.axis_size("src"), lax.axis_size("tgt")
    total_src = src_rows * n_src
    total_tgt = targets.shape[0] * n_tgt
    src_blocked = sources.reshape(src_blocks, BLK, features)
    tgt_blocked = targets.reshape(tgt_blocks, BLK, features)
    lists = (block_lists[:, 0, :].T, live_counts.T)
    tiles = v32(src_blocks, slots, BLK, BLK)
    row_shape, col_shape = f32(src_blocks, BLK), f32(tgt_blocks, BLK)
    row_sends, col_sends = v32(n_tgt, src_blocks, BLK), v32(n_src, tgt_blocks, BLK)
    row_scratch, col_scratch = v32(src_blocks, SUB, BLK), v32(tgt_blocks, SUB, BLK)

    tgt_vmem, z, rows = pl.pallas_call(
        functools.partial(cost_kernel, features=features),
        in_specs=[SMEM, SMEM, HBM, HBM],
        out_specs=[VMEM, VMEM, VMEM],
        out_shape=[pltpu.VMEM(tgt_blocked.shape, jnp.bfloat16), tiles, row_sends],
        scratch_shapes=[
            pltpu.VMEM(src_blocked.shape, jnp.bfloat16),
            col_scratch,
            row_scratch,
            pltpu.SemaphoreType.DMA((tgt_blocks + src_blocks,)),
        ],
        compiler_params=PARAMS,
        name="cost",
    )(*lists, in_hbm(src_blocked), in_hbm(tgt_blocked))

    w, row_lse, cols = pl.pallas_call(
        first_col_kernel,
        in_specs=[SMEM, SMEM, VMEM, VMEM],
        out_specs=[VMEM, VMEM, VMEM],
        out_shape=[tiles, row_shape, col_sends],
        scratch_shapes=[col_scratch, col_scratch],
        input_output_aliases={2: 0},
        compiler_params=PARAMS,
        name="first_col",
    )(*lists, in_vmem(z), exchange(rows, "tgt"))

    q, col_lse, rows = pl.pallas_call(
        first_row_kernel,
        in_specs=[SMEM, SMEM, VMEM, VMEM],
        out_specs=[VMEM, VMEM, VMEM],
        out_shape=[tiles, col_shape, row_sends],
        scratch_shapes=[row_scratch],
        input_output_aliases={2: 0},
        compiler_params=PARAMS,
        name="first_row",
    )(*lists, in_vmem(w), exchange(cols, "src"))
    q = in_vmem(q)

    for sweep in range(1, ITERS):
        row_scale, cols = pl.pallas_call(
            functools.partial(col_kernel, share=total_tgt / total_src),
            in_specs=[SMEM, SMEM, VMEM, VMEM],
            out_specs=[VMEM, VMEM],
            out_shape=[row_shape, col_sends],
            scratch_shapes=[col_scratch],
            compiler_params=PARAMS,
            name="col_sums",
        )(*lists, q, exchange(rows, "tgt"))
        col_parts = exchange(cols, "src")
        if sweep < ITERS - 1:
            col_scale, rows = pl.pallas_call(
                row_kernel,
                in_specs=[SMEM, SMEM, VMEM, VMEM],
                out_specs=[VMEM, VMEM],
                out_shape=[col_shape, row_sends],
                scratch_shapes=[row_scratch],
                compiler_params=PARAMS,
                name="row_sums",
            )(*lists, q, col_parts)

    chips = n_tgt // 2
    tgt_vmem = in_vmem(tgt_vmem)
    half = v32(2, BLK, features // 2)

    def swap(x):
        return lax.ppermute(x, "tgt", [(t, t ^ 1) for t in range(n_tgt)])

    def along(x, step):
        pairs = [(t, 2 * ((t // 2 + step) % chips) + t % 2) for t in range(n_tgt)]
        return lax.ppermute(x, "tgt", pairs)

    col_scale, own, other = pl.pallas_call(
        first_project_kernel,
        in_specs=[SMEM, SMEM, VMEM, VMEM, VMEM],
        out_specs=[VMEM] * 3,
        out_shape=[col_shape, half, half],
        compiler_params=PARAMS,
        name="project_first",
    )(*lists, q, col_parts, tgt_vmem)
    first = own + swap(other)
    own_middle, other_middle = pl.pallas_call(
        middle_project_kernel,
        in_specs=[SMEM, SMEM, VMEM, VMEM, VMEM],
        out_specs=[VMEM] * 2,
        out_shape=[half] * 2,
        compiler_params=PARAMS,
        name="project_middle",
    )(*lists, q, col_scale, tgt_vmem)
    up, down = along(first[0], 1), along(first[1], -1)
    first, col_scale = lax.optimization_barrier((first, col_scale))
    own_last, other_last, own_end, other_end, mass = pl.pallas_call(
        last_project_kernel,
        in_specs=[SMEM, SMEM, VMEM, VMEM, VMEM],
        out_specs=[VMEM] * 5,
        out_shape=[half] * 4 + [v32(src_blocks, 1, BLK)],
        scratch_shapes=[row_scratch],
        compiler_params=PARAMS,
        name="project_last",
    )(*lists, q, col_scale, tgt_vmem)
    middle = own_middle + swap(other_middle)
    up, down = along(up + middle[0], 1), along(down + middle[1], -1)
    last = own_last + swap(other_last)
    up, down = along(up + last[0], 1), along(down + last[1], -1)
    mapped = pl.pallas_call(
        finish_kernel,
        in_specs=[VMEM] * 5,
        out_specs=VMEM,
        out_shape=f32(BLK, features),
        compiler_params=PARAMS,
        name="finish",
    )(up, down, own_end, swap(other_end), lax.all_to_all(mass, "tgt", 0, 0))

    src_square = jnp.sum(jnp.square(sources.astype(jnp.float32)), -1)
    row_potential = (
        EPSILON * (jnp.log(row_scale) - LN2 * row_lse - math.log(total_src))
    ).reshape(src_rows) + src_square / features
    col_potential = EPSILON * (
        jnp.log(col_scale) - LN2 * col_lse + (math.log(total_src) - math.log(total_tgt))
    )
    return (mapped, row_potential, col_potential.reshape(tgt_blocks * BLK))


def solution(mesh):
    in_specs = (P("src", None), P("tgt", None), P("src", "tgt", None), P("src", "tgt"))
    out_specs = (P(("src", "tgt"), None), P("src"), P("tgt"))
    return jax.shard_map(local, mesh=mesh, in_specs=in_specs, out_specs=out_specs, check_vma=False)
```

time: 200 us -> 172 us (0.86)
  blocking collectives: 118 us -> 97.3 us
  starting transfers between devices: 0.04 us -> 20.5 us
  between operations: 14.2 us -> 0.76 us
  waiting for transfers between devices: 23.8 us -> 10.9 us
  local copies, waits for them, and re-layouts: 5.26 us -> 2.02 us
  Pallas kernels: 34.6 us -> 37.8 us
    reduce_scatter x1 -> x0, waiting for transfers between devices: 23.8 us -> none  [local(): lax.psum_scatter(numerator.reshape(src_rows, features), 'tgt', tiled=True)]
    unnamed x1 -> x0, blocking collectives: 16.6 us -> none
    ppermute x0 -> x10, starting transfers between devices: none -> 14.5 us  [the longest x6 8.18 us: along(): return lax.ppermute(x, 'tgt', pairs)]
    ppermute x0 -> x10, waiting for transfers between devices: none -> 6.9 us  [the longest x6 6.89 us: along(): return lax.ppermute(x, 'tgt', pairs)]
    all_to_all x0 -> x1, starting transfers between devices: none -> 6.02 us  [local(): lax.all_to_all(mass, 'tgt', 0, 0)]
    all_to_all x6, blocking collectives: 102 us -> 97.3 us  [exchange(): return in_vmem(lax.all_to_all(copies, axis, 0, 0))]
    all_to_all x0 -> x1, waiting for transfers between devices: none -> 4 us  [local(): lax.all_to_all(mass, 'tgt', 0, 0)]
    pallas_call x1 -> x4, Pallas kernels: 8.13 us -> 11.4 us  [the longest x1 5.73 us: local(): pl.pallas_call(last_project_kernel, in_specs=[SMEM, SMEM, VMEM, VMEM, VME...]
  transfers between devices with their start and end apart: 1 -> 11, of which waited for: 1 -> 3; matrix products, arithmetic and copies ran while one was open for 2% -> 2% of each run, Pallas kernels for 0% -> 5%
where the time goes in v2:
time: 172 us
  blocking collectives  97.3 us (57%)
  Pallas kernels  37.8 us (22%)
  starting transfers between devices  20.5 us (12%)
  waiting for transfers between devices  10.9 us (6%)
  other arithmetic  2.68 us (2%)
  local copies, waits for them, and re-layouts  2.02 us (1%)
    all_to_all x6, blocking collectives, exchange(): return in_vmem(lax.all_to_all(copies, axis, 0, 0))  97.3 us
    pallas_call x1, Pallas kernels, local(): pl.pallas_call(functools.partial(cost_kernel, features=features), in_spec...  11.2 us
    ppermute x6, starting transfers between devices, along(): return lax.ppermute(x, 'tgt', pairs)  8.18 us
    ppermute x6, waiting for transfers between devices, along(): return lax.ppermute(x, 'tgt', pairs)  6.89 us
    ppermute x4, starting transfers between devices, swap(): return lax.ppermute(x, 'tgt', [(t, t ^ 1) for t in range(n_tgt)])  6.29 us
    all_to_all x1, starting transfers between devices, local(): lax.all_to_all(mass, 'tgt', 0, 0)  6.02 us
    pallas_call x1, Pallas kernels, local(): pl.pallas_call(last_project_kernel, in_specs=[SMEM, SMEM, VMEM, VMEM, VME...  5.73 us
    pallas_call x2, Pallas kernels, local(): pl.pallas_call(functools.partial(col_kernel, share=total_tgt / total_src)...  5.52 us
  transfers between devices with their start and end apart: 11, of which 3 were waited for; matrix products, arithmetic and copies ran while one was open for 2% of the time, Pallas kernels for 5%

profile of v2, /device:TPU:1, one launch (start us, length us, event | category | flops | bytes accessed | tf_op | source)
XLA Modules:
  0.0 171.9 jit_solution(8245895642529446812)
XLA Ops:
  0.6 0.0 copy-start
  0.6 0.7 copy-done
  1.3 0.7 copy-done.2
  2.0 11.2 %cost.1 = (bf16[16,256,768]{2,1,0:T(8,128)(2,1)S(1)}, f32[8,4,256,256]{3,2,1,0:T(8,128)S(1)}, f32[8,8,256]{2,1,0:T(8,128)S(1)}) custom-call(s32[4,8]{1,0:T(4,128)S(1)} %bitcast.32, s32[1,8]{1,0:T(1,128)S(1)} %bitcast.41, bf16[8,256,768]{2,1,0:T(8,128)(2,1)} %bitcast.50, bf16[16,256,768]{2,1,0:T(8,128)(2,1)} %bitcast.51), custom_call_target="tpu_custom_call" | custom-call | tf_op jit(solution)/shard_map/cost/pallas_call | solution.py:335
  13.2 10.6 %all_to_all.35.row_parts = f32[8,8,256]{2,1,0:T(8,128)S(1)} all-to-all(f32[8,8,256]{2,1,0:T(8,128)S(1)} %get-tuple-element.28), channel_id=1, replica_groups=mesh['src'=32,'tgt'=8] {'tgt'}, dimensions={0} | all-to-all | bytes 131072 | tf_op jit(solution)/shard_map/all_to_all | solution.py:316
  23.8 4.6 %first_col.1 = (f32[8,4,256,256]{3,2,1,0:T(8,128)S(1)}, f32[8,256]{1,0:T(8,128)S(1)}, f32[32,16,256]{2,1,0:T(8,128)S(1)}) custom-call(s32[4,8]{1,0:T(4,128)S(1)} %bitcast.33, s32[1,8]{1,0:T(1,128)S(1)} %bitcast.42, f32[8,4,256,256]{3,2,1,0:T(8,128)S(1)} %get-tuple-element.27.z_ref, ...), custom_call_target="tpu_custom_call", output_to_operand_aliasing={{0}: (2, {})} | custom-call | tf_op jit(solution)/shard_map/first_col/pallas_call | solution.py:350
  28.4 26.5 %all_to_all.36.col_parts = f32[32,16,256]{2,1,0:T(8,128)S(1)} all-to-all(f32[32,16,256]{2,1,0:T(8,128)S(1)} %get-tuple-element.30), channel_id=1, replica_groups=mesh['src'=32,'tgt'=8] {'src'}, dimensions={0} | all-to-all | bytes 1048576 | tf_op jit(solution)/shard_map/all_to_all | solution.py:316
  54.8 2.7 %first_row.1 = (f32[8,4,256,256]{3,2,1,0:T(8,128)S(1)}, f32[16,256]{1,0:T(8,128)S(1)}, f32[8,8,256]{2,1,0:T(8,128)S(1)}) custom-call(s32[4,8]{1,0:T(4,128)S(1)} %bitcast.34, s32[1,8]{1,0:T(1,128)S(1)} %bitcast.43, f32[8,4,256,256]{3,2,1,0:T(8,128)S(1)} %get-tuple-element.29.w_ref, ...), custom_call_target="tpu_custom_call", output_to_operand_aliasing={{0}: (2, {})} | custom-call | tf_op jit(solution)/shard_map/first_row/pallas_call | solution.py:361
  57.6 10.3 %all_to_all.37.row_parts = f32[8,8,256]{2,1,0:T(8,128)S(1)} all-to-all(f32[8,8,256]{2,1,0:T(8,128)S(1)} %get-tuple-element.32), channel_id=1, replica_groups=mesh['src'=32,'tgt'=8] {'tgt'}, dimensions={0} | all-to-all | bytes 131072 | tf_op jit(solution)/shard_map/all_to_all | solution.py:316
  67.9 2.9 %col_sums.2 = (f32[8,256]{1,0:T(8,128)}, f32[32,16,256]{2,1,0:T(8,128)S(1)}) custom-call(s32[4,8]{1,0:T(4,128)S(1)} %bitcast.35, s32[1,8]{1,0:T(1,128)S(1)} %bitcast.44, f32[8,4,256,256]{3,2,1,0:T(8,128)S(1)} %get-tuple-element.31.q_ref, f32[8,8,256]{2,1,0:T(8,128)S(1)} %all_to_all.37.row_parts), custom_call_target="tpu_custom_call" | custom-call | tf_op jit(solution)/shard_map/col_sums/pallas_call | solution.py:374
  70.8 19.8 %all_to_all.38.col_parts = f32[32,16,256]{2,1,0:T(8,128)S(1)} all-to-all(f32[32,16,256]{2,1,0:T(8,128)S(1)} %get-tuple-element.33), channel_id=1, replica_groups=mesh['src'=32,'tgt'=8] {'src'}, dimensions={0} | all-to-all | bytes 1048576 | tf_op jit(solution)/shard_map/all_to_all | solution.py:316
  90.6 2.3 %row_sums.1 = (f32[16,256]{1,0:T(8,128)}, f32[8,8,256]{2,1,0:T(8,128)S(1)}) custom-call(s32[4,8]{1,0:T(4,128)S(1)} %bitcast.36, s32[1,8]{1,0:T(1,128)S(1)} %bitcast.45, f32[8,4,256,256]{3,2,1,0:T(8,128)S(1)} %get-tuple-element.31.q_ref, f32[32,16,256]{2,1,0:T(8,128)S(1)} %all_to_all.38.col_parts), custom_call_target="tpu_custom_call" | custom-call | tf_op jit(solution)/shard_map/row_sums/pallas_call | solution.py:385
  92.9 10.3 %all_to_all.39.row_parts = f32[8,8,256]{2,1,0:T(8,128)S(1)} all-to-all(f32[8,8,256]{2,1,0:T(8,128)S(1)} %get-tuple-element.34), channel_id=1, replica_groups=mesh['src'=32,'tgt'=8] {'tgt'}, dimensions={0} | all-to-all | bytes 131072 | tf_op jit(solution)/shard_map/all_to_all | solution.py:316
  103.2 2.6 %col_sums.3 = (f32[8,256]{1,0:T(8,128)S(1)}, f32[32,16,256]{2,1,0:T(8,128)S(1)}) custom-call(s32[4,8]{1,0:T(4,128)S(1)} %bitcast.37, s32[1,8]{1,0:T(1,128)S(1)} %bitcast.46, f32[8,4,256,256]{3,2,1,0:T(8,128)S(1)} %get-tuple-element.31.q_ref, f32[8,8,256]{2,1,0:T(8,128)S(1)} %all_to_all.39.row_parts), custom_call_target="tpu_custom_call" | custom-call | tf_op jit(solution)/shard_map/col_sums/pallas_call | solution.py:374
  105.8 19.8 %all_to_all.40.col_parts = f32[32,16,256]{2,1,0:T(8,128)S(1)} all-to-all(f32[32,16,256]{2,1,0:T(8,128)S(1)} %get-tuple-element.35), channel_id=1, replica_groups=mesh['src'=32,'tgt'=8] {'src'}, dimensions={0} | all-to-all | bytes 1048576 | tf_op jit(solution)/shard_map/all_to_all | solution.py:316
  125.6 2.1 %project_first.1 = (f32[16,256]{1,0:T(8,128)S(1)}, f32[2,256,384]{2,1,0:T(8,128)S(1)}, f32[2,256,384]{2,1,0:T(8,128)S(1)}) custom-call(s32[4,8]{1,0:T(4,128)S(1)} %bitcast.38, s32[1,8]{1,0:T(1,128)S(1)} %bitcast.47, f32[8,4,256,256]{3,2,1,0:T(8,128)S(1)} %get-tuple-element.31.q_ref, f32[32,16,256]{2,1,0:T(8,128)S(1)} %all_to_all.40.col_parts, ...), custom_call_target="tpu_custom_call" | custom-call | tf_op jit(solution)/shard_map/project_first/pallas_call | solution.py:406
  127.7 3.2 %collective-permute-start = (f32[2,256,384]{2,1,0:T(8,128)S(1)}, f32[2,256,384]{2,1,0:T(8,128)S(1)}, u32[]{:S(2)}, u32[]{:S(2)}) collective-permute-start(f32[2,256,384]{2,1,0:T(8,128)S(1)} %get-tuple-element.38), channel_id=1, source_target_pairs={{0,1},{1,0},{2,3},{3,2},{4,5},{5,4},{6,7},{7,6},{8,9},{9,8},{10,11... | collective-permute-start | bytes 2359304 | tf_op jit(solution)/shard_map/ppermute | solution.py:400
  130.9 2.5 %project_middle.1 = (f32[2,256,384]{2,1,0:T(8,128)S(1)}, f32[2,256,384]{2,1,0:T(8,128)S(1)}) custom-call(s32[4,8]{1,0:T(4,128)S(1)} %bitcast.39, s32[1,8]{1,0:T(1,128)S(1)} %bitcast.48, f32[8,4,256,256]{3,2,1,0:T(8,128)S(1)} %get-tuple-element.31.q_ref, f32[16,256]{1,0:T(8,128)S(1)} %get-tuple-element.42.col_scale, ...), custom_call_target="tpu_custom_call" | custom-call | tf_op jit(solution)/shard_map/project_middle/pallas_call | solution.py:415
  133.3 0.1 collective-permute-start.2
  133.5 0.0 collective-permute-done
  133.5 0.1 add.28
  133.6 0.1 slice_bitcast_fusion.2
  133.6 0.4 collective-permute-start.1
  134.0 2.4 %collective-permute-start.6 = (f32[256,384]{1,0:T(8,128)S(1)}, f32[256,384]{1,0:T(8,128)S(1)}, u32[]{:S(2)}, u32[]{:S(2)}) collective-permute-start(f32[256,384]{1,0:T(8,128)S(1)} %get-tuple-element.55), channel_id=1, source_target_pairs={{0,6},{1,7},{2,0},{3,1},{4,2},{5,3},{6,4},{7,5},{8,14},{9,15},{10,... | collective-permute-start | bytes 1179656 | tf_op jit(solution)/shard_map/ppermute | solution.py:404
  136.4 5.7 %project_last.1 = (f32[2,256,384]{2,1,0:T(8,128)S(1)}, f32[2,256,384]{2,1,0:T(8,128)S(1)}, f32[2,256,384]{2,1,0:T(8,128)S(1)}, f32[2,256,384]{2,1,0:T(8,128)S(1)}, f32[8,1,256]{2,1,0:T(1,128)}) custom-call(s32[4,8]{1,0:T(4,128)S(1)} %bitcast.40, s32[1,8]{1,0:T(1,128)S(1)} %bitcast.49, f32[8,4,256,256]{3,2,1,0:T(8,128)S(1)} %get-tuple-element.31.q_ref, ...), custom_call_target="tpu_custom_call" | custom-call | tf_op jit(solution)/shard_map/project_last/pallas_call | solution.py:425
  142.1 1.0 collective-permute-start.4
  143.2 0.0 collective-permute-done.2
  143.2 0.1 add.29
  143.3 1.8 %collective-permute-done.1 = f32[256,384]{1,0:T(8,128)S(1)} collective-permute-done((f32[256,384]{1,0:T(8,128)S(1)}, f32[256,384]{1,0:T(8,128)S(1)}, u32[]{:S(2)}, u32[]{:S(2)}) %collective-permute-start.1) | collective-permute-done | bytes 393248 | tf_op jit(solution)/shard_map/ppermute | solution.py:404
  145.1 0.0 collective-permute-done.6
  145.1 0.1 fusion.1
  145.2 0.1 collective-permute-start.3
  145.3 2.7 %collective-permute-start.7 = (f32[256,384]{1,0:T(8,128)S(1)}, f32[256,384]{1,0:T(8,128)S(1)}, u32[]{:S(2)}, u32[]{:S(2)}) collective-permute-start(f32[256,384]{1,0:T(8,128)S(1)} %get-tuple-element.53), channel_id=1, source_target_pairs={{0,6},{1,7},{2,0},{3,1},{4,2},{5,3},{6,4},{7,5},{8,14},{9,15},{10,... | collective-permute-start | bytes 1179656 | tf_op jit(solution)/shard_map/ppermute | solution.py:404
  148.0 0.7 multiply_reduce_fusion
  148.7 2.0 %collective-permute-start.9 = (f32[2,256,384]{2,1,0:T(8,128)S(1)}, f32[2,256,384]{2,1,0:T(8,128)S(1)}, u32[]{:S(2)}, u32[]{:S(2)}) collective-permute-start(f32[2,256,384]{2,1,0:T(8,128)S(1)} %get-tuple-element.46), channel_id=1, source_target_pairs={{0,1},{1,0},{2,3},{3,2},{4,5},{5,4},{6,7},{7,6},{8,9},{9,8},{10,11... | collective-permute-start | bytes 2359304 | tf_op jit(solution)/shard_map/ppermute | solution.py:400
  150.7 0.0 collective-permute-done.4
  150.7 0.1 add.31
  150.8 5.0 %collective-permute-done.3 = f32[256,384]{1,0:T(8,128)S(1)} collective-permute-done((f32[256,384]{1,0:T(8,128)S(1)}, f32[256,384]{1,0:T(8,128)S(1)}, u32[]{:S(2)}, u32[]{:S(2)}) %collective-permute-start.3) | collective-permute-done | bytes 393248 | tf_op jit(solution)/shard_map/ppermute | solution.py:404
  155.8 1.0 fusion
  156.8 0.2 collective-permute-start.5
  157.0 2.5 %collective-permute-start.8 = (f32[256,384]{1,0:T(8,128)}, f32[256,384]{1,0:T(8,128)S(1)}, u32[]{:S(2)}, u32[]{:S(2)}) collective-permute-start(f32[256,384]{1,0:T(8,128)} %get-tuple-element.51), channel_id=1, source_target_pairs={{0,6},{1,7},{2,0},{3,1},{4,2},{5,3},{6,4},{7,5},{8,14},{9,15},{10,... | collective-permute-start | bytes 1179656 | tf_op jit(solution)/shard_map/ppermute | solution.py:404
  159.5 0.6 multiply_add_fusion
  160.1 6.0 %all-to-all-start.6 = ((f32[8,1,256]{2,1,0:T(1,128)}), f32[8,1,256]{2,1,0:T(1,128)S(1)}, u32[]{:S(2)}, u32[]{:S(2)}) async-start(f32[8,1,256]{2,1,0:T(1,128)} %get-tuple-element.47), calls=%async_computation.6 | async-start | bytes 16384 | tf_op jit(solution)/shard_map/all_to_all | solution.py:445
  166.1 0.6 copy.10
  166.7 4.0 %all-to-all-done.6.mass = f32[8,1,256]{2,1,0:T(1,128)S(1)} async-done(((f32[8,1,256]{2,1,0:T(1,128)}), f32[8,1,256]{2,1,0:T(1,128)S(1)}, u32[]{:S(2)}, u32[]{:S(2)}) %all-to-all-start.6) | async-done | bytes 8224 | tf_op jit(solution)/shard_map/all_to_all | solution.py:445
  170.7 0.0 collective-permute-done.9.other
  170.7 0.0 collective-permute-done.5.up
  170.7 1.1 finish.1
  (12 shorter events, 0.0 us)
Async XLA Ops:
  0.6 0.7 copy-start
  1.3 0.7 copy-start.2
  127.7 5.8 %collective-permute-start = (f32[2,256,384]{2,1,0:T(8,128)S(1)}, f32[2,256,384]{2,1,0:T(8,128)S(1)}, u32[]{:S(2)}, u32[]{:S(2)}) collective-permute-start(f32[2,256,384]{2,1,0:T(8,128)S(1)} %get-tuple-element.38), channel_id=1, source_target_pairs={{0,1},{1,0},{2,3},{3,2},{4,5},{5,4},{6,7},{7,6},{8,9},{9,8},{10,11... | collective-permute-start | bytes 2359304 | tf_op jit(solution)/shard_map/ppermute | solution.py:400
  130.9 5.5 %copy-start.1 = (s32[8,1,4]{0,2,1:T(4,128)S(1)}, s32[8,1,4]{0,2,1:T(4,128)}, u32[]{:S(2)}) copy-start(s32[8,1,4]{0,2,1:T(4,128)} %param.6) | copy-start | bytes 388
  130.9 5.5 %copy-start.3 = (s32[8,1]{0,1:T(1,128)S(1)}, s32[8,1]{0,1:T(1,128)}, u32[]{:S(2)}) copy-start(s32[8,1]{0,1:T(1,128)} %param.7) | copy-start | bytes 100
  133.3 9.8 %collective-permute-start.2 = (f32[2,256,384]{2,1,0:T(8,128)S(1)}, f32[2,256,384]{2,1,0:T(8,128)S(1)}, u32[]{:S(2)}, u32[]{:S(2)}) collective-permute-start(f32[2,256,384]{2,1,0:T(8,128)S(1)} %get-tuple-element.41), channel_id=1, source_target_pairs={{0,1},{1,0},{2,3},{3,2},{4,5},{5,4},{6,7},{7,6},{8,9},{9,8},{10,11... | collective-permute-start | bytes 2359304 | tf_op jit(solution)/shard_map/ppermute | solution.py:400
  133.6 11.5 %collective-permute-start.1 = (f32[256,384]{1,0:T(8,128)S(1)}, f32[256,384]{1,0:T(8,128)S(1)}, u32[]{:S(2)}, u32[]{:S(2)}) collective-permute-start(f32[256,384]{1,0:T(8,128)S(1)} %get-tuple-element.56), channel_id=1, source_target_pairs={{0,2},{1,3},{2,4},{3,5},{4,6},{5,7},{6,0},{7,1},{8,10},{9,11},{10,... | collective-permute-start | bytes 1179656 | tf_op jit(solution)/shard_map/ppermute | solution.py:404
  134.0 14.0 %copy-start.4 = (bf16[2048,768]{1,0:T(8,128)(2,1)S(1)}, bf16[2048,768]{1,0:T(8,128)(2,1)}, u32[]{:S(2)}) copy-start(bf16[2048,768]{1,0:T(8,128)(2,1)} %param.4) | copy-start | bytes 9437188
  134.0 11.1 %collective-permute-start.6 = (f32[256,384]{1,0:T(8,128)S(1)}, f32[256,384]{1,0:T(8,128)S(1)}, u32[]{:S(2)}, u32[]{:S(2)}) collective-permute-start(f32[256,384]{1,0:T(8,128)S(1)} %get-tuple-element.55), channel_id=1, source_target_pairs={{0,6},{1,7},{2,0},{3,1},{4,2},{5,3},{6,4},{7,5},{8,14},{9,15},{10,... | collective-permute-start | bytes 1179656 | tf_op jit(solution)/shard_map/ppermute | solution.py:404
  142.1 8.6 %collective-permute-start.4 = (f32[2,256,384]{2,1,0:T(8,128)S(1)}, f32[2,256,384]{2,1,0:T(8,128)S(1)}, u32[]{:S(2)}, u32[]{:S(2)}) collective-permute-start(f32[2,256,384]{2,1,0:T(8,128)S(1)} %get-tuple-element.44), channel_id=1, source_target_pairs={{0,1},{1,0},{2,3},{3,2},{4,5},{5,4},{6,7},{7,6},{8,9},{9,8},{10,11... | collective-permute-start | bytes 2359304 | tf_op jit(solution)/shard_map/ppermute | solution.py:400
  145.2 10.6 %collective-permute-start.3 = (f32[256,384]{1,0:T(8,128)S(1)}, f32[256,384]{1,0:T(8,128)S(1)}, u32[]{:S(2)}, u32[]{:S(2)}) collective-permute-start(f32[256,384]{1,0:T(8,128)S(1)} %get-tuple-element.54), channel_id=1, source_target_pairs={{0,2},{1,3},{2,4},{3,5},{4,6},{5,7},{6,0},{7,1},{8,10},{9,11},{10,... | collective-permute-start | bytes 1179656 | tf_op jit(solution)/shard_map/ppermute | solution.py:404
  145.3 10.5 %collective-permute-start.7 = (f32[256,384]{1,0:T(8,128)S(1)}, f32[256,384]{1,0:T(8,128)S(1)}, u32[]{:S(2)}, u32[]{:S(2)}) collective-permute-start(f32[256,384]{1,0:T(8,128)S(1)} %get-tuple-element.53), channel_id=1, source_target_pairs={{0,6},{1,7},{2,0},{3,1},{4,2},{5,3},{6,4},{7,5},{8,14},{9,15},{10,... | collective-permute-start | bytes 1179656 | tf_op jit(solution)/shard_map/ppermute | solution.py:404
  148.7 22.1 %collective-permute-start.9 = (f32[2,256,384]{2,1,0:T(8,128)S(1)}, f32[2,256,384]{2,1,0:T(8,128)S(1)}, u32[]{:S(2)}, u32[]{:S(2)}) collective-permute-start(f32[2,256,384]{2,1,0:T(8,128)S(1)} %get-tuple-element.46), channel_id=1, source_target_pairs={{0,1},{1,0},{2,3},{3,2},{4,5},{5,4},{6,7},{7,6},{8,9},{9,8},{10,11... | collective-permute-start | bytes 2359304 | tf_op jit(solution)/shard_map/ppermute | solution.py:400
  156.8 13.9 %collective-permute-start.5 = (f32[256,384]{1,0:T(8,128)}, f32[256,384]{1,0:T(8,128)S(1)}, u32[]{:S(2)}, u32[]{:S(2)}) collective-permute-start(f32[256,384]{1,0:T(8,128)} %get-tuple-element.52), channel_id=1, source_target_pairs={{0,2},{1,3},{2,4},{3,5},{4,6},{5,7},{6,0},{7,1},{8,10},{9,11},{10,... | collective-permute-start | bytes 1179656 | tf_op jit(solution)/shard_map/ppermute | solution.py:404
  157.0 13.7 %collective-permute-start.8 = (f32[256,384]{1,0:T(8,128)}, f32[256,384]{1,0:T(8,128)S(1)}, u32[]{:S(2)}, u32[]{:S(2)}) collective-permute-start(f32[256,384]{1,0:T(8,128)} %get-tuple-element.51), channel_id=1, source_target_pairs={{0,6},{1,7},{2,0},{3,1},{4,2},{5,3},{6,4},{7,5},{8,14},{9,15},{10,... | collective-permute-start | bytes 1179656 | tf_op jit(solution)/shard_map/ppermute | solution.py:404
  160.1 10.7 %all-to-all-start.6 = ((f32[8,1,256]{2,1,0:T(1,128)}), f32[8,1,256]{2,1,0:T(1,128)S(1)}, u32[]{:S(2)}, u32[]{:S(2)}) async-start(f32[8,1,256]{2,1,0:T(1,128)} %get-tuple-element.47), calls=%async_computation.6 | async-start | bytes 16384 | tf_op jit(solution)/shard_map/all_to_all | solution.py:445

commit v3 on v2

v3 whole, which is shorter than its diff:
```python
import functools
import math

import jax
import jax.numpy as jnp
from jax import lax
from jax.experimental import pallas as pl
from jax.experimental.pallas import tpu as pltpu
from jax.sharding import Mesh
from jax.sharding import PartitionSpec as P

BLK = 256
ITERS = 3
EPSILON = 0.1
NEGATIVE = -1e30
LOG2E = math.log2(math.e)
LN2 = math.log(2.0)
LANES = 128
SUB = 8
GROUP = 8
CHIPS_X = 4
SRC = ("z", "x")

VMEM = pl.BlockSpec(memory_space=pltpu.VMEM)
SMEM = pl.BlockSpec(memory_space=pltpu.SMEM)
HBM = pl.BlockSpec(memory_space=pltpu.HBM)
PARAMS = pltpu.CompilerParams(vmem_limit_bytes=12 * 1024 * 1024)
NT_DIMS = (((1,), (1,)), ((), ()))


def eye():
    shape = (LANES, LANES)
    return lax.broadcasted_iota(jnp.int32, shape, 0) == lax.broadcasted_iota(jnp.int32, shape, 1)


def lane_halves(x):
    return [x[:, h : h + LANES] for h in range(0, x.shape[1], LANES)]


def to_lanes(column):
    mask = eye()
    halves = [
        jnp.sum(jnp.where(mask, column[h : h + LANES], 0.0), axis=0, keepdims=True)
        for h in range(0, BLK, LANES)
    ]
    return jnp.concatenate(halves, axis=1)


def to_sublanes(row):
    mask = eye()
    halves = [
        jnp.sum(jnp.where(mask, half, 0.0), axis=1, keepdims=True) for half in lane_halves(row)
    ]
    return jnp.concatenate(halves, axis=0)


def along_rows(row):
    halves = [
        jnp.transpose(jnp.broadcast_to(half, (LANES, LANES))) for half in lane_halves(row)
    ]
    column = jnp.concatenate(halves, axis=0)
    return jnp.concatenate([column] * (BLK // LANES), axis=1)


def lane_total(x):
    halves = [
        jnp.sum(jnp.transpose(x[h : h + LANES]), axis=0, keepdims=True)
        for h in range(0, BLK, LANES)
    ]
    return jnp.concatenate(halves, axis=1)


def fold_rows(tile, op):
    parts = [tile[r : r + SUB] for r in range(0, BLK, SUB)]
    while len(parts) > 1:
        parts = [op(parts[i], parts[i + 1]) for i in range(0, len(parts), 2)]
    return parts[0]


def fold_lanes(tile, op):
    return functools.reduce(op, lane_halves(tile))


def merge_lse(values):
    peak = jnp.max(values, axis=0)
    return peak + jnp.log2(jnp.sum(jnp.exp2(values - peak[None]), axis=0))


def spread(out, scratch, n):
    packed = jnp.concatenate([scratch[i, 0:1, :] for i in range(scratch.shape[0])], axis=0)
    for d in range(n):
        out[d] = packed


def cost_kernel(
    lists_hbm, counts_hbm, src_hbm, tgt_hbm,
    tgt, z_ref, rows, table,
    lists, counts, order, place, src, bias, totals, sems, list_sems,
    *, features,
):
    tgt_blocks, src_blocks, slots = tgt.shape[0], src.shape[0], z_ref.shape[1]
    share = tgt_blocks * GROUP // (src_blocks * slots)
    list_copies = [
        pltpu.make_async_copy(lists_hbm, lists, list_sems.at[0]),
        pltpu.make_async_copy(counts_hbm, counts, list_sems.at[1]),
    ]

    def tgt_copy(t):
        return pltpu.make_async_copy(tgt_hbm.at[t], tgt.at[t], sems.at[t])

    def src_copy(b):
        return pltpu.make_async_copy(src_hbm.at[b], src.at[b], sems.at[tgt_blocks + b])

    for copy in list_copies:
        copy.start()
    for b in range(src_blocks):
        src_copy(b).start()
    for t in range(tgt_blocks):
        tgt_copy(t).start()
    for copy in list_copies:
        copy.wait()

    for t in range(tgt_blocks):
        place[t] = 0
    for b in range(src_blocks):
        for k in range(slots):
            t = jnp.where(k < counts[0, b], lists[k, b], lists[0, b])
            table[b * slots + k] = t
            place[t] = place[t] + 1
    start = 0
    for t in range(tgt_blocks):
        count = place[t]
        place[t] = start
        start = start + count
    for n in range(src_blocks * slots):
        t = table[n]
        order[place[t]] = n
        place[t] = place[t] + 1

    for b in range(src_blocks):
        src_copy(b).wait()
    scale = LOG2E / (features * EPSILON)

    def arrived(t, carry):
        tgt_copy(t).wait()
        return carry

    def cross_terms(g, ready):
        entries = [order[g * GROUP + i] for i in range(GROUP)]
        blocks = [table[n] for n in entries]
        squares = [g * share + i for i in range(share)]
        needed = jnp.maximum(ready, jnp.maximum(squares[-1], blocks[-1]) + 1)
        lax.fori_loop(ready, needed, arrived, 0)
        for n, block in zip(entries, blocks):
            z_ref[n // slots, n % slots] = lax.dot_general(
                src[n // slots], tgt[block], NT_DIMS, preferred_element_type=jnp.float32
            )
        for t in squares:
            y = tgt[t].astype(jnp.float32)
            square = fold_lanes(y * y, jnp.add)
            bias[t] = jnp.broadcast_to(-scale * lane_total(square), (SUB, BLK))
        return needed

    lax.fori_loop(0, src_blocks * slots // GROUP, cross_terms, 0)

    @pl.loop(0, src_blocks, unroll=2)
    def _(b):
        peak = None
        for k in range(slots):
            live = k < counts[0, b]
            offset = jnp.where(live, bias[table[b * slots + k], 0:1, :], NEGATIVE)
            z = (2.0 * scale) * z_ref[b, k] + offset
            z_ref[b, k] = z
            top = fold_lanes(z, jnp.maximum)
            peak = top if peak is None else jnp.maximum(peak, top)
        peak = jnp.max(peak, axis=1, keepdims=True)
        total = None
        for k in range(slots):
            part = fold_lanes(jnp.exp2(z_ref[b, k] - peak), jnp.add)
            total = part if total is None else total + part
        lse = to_lanes(peak) + jnp.log2(lane_total(total))
        totals[b] = jnp.broadcast_to(lse, (SUB, BLK))

    spread(rows, totals, rows.shape[0])


def first_col_kernel(table, z_ref, row_parts, w_ref, row_lse, cols, peaks, sums):
    src_blocks, slots, tgt_blocks = z_ref.shape[0], z_ref.shape[1], peaks.shape[0]
    row_lse[...] = merge_lse(row_parts[...])
    peaks[...] = jnp.full(peaks.shape, NEGATIVE, jnp.float32)
    sums[...] = jnp.zeros(sums.shape, jnp.float32)

    @pl.loop(0, src_blocks)
    def _(b):
        shift = along_rows(row_lse[pl.ds(b, 1), :])
        for k in range(slots):
            t = table[b * slots + k]
            w = z_ref[b, k] - shift
            w_ref[b, k] = w
            top = jnp.max(fold_rows(w, jnp.maximum), axis=0, keepdims=True)
            total = fold_rows(jnp.exp2(w - top), jnp.add)
            old = peaks[t]
            new = jnp.maximum(old, top)
            peaks[t] = new
            sums[t] = sums[t] * jnp.exp2(old - new) + total * jnp.exp2(top - new)

    for t in range(tgt_blocks):
        total = jnp.sum(sums[t], axis=0, keepdims=True)
        lse = jnp.where(total > 0.0, peaks[t, 0:1, :] + jnp.log2(total), NEGATIVE)
        sums[t] = jnp.broadcast_to(lse, (SUB, BLK))
    spread(cols, sums, cols.shape[0])


def row_totals(table, tile, totals, src_blocks, slots):
    @pl.loop(0, src_blocks)
    def _(b):
        total = None
        for k in range(slots):
            t = table[b * slots + k]
            part = fold_lanes(tile(b, k, t), jnp.add)
            total = part if total is None else total + part
        totals[b] = jnp.broadcast_to(lane_total(total), (SUB, BLK))


def first_row_kernel(table, w_ref, col_parts, q_ref, col_lse, rows, totals):
    col_lse[...] = merge_lse(col_parts[...])

    def tile(b, k, t):
        q = jnp.exp2(w_ref[b, k] - col_lse[pl.ds(t, 1), :])
        q_ref[b, k] = q
        return q

    row_totals(table, tile, totals, w_ref.shape[0], w_ref.shape[1])
    spread(rows, totals, rows.shape[0])


def col_kernel(table, q_ref, row_parts, row_scale, cols, sums, *, share):
    src_blocks, slots, tgt_blocks = q_ref.shape[0], q_ref.shape[1], sums.shape[0]
    row_scale[...] = share / jnp.sum(row_parts[...], axis=0)
    sums[...] = jnp.zeros(sums.shape, jnp.float32)

    @pl.loop(0, src_blocks)
    def _(b):
        scale = along_rows(row_scale[pl.ds(b, 1), :])
        for k in range(slots):
            t = table[b * slots + k]
            sums[t] += fold_rows(q_ref[b, k] * scale, jnp.add)

    for t in range(tgt_blocks):
        sums[t] = jnp.broadcast_to(jnp.sum(sums[t], axis=0, keepdims=True), (SUB, BLK))
    spread(cols, sums, cols.shape[0])


def row_kernel(table, q_ref, col_parts, col_scale, rows, totals):
    col_scale[...] = 1.0 / jnp.sum(col_parts[...], axis=0)

    def tile(b, k, t):
        return q_ref[b, k] * col_scale[pl.ds(t, 1), :]

    row_totals(table, tile, totals, q_ref.shape[0], q_ref.shape[1])
    spread(rows, totals, rows.shape[0])


def block_at(flip, sibling):
    chip, core = lax.div(lax.axis_index("tgt"), 2), lax.rem(lax.axis_index("tgt"), 2)
    return 2 * lax.bitwise_xor(chip, flip) + (1 - core if sibling else core)


def weighted(table, q_ref, col_scale, b):
    slots = q_ref.shape[1]
    entries = [table[b * slots + k] for k in range(slots)]
    return [(t, q_ref[b, k] * col_scale[pl.ds(t, 1), :]) for k, t in enumerate(entries)]


def project(table, q_ref, col_scale, tgt, block, outs, width):
    weights = weighted(table, q_ref, col_scale, block)
    rows = [(t, w.astype(jnp.bfloat16)) for t, w in weights]
    total = functools.reduce(jnp.add, [fold_lanes(w, jnp.add) for _, w in weights])
    mass = jnp.broadcast_to(lane_total(total), (SUB, BLK))
    for n, out in enumerate(outs):
        columns = slice(n * width, (n + 1) * width)
        terms = [
            jnp.dot(w, tgt[t, :, columns], preferred_element_type=jnp.float32) for t, w in rows
        ]
        out[:BLK, :] = functools.reduce(jnp.add, terms)
        out[BLK:, :BLK] = mass
        out[BLK:, BLK:] = jnp.zeros((SUB, width - BLK), jnp.float32)


def far_kernel(table, q_ref, col_parts, tgt, col_scale, own, other):
    col_scale[...] = 1.0 / jnp.sum(col_parts[...], axis=0)
    for sibling, out in ((True, other), (False, own)):
        halves = [out.at[0], out.at[1]]
        project(table, q_ref, col_scale, tgt, block_at(2, sibling), halves, out.shape[2])


def side_kernel(table, q_ref, col_scale, tgt, own, other):
    @pl.loop(0, 2)
    def _(i):
        for sibling, out in ((True, other), (False, own)):
            block = block_at(2 * i + 1, sibling)
            project(table, q_ref, col_scale, tgt, block, [out.at[i]], out.shape[2])


def end_kernel(table, q_ref, col_scale, tgt, own, other):
    for sibling, out in ((True, other), (False, own)):
        project(table, q_ref, col_scale, tgt, block_at(0, sibling), [out], out.shape[1])


def far_sum_kernel(own, other, low, high):
    low[...] = own[0] + other[0]
    high[...] = own[1] + other[1]


def side_sum_kernel(own, other, low, high, first, second):
    width = low.shape[1]
    first[:, :width] = own[0, :, :width] + other[0, :, :width]
    first[:, width:] = own[0, :, width:] + other[0, :, width:] + high[...]
    second[:, :width] = own[1, :, :width] + other[1, :, :width] + low[...]
    second[:, width:] = own[1, :, width:] + other[1, :, width:]


def finish_kernel(first, second, own, other, out):
    mass = (first[BLK:] + second[BLK:] + own[BLK:] + other[BLK:])[0:1, :BLK]
    total = first[:BLK] + second[:BLK] + own[:BLK] + other[:BLK]
    out[...] = total * to_sublanes(1.0 / mass)


def in_vmem(x):
    return pltpu.with_memory_space_constraint(x, pltpu.VMEM)


def in_hbm(x):
    return pltpu.with_memory_space_constraint(x, pltpu.HBM)


def f32(*shape):
    return jax.ShapeDtypeStruct(shape, jnp.float32)


def v32(*shape):
    return pltpu.VMEM(shape, jnp.float32)


def exchange(copies, axis):
    return in_vmem(lax.all_to_all(copies, axis, 0, 0))


def add_parts(values):
    return jnp.sum(values, axis=0)


def merge_kernel(merge, parts, tiles, out, kept):
    merged = merge(parts[...])
    for d in range(out.shape[0]):
        out[d] = merged


def exchange_cols(copies, merge, tiles):
    parts = exchange(copies, "z")
    sends, tiles = pl.pallas_call(
        functools.partial(merge_kernel, merge),
        in_specs=[VMEM] * 2,
        out_specs=[VMEM] * 2,
        out_shape=[
            v32(lax.axis_size("x"), *parts.shape[1:]),
            pltpu.VMEM(tiles.shape, jnp.float32),
        ],
        input_output_aliases={1: 1},
        compiler_params=PARAMS,
        name="merge",
    )(parts, tiles)
    return exchange(sends, "x"), in_vmem(tiles)


def local(sources, targets, block_lists, live_counts):
    src_rows, features = sources.shape
    src_blocks = src_rows // BLK
    tgt_blocks = targets.shape[0] // BLK
    slots = block_lists.shape[2]
    n_z, n_x, n_tgt = (lax.axis_size(a) for a in ("z", "x", "tgt"))
    total_src = src_rows * n_z * n_x
    total_tgt = targets.shape[0] * n_tgt
    src_blocked = sources.reshape(src_blocks, BLK, features)
    tgt_blocked = targets.reshape(tgt_blocks, BLK, features)
    lists = (block_lists[:, 0, :].T, live_counts.T)
    tiles = v32(src_blocks, slots, BLK, BLK)
    row_shape, col_shape = v32(src_blocks, BLK), v32(tgt_blocks, BLK)
    row_sends, col_sends = v32(n_tgt, src_blocks, BLK), v32(n_z, tgt_blocks, BLK)
    row_scratch, col_scratch = v32(src_blocks, SUB, BLK), v32(tgt_blocks, SUB, BLK)

    tgt_vmem, z, rows, table = pl.pallas_call(
        functools.partial(cost_kernel, features=features),
        in_specs=[HBM] * 4,
        out_specs=[VMEM, VMEM, VMEM, SMEM],
        out_shape=[
            pltpu.VMEM(tgt_blocked.shape, jnp.bfloat16),
            tiles,
            row_sends,
            pltpu.SMEM((src_blocks * slots,), jnp.int32),
        ],
        scratch_shapes=[
            pltpu.SMEM((slots, src_blocks), jnp.int32),
            pltpu.SMEM((1, src_blocks), jnp.int32),
            pltpu.SMEM((src_blocks * slots,), jnp.int32),
            pltpu.SMEM((tgt_blocks,), jnp.int32),
            pltpu.VMEM(src_blocked.shape, jnp.bfloat16),
            col_scratch,
            row_scratch,
            pltpu.SemaphoreType.DMA((tgt_blocks + src_blocks,)),
            pltpu.SemaphoreType.DMA((2,)),
        ],
        compiler_params=PARAMS,
        name="cost",
    )(*[in_hbm(x) for x in (*lists, src_blocked, tgt_blocked)])
    table = pltpu.with_memory_space_constraint(table, pltpu.SMEM)

    w, row_lse, cols = pl.pallas_call(
        first_col_kernel,
        in_specs=[SMEM, VMEM, VMEM],
        out_specs=[VMEM, VMEM, VMEM],
        out_shape=[tiles, f32(src_blocks, BLK), col_sends],
        scratch_shapes=[col_scratch, col_scratch],
        input_output_aliases={1: 0},
        compiler_params=PARAMS,
        name="first_col",
    )(table, in_vmem(z), exchange(rows, "tgt"))

    col_parts, w = exchange_cols(cols, merge_lse, in_vmem(w))
    q, col_lse, rows = pl.pallas_call(
        first_row_kernel,
        in_specs=[SMEM, VMEM, VMEM],
        out_specs=[VMEM, VMEM, VMEM],
        out_shape=[tiles, f32(tgt_blocks, BLK), row_sends],
        scratch_shapes=[row_scratch],
        input_output_aliases={1: 0},
        compiler_params=PARAMS,
        name="first_row",
    )(table, w, col_parts)
    q = in_vmem(q)

    for sweep in range(1, ITERS):
        row_scale, cols = pl.pallas_call(
            functools.partial(col_kernel, share=total_tgt / total_src),
            in_specs=[SMEM, VMEM, VMEM],
            out_specs=[VMEM, VMEM],
            out_shape=[row_shape, col_sends],
            scratch_shapes=[col_scratch],
            compiler_params=PARAMS,
            name="col_sums",
        )(table, q, exchange(rows, "tgt"))
        col_parts, q = exchange_cols(cols, add_parts, q)
        if sweep < ITERS - 1:
            col_scale, rows = pl.pallas_call(
                row_kernel,
                in_specs=[SMEM, VMEM, VMEM],
                out_specs=[VMEM, VMEM],
                out_shape=[col_shape, row_sends],
                scratch_shapes=[row_scratch],
                compiler_params=PARAMS,
                name="row_sums",
            )(table, q, col_parts)

    tgt_vmem = in_vmem(tgt_vmem)
    block = v32(BLK + SUB, features)
    blocks = v32(2, BLK + SUB, features)
    halves = v32(2, BLK + SUB, features // 2)
    half = v32(BLK + SUB, features // 2)

    def swap(x, flip=1):
        return in_vmem(lax.ppermute(x, "tgt", [(t, t ^ flip) for t in range(n_tgt)]))

    def call(kernel, name, operands, out_shape, spec=VMEM):
        return pl.pallas_call(
            kernel,
            in_specs=[spec] + [VMEM] * (len(operands) - 1),
            out_specs=[VMEM] * len(out_shape),
            out_shape=out_shape,
            compiler_params=PARAMS,
            name=name,
        )(*operands)

    col_scale, own_far, other_far = call(
        far_kernel, "far", [table, q, col_parts, tgt_vmem], [col_shape, halves, halves], SMEM
    )
    low, high = call(
        far_sum_kernel, "far_sum", [in_vmem(own_far), swap(other_far)], [half, half]
    )
    (low, high), col_scale = lax.optimization_barrier(((low, high), col_scale))
    low, high = swap(low, 2), swap(high, 6)
    own_side, other_side = call(
        side_kernel, "side", [table, q, in_vmem(col_scale), tgt_vmem], [blocks, blocks], SMEM
    )
    own_side, col_scale = lax.optimization_barrier((own_side, col_scale))
    own_end, other_end = call(
        end_kernel, "end", [table, q, in_vmem(col_scale), tgt_vmem], [block, block], SMEM
    )
    first, second = call(
        side_sum_kernel,
        "side_sum",
        [in_vmem(own_side), swap(other_side), low, high],
        [block, block],
    )
    mapped = call(
        finish_kernel,
        "finish",
        [swap(first, 2), swap(second, 6), in_vmem(own_end), swap(other_end)],
        [f32(BLK, features)],
    )[0]

    src_square = jnp.sum(jnp.square(sources.astype(jnp.float32)), -1)
    row_potential = (
        EPSILON * (jnp.log(row_scale) - LN2 * row_lse - math.log(total_src))
    ).reshape(src_rows) + src_square / features
    col_potential = EPSILON * (
        jnp.log(col_scale) - LN2 * col_lse + (math.log(total_src) - math.log(total_tgt))
    )
    return (mapped, row_potential, col_potential.reshape(tgt_blocks * BLK))


def solution(mesh):
    n_src, n_tgt = mesh.shape["src"], mesh.shape["tgt"]
    grid = Mesh(mesh.devices.reshape(n_src // CHIPS_X, CHIPS_X, n_tgt), ("z", "x", "tgt"))
    in_specs = (P(SRC, None), P("tgt", None), P(SRC, "tgt", None), P(SRC, "tgt"))
    out_specs = (P((*SRC, "tgt"), None), P(SRC), P("tgt"))
    return jax.shard_map(local, mesh=grid, in_specs=in_specs, out_specs=out_specs, check_vma=False)
```

time: 172 us -> 153 us (0.89)
  waiting for transfers between devices: 10.9 us -> 27.9 us
  starting transfers between devices: 20.5 us -> 6.63 us
  Pallas kernels: 37.8 us -> 25.2 us
  blocking collectives: 97.3 us -> 90.4 us
    ppermute x10 -> x7, waiting for transfers between devices: 6.9 us -> 27.9 us  [swap(): lax.ppermute(x, 'tgt', [(t, t ^ flip) for t in range(n_tgt)])]
    pallas_call x7 -> x12, Pallas kernels: 21.1 us -> 12.8 us  [the longest x6 5.83 us: call(): pl.pallas_call(kernel, in_specs=[spec] + [VMEM] * (len(operands) - 1), ou...]
    ppermute x10 -> x7, starting transfers between devices: 14.5 us -> 6.63 us  [swap(): lax.ppermute(x, 'tgt', [(t, t ^ flip) for t in range(n_tgt)])]
    all_to_all x6 -> x9, blocking collectives: 97.3 us -> 90.4 us  [exchange(): return in_vmem(lax.all_to_all(copies, axis, 0, 0))]
    all_to_all x1 -> x0, starting transfers between devices: 6.02 us -> none  [local(): lax.all_to_all(mass, 'tgt', 0, 0)]
    all_to_all x1 -> x0, waiting for transfers between devices: 4 us -> none  [local(): lax.all_to_all(mass, 'tgt', 0, 0)]
    pallas_call x2, Pallas kernels: 5.52 us -> 3.06 us  [local(): pl.pallas_call(functools.partial(col_kernel, share=total_tgt / total_src)...]
    pallas_call x1, Pallas kernels: 11.2 us -> 9.33 us  [local(): pl.pallas_call(functools.partial(cost_kernel, features=features), in_spec...]
  transfers between devices with their start and end apart: 11 -> 7, of which waited for: 3 -> 5; matrix products, arithmetic and copies ran while one was open for 2% -> 1% of each run, Pallas kernels for 5% -> 1%
where the time goes in v3:
time: 153 us
  blocking collectives  90.4 us (59%)
  waiting for transfers between devices  27.9 us (18%)
  Pallas kernels  25.2 us (16%)
  starting transfers between devices  6.63 us (4%)
    all_to_all x9, blocking collectives, exchange(): return in_vmem(lax.all_to_all(copies, axis, 0, 0))  90.4 us
    ppermute x7, waiting for transfers between devices, swap(): lax.ppermute(x, 'tgt', [(t, t ^ flip) for t in range(n_tgt)])  27.9 us
    pallas_call x1, Pallas kernels, local(): pl.pallas_call(functools.partial(cost_kernel, features=features), in_spec...  9.33 us
    ppermute x7, starting transfers between devices, swap(): lax.ppermute(x, 'tgt', [(t, t ^ flip) for t in range(n_tgt)])  6.63 us
    pallas_call x6, Pallas kernels, call(): pl.pallas_call(kernel, in_specs=[spec] + [VMEM] * (len(operands) - 1), ou...  5.83 us
    pallas_call x1, Pallas kernels, local(): pl.pallas_call(first_col_kernel, in_specs=[SMEM, VMEM, VMEM], out_specs=[...  3.09 us
  transfers between devices with their start and end apart: 7, of which 5 were waited for; matrix products, arithmetic and copies ran while one was open for 1% of the time, Pallas kernels for 1%

profile of v3, /device:TPU:1, one launch (start us, length us, event | category | flops | bytes accessed | tf_op | source)
XLA Modules:
  0.0 152.7 jit_solution(965174944075548167)
XLA Ops:
  0.6 9.3 %cost.1 = (bf16[16,256,768]{2,1,0:T(8,128)(2,1)S(1)}, f32[8,4,256,256]{3,2,1,0:T(8,128)S(1)}, f32[8,8,256]{2,1,0:T(8,128)S(1)}, s32[32]{0:T(128)S(4)}) custom-call(s32[4,8]{1,0:T(4,128)} %bitcast.16, s32[1,8]{1,0:T(1,128)} %bitcast.17, bf16[8,256,768]{2,1,0:T(8,128)(2,1)} %bitcast.12, bf16[16,256,768]{2,1,0:T(8,128)(2,1)} %bitcast.13), custom_call_target="tpu_custom_call" | custom-call | tf_op jit(solution)/shard_map/cost/pallas_call | solution.py:392
  10.0 10.8 %all_to_all.45.row_parts = f32[8,8,256]{2,1,0:T(8,128)S(1)} all-to-all(f32[8,8,256]{2,1,0:T(8,128)S(1)} %get-tuple-element.41), channel_id=1, replica_groups=mesh['z'=8,'x'=4,'tgt'=8] {'tgt'}, dimensions={0} | all-to-all | bytes 131072 | tf_op jit(solution)/shard_map/all_to_all | solution.py:346
  20.8 3.1 %first_col.1 = (f32[8,4,256,256]{3,2,1,0:T(8,128)S(1)}, f32[8,256]{1,0:T(8,128)S(1)}, f32[8,16,256]{2,1,0:T(8,128)S(1)}) custom-call(s32[32]{0:T(128)S(4)} %get-tuple-element.39.table, f32[8,4,256,256]{3,2,1,0:T(8,128)S(1)} %get-tuple-element.40.z_ref, f32[8,8,256]{2,1,0:T(8,128)S(1)} %all_to_all.45.row_parts), custom_call_target="tpu_custom_call", output_to_operand_aliasing={{0}: (1, {})} | custom-call | tf_op jit(solution)/shard_map/first_col/pallas_call | solution.py:418
  23.9 15.6 %all_to_all.46.parts = f32[8,16,256]{2,1,0:T(8,128)S(1)} all-to-all(f32[8,16,256]{2,1,0:T(8,128)S(1)} %get-tuple-element.42), channel_id=1, replica_groups=mesh['z'=8,'x'=4,'tgt'=8] {'z'}, dimensions={0} | all-to-all | bytes 262144 | tf_op jit(solution)/shard_map/all_to_all | solution.py:346
  39.6 8.3 %all_to_all.47.col_parts = f32[4,16,256]{2,1,0:T(8,128)S(1)} all-to-all(f32[4,16,256]{2,1,0:T(8,128)S(1)} %get-tuple-element.45), channel_id=1, replica_groups=mesh['z'=8,'x'=4,'tgt'=8] {'x'}, dimensions={0} | all-to-all | bytes 131072 | tf_op jit(solution)/shard_map/all_to_all | solution.py:346
  47.9 2.1 %first_row.1 = (f32[8,4,256,256]{3,2,1,0:T(8,128)S(1)}, f32[16,256]{1,0:T(8,128)S(1)}, f32[8,8,256]{2,1,0:T(8,128)S(1)}) custom-call(s32[32]{0:T(128)S(4)} %get-tuple-element.39.table, f32[8,4,256,256]{3,2,1,0:T(8,128)S(1)} %get-tuple-element.44.w_ref, f32[4,16,256]{2,1,0:T(8,128)S(1)} %all_to_all.47.col_parts), custom_call_target="tpu_custom_call", output_to_operand_aliasing={{0}: (1, {})} | custom-call | tf_op jit(solution)/shard_map/first_row/pallas_call | solution.py:430
  50.0 11.0 %all_to_all.48.row_parts = f32[8,8,256]{2,1,0:T(8,128)S(1)} all-to-all(f32[8,8,256]{2,1,0:T(8,128)S(1)} %get-tuple-element.47), channel_id=1, replica_groups=mesh['z'=8,'x'=4,'tgt'=8] {'tgt'}, dimensions={0} | all-to-all | bytes 131072 | tf_op jit(solution)/shard_map/all_to_all | solution.py:346
  61.0 1.7 %col_sums.2 = (f32[8,256]{1,0:T(8,128)}, f32[8,16,256]{2,1,0:T(8,128)S(1)}) custom-call(s32[32]{0:T(128)S(4)} %get-tuple-element.39.table, f32[8,4,256,256]{3,2,1,0:T(8,128)S(1)} %get-tuple-element.46.q_ref.tiles, f32[8,8,256]{2,1,0:T(8,128)S(1)} %all_to_all.48.row_parts), custom_call_target="tpu_custom_call" | custom-call | tf_op jit(solution)/shard_map/col_sums/pallas_call | solution.py:443
  62.7 10.1 %all_to_all.49.parts = f32[8,16,256]{2,1,0:T(8,128)S(1)} all-to-all(f32[8,16,256]{2,1,0:T(8,128)S(1)} %get-tuple-element.48), channel_id=1, replica_groups=mesh['z'=8,'x'=4,'tgt'=8] {'z'}, dimensions={0} | all-to-all | bytes 262144 | tf_op jit(solution)/shard_map/all_to_all | solution.py:346
  72.9 6.8 %all_to_all.50.col_parts = f32[4,16,256]{2,1,0:T(8,128)S(1)} all-to-all(f32[4,16,256]{2,1,0:T(8,128)S(1)} %get-tuple-element.50), channel_id=1, replica_groups=mesh['z'=8,'x'=4,'tgt'=8] {'x'}, dimensions={0} | all-to-all | bytes 131072 | tf_op jit(solution)/shard_map/all_to_all | solution.py:346
  79.7 1.7 %row_sums.1 = (f32[16,256]{1,0:T(8,128)}, f32[8,8,256]{2,1,0:T(8,128)S(1)}) custom-call(s32[32]{0:T(128)S(4)} %get-tuple-element.39.table, f32[8,4,256,256]{3,2,1,0:T(8,128)S(1)} %get-tuple-element.49.q_ref.tiles, f32[4,16,256]{2,1,0:T(8,128)S(1)} %all_to_all.50.col_parts), custom_call_target="tpu_custom_call" | custom-call | tf_op jit(solution)/shard_map/row_sums/pallas_call | solution.py:454
  81.4 10.6 %all_to_all.51.row_parts = f32[8,8,256]{2,1,0:T(8,128)S(1)} all-to-all(f32[8,8,256]{2,1,0:T(8,128)S(1)} %get-tuple-element.51), channel_id=1, replica_groups=mesh['z'=8,'x'=4,'tgt'=8] {'tgt'}, dimensions={0} | all-to-all | bytes 131072 | tf_op jit(solution)/shard_map/all_to_all | solution.py:346
  92.0 1.3 col_sums.3
  93.3 10.1 %all_to_all.52.parts = f32[8,16,256]{2,1,0:T(8,128)S(1)} all-to-all(f32[8,16,256]{2,1,0:T(8,128)S(1)} %get-tuple-element.52), channel_id=1, replica_groups=mesh['z'=8,'x'=4,'tgt'=8] {'z'}, dimensions={0} | all-to-all | bytes 262144 | tf_op jit(solution)/shard_map/all_to_all | solution.py:346
  103.5 6.8 %all_to_all.53.col_parts = f32[4,16,256]{2,1,0:T(8,128)S(1)} all-to-all(f32[4,16,256]{2,1,0:T(8,128)S(1)} %get-tuple-element.54), channel_id=1, replica_groups=mesh['z'=8,'x'=4,'tgt'=8] {'x'}, dimensions={0} | all-to-all | bytes 131072 | tf_op jit(solution)/shard_map/all_to_all | solution.py:346
  110.4 1.3 far.1
  111.6 3.5 %collective-permute-start = (f32[2,264,384]{2,1,0:T(8,128)S(1)}, f32[2,264,384]{2,1,0:T(8,128)S(1)}, u32[]{:S(2)}, u32[]{:S(2)}) collective-permute-start(f32[2,264,384]{2,1,0:T(8,128)S(1)} %get-tuple-element.57), channel_id=1, source_target_pairs={{0,1},{1,0},{2,3},{3,2},{4,5},{5,4},{6,7},{7,6},{8,9},{9,8},{10,11... | collective-permute-start | bytes 2433032 | tf_op jit(solution)/shard_map/ppermute | solution.py:471
  115.1 1.9 %collective-permute-done.other = f32[2,264,384]{2,1,0:T(8,128)S(1)} collective-permute-done((f32[2,264,384]{2,1,0:T(8,128)S(1)}, f32[2,264,384]{2,1,0:T(8,128)S(1)}, u32[]{:S(2)}, u32[]{:S(2)}) %collective-permute-start) | collective-permute-done | bytes 811040 | tf_op jit(solution)/shard_map/ppermute | solution.py:471
  117.1 0.1 far_sum.1
  117.2 2.0 %side.1 = (f32[2,264,768]{2,1,0:T(8,128)S(1)}, f32[2,264,768]{2,1,0:T(8,128)S(1)}) custom-call(s32[32]{0:T(128)S(4)} %get-tuple-element.39.table, f32[8,4,256,256]{3,2,1,0:T(8,128)S(1)} %get-tuple-element.53.q_ref, f32[16,256]{1,0:T(8,128)S(1)} %get-tuple-element.69.col_scale, bf16[16,256,768]{2,1,0:T(8,128)(2,1)S(1)} %get-tuple-element.55.tgt), custom_call_target="tpu_custom_call" | custom-call | tf_op jit(solution)/shard_map/side/pallas_call | solution.py:474
  119.2 0.5 collective-permute-start.1
  119.7 0.3 collective-permute-start.2
  120.0 0.7 collective-permute-start.3
  120.7 0.0 copy-start
  120.7 1.0 end.1
  121.7 0.8 collective-permute-start.6
  122.5 8.0 %collective-permute-done.2.low = f32[264,384]{1,0:T(8,128)S(1)} collective-permute-done((f32[264,384]{1,0:T(8,128)S(1)}, f32[264,384]{1,0:T(8,128)S(1)}, u32[]{:S(2)}, u32[]{:S(2)}) %collective-permute-start.2) | collective-permute-done | bytes 405536 | tf_op jit(solution)/shard_map/ppermute | solution.py:471
  130.5 1.2 collective-permute-done.3.high
  131.7 0.0 collective-permute-done.1.other
  131.7 0.2 side_sum.1
  131.9 0.1 collective-permute-start.4
  132.0 0.8 collective-permute-start.5
  132.8 0.0 copy-done
  132.8 0.7 multiply_reduce_fusion
  133.6 0.6 multiply_add_fusion
  134.2 0.6 copy.13
  134.8 0.0 collective-permute-done.6.other
  134.8 15.5 %collective-permute-done.4.first = f32[264,768]{1,0:T(8,128)S(1)} collective-permute-done((f32[264,768]{1,0:T(8,128)S(1)}, f32[264,768]{1,0:T(8,128)S(1)}, u32[]{:S(2)}, u32[]{:S(2)}) %collective-permute-start.4) | collective-permute-done | bytes 811040 | tf_op jit(solution)/shard_map/ppermute | solution.py:471
  150.3 1.2 collective-permute-done.5.second
  151.5 1.2 finish.1
  (6 shorter events, 0.1 us)
Async XLA Ops:
  111.6 5.4 %collective-permute-start = (f32[2,264,384]{2,1,0:T(8,128)S(1)}, f32[2,264,384]{2,1,0:T(8,128)S(1)}, u32[]{:S(2)}, u32[]{:S(2)}) collective-permute-start(f32[2,264,384]{2,1,0:T(8,128)S(1)} %get-tuple-element.57), channel_id=1, source_target_pairs={{0,1},{1,0},{2,3},{3,2},{4,5},{5,4},{6,7},{7,6},{8,9},{9,8},{10,11... | collective-permute-start | bytes 2433032 | tf_op jit(solution)/shard_map/ppermute | solution.py:471
  119.2 12.5 %collective-permute-start.1 = (f32[2,264,768]{2,1,0:T(8,128)S(1)}, f32[2,264,768]{2,1,0:T(8,128)S(1)}, u32[]{:S(2)}, u32[]{:S(2)}) collective-permute-start(f32[2,264,768]{2,1,0:T(8,128)S(1)} %get-tuple-element.64), channel_id=1, source_target_pairs={{0,1},{1,0},{2,3},{3,2},{4,5},{5,4},{6,7},{7,6},{8,9},{9,8},{10,11... | collective-permute-start | bytes 4866056 | tf_op jit(solution)/shard_map/ppermute | solution.py:471
  119.7 10.8 %collective-permute-start.2 = (f32[264,384]{1,0:T(8,128)S(1)}, f32[264,384]{1,0:T(8,128)S(1)}, u32[]{:S(2)}, u32[]{:S(2)}) collective-permute-start(f32[264,384]{1,0:T(8,128)S(1)} %get-tuple-element.65), channel_id=1, source_target_pairs={{0,2},{1,3},{2,0},{3,1},{4,6},{5,7},{6,4},{7,5},{8,10},{9,11},{10,... | collective-permute-start | bytes 1216520 | tf_op jit(solution)/shard_map/ppermute | solution.py:471
  120.0 11.7 %collective-permute-start.3 = (f32[264,384]{1,0:T(8,128)S(1)}, f32[264,384]{1,0:T(8,128)S(1)}, u32[]{:S(2)}, u32[]{:S(2)}) collective-permute-start(f32[264,384]{1,0:T(8,128)S(1)} %get-tuple-element.66), channel_id=1, source_target_pairs={{0,6},{1,7},{2,4},{3,5},{4,2},{5,3},{6,0},{7,1},{8,14},{9,15},{10,... | collective-permute-start | bytes 1216520 | tf_op jit(solution)/shard_map/ppermute | solution.py:471
  120.7 12.2 %copy-start = (bf16[2048,768]{1,0:T(8,128)(2,1)S(1)}, bf16[2048,768]{1,0:T(8,128)(2,1)}, u32[]{:S(2)}) copy-start(bf16[2048,768]{1,0:T(8,128)(2,1)} %param.4) | copy-start | bytes 9437188
  121.7 13.1 %collective-permute-start.6 = (f32[264,768]{1,0:T(8,128)S(1)}, f32[264,768]{1,0:T(8,128)S(1)}, u32[]{:S(2)}, u32[]{:S(2)}) collective-permute-start(f32[264,768]{1,0:T(8,128)S(1)} %get-tuple-element.71), channel_id=1, source_target_pairs={{0,1},{1,0},{2,3},{3,2},{4,5},{5,4},{6,7},{7,6},{8,9},{9,8},{10,11... | collective-permute-start | bytes 2433032 | tf_op jit(solution)/shard_map/ppermute | solution.py:471
  131.9 18.4 %collective-permute-start.4 = (f32[264,768]{1,0:T(8,128)S(1)}, f32[264,768]{1,0:T(8,128)S(1)}, u32[]{:S(2)}, u32[]{:S(2)}) collective-permute-start(f32[264,768]{1,0:T(8,128)S(1)} %get-tuple-element.67), channel_id=1, source_target_pairs={{0,2},{1,3},{2,0},{3,1},{4,6},{5,7},{6,4},{7,5},{8,10},{9,11},{10,... | collective-permute-start | bytes 2433032 | tf_op jit(solution)/shard_map/ppermute | solution.py:471
  132.0 19.5 %collective-permute-start.5 = (f32[264,768]{1,0:T(8,128)S(1)}, f32[264,768]{1,0:T(8,128)S(1)}, u32[]{:S(2)}, u32[]{:S(2)}) collective-permute-start(f32[264,768]{1,0:T(8,128)S(1)} %get-tuple-element.68), channel_id=1, source_target_pairs={{0,6},{1,7},{2,4},{3,5},{4,2},{5,3},{6,0},{7,1},{8,14},{9,15},{10,... | collective-permute-start | bytes 2433032 | tf_op jit(solution)/shard_map/ppermute | solution.py:471

commit v4 on v3

--- a/solution.py
+++ b/solution.py
@@ -18,8 +18,10 @@
 LANES = 128
 SUB = 8
 GROUP = 8
-CHIPS_X = 4
-SRC = ("z", "x")
+X_HALVES = 2
+X_AXES = ("x_high", "x_low")
+SRC = ("z", *X_AXES)
+GATHER = ("z", "x_low")
 
 VMEM = pl.BlockSpec(memory_space=pltpu.VMEM)
 SMEM = pl.BlockSpec(memory_space=pltpu.SMEM)
@@ -81,9 +83,14 @@
     return functools.reduce(op, lane_halves(tile))
 
 
+def add_parts(values):
+    pairs = [values[i] + values[i + 1] for i in range(0, values.shape[0], 2)]
+    return functools.reduce(jnp.add, pairs)
+
+
 def merge_lse(values):
     peak = jnp.max(values, axis=0)
-    return peak + jnp.log2(jnp.sum(jnp.exp2(values - peak[None]), axis=0))
+    return peak + jnp.log2(add_parts(jnp.exp2(values - peak[None])))
 
 
 def spread(out, scratch, n):
@@ -163,7 +170,7 @@
 
     lax.fori_loop(0, src_blocks * slots // GROUP, cross_terms, 0)
 
-    @pl.loop(0, src_blocks, unroll=2)
+    @pl.loop(0, src_blocks, unroll=4)
     def _(b):
         peak = None
         for k in range(slots):
@@ -236,7 +243,7 @@
 
 def col_kernel(table, q_ref, row_parts, row_scale, cols, sums, *, share):
     src_blocks, slots, tgt_blocks = q_ref.shape[0], q_ref.shape[1], sums.shape[0]
-    row_scale[...] = share / jnp.sum(row_parts[...], axis=0)
+    row_scale[...] = share / add_parts(row_parts[...])
     sums[...] = jnp.zeros(sums.shape, jnp.float32)
 
     @pl.loop(0, src_blocks)
@@ -252,7 +259,7 @@
 
 
 def row_kernel(table, q_ref, col_parts, col_scale, rows, totals):
-    col_scale[...] = 1.0 / jnp.sum(col_parts[...], axis=0)
+    col_scale[...] = 1.0 / add_parts(col_parts[...])
 
     def tile(b, k, t):
         return q_ref[b, k] * col_scale[pl.ds(t, 1), :]
@@ -288,23 +295,15 @@
 
 
 def far_kernel(table, q_ref, col_parts, tgt, col_scale, own, other):
-    col_scale[...] = 1.0 / jnp.sum(col_parts[...], axis=0)
+    col_scale[...] = 1.0 / add_parts(col_parts[...])
     for sibling, out in ((True, other), (False, own)):
         halves = [out.at[0], out.at[1]]
         project(table, q_ref, col_scale, tgt, block_at(2, sibling), halves, out.shape[2])
 
 
-def side_kernel(table, q_ref, col_scale, tgt, own, other):
-    @pl.loop(0, 2)
-    def _(i):
-        for sibling, out in ((True, other), (False, own)):
-            block = block_at(2 * i + 1, sibling)
-            project(table, q_ref, col_scale, tgt, block, [out.at[i]], out.shape[2])
-
-
-def end_kernel(table, q_ref, col_scale, tgt, own, other):
+def block_kernel(flip, table, q_ref, col_scale, tgt, own, other):
     for sibling, out in ((True, other), (False, own)):
-        project(table, q_ref, col_scale, tgt, block_at(0, sibling), [out], out.shape[1])
+        project(table, q_ref, col_scale, tgt, block_at(flip, sibling), [out], out.shape[1])
 
 
 def far_sum_kernel(own, other, low, high):
@@ -312,12 +311,12 @@
     high[...] = own[1] + other[1]
 
 
-def side_sum_kernel(own, other, low, high, first, second):
-    width = low.shape[1]
-    first[:, :width] = own[0, :, :width] + other[0, :, :width]
-    first[:, width:] = own[0, :, width:] + other[0, :, width:] + high[...]
-    second[:, :width] = own[1, :, :width] + other[1, :, :width] + low[...]
-    second[:, width:] = own[1, :, width:] + other[1, :, width:]
+def side_sum_kernel(way, own, other, received, out):
+    width = received.shape[1]
+    for n in range(2):
+        columns = slice(n * width, (n + 1) * width)
+        total = own[:, columns] + other[:, columns]
+        out[:, columns] = total + received[...] if n == way else total
 
 
 def finish_kernel(first, second, own, other, out):
@@ -346,31 +345,27 @@
     return in_vmem(lax.all_to_all(copies, axis, 0, 0))
 
 
-def add_parts(values):
-    return jnp.sum(values, axis=0)
-
-
-def merge_kernel(merge, parts, tiles, out, kept):
-    merged = merge(parts[...])
+def merge_kernel(merge, own, other, tiles, out, kept):
+    merged = merge(jnp.concatenate([own[...], other[...]], axis=0))
     for d in range(out.shape[0]):
         out[d] = merged
 
 
-def exchange_cols(copies, merge, tiles):
-    parts = exchange(copies, "z")
+def exchange_cols(cols, merge, tiles):
+    pairs = [(i, i ^ 3) for i in range(X_HALVES**2)]
     sends, tiles = pl.pallas_call(
         functools.partial(merge_kernel, merge),
-        in_specs=[VMEM] * 2,
+        in_specs=[VMEM] * 3,
         out_specs=[VMEM] * 2,
         out_shape=[
-            v32(lax.axis_size("x"), *parts.shape[1:]),
+            v32(lax.axis_size(GATHER), *cols.shape[1:]),
             pltpu.VMEM(tiles.shape, jnp.float32),
         ],
-        input_output_aliases={1: 1},
+        input_output_aliases={2: 1},
         compiler_params=PARAMS,
         name="merge",
-    )(parts, tiles)
-    return exchange(sends, "x"), in_vmem(tiles)
+    )(in_vmem(cols), in_vmem(lax.ppermute(in_vmem(cols), X_AXES, pairs)), tiles)
+    return exchange(sends, GATHER), in_vmem(tiles)
 
 
 def local(sources, targets, block_lists, live_counts):
@@ -378,15 +373,15 @@
     src_blocks = src_rows // BLK
     tgt_blocks = targets.shape[0] // BLK
     slots = block_lists.shape[2]
-    n_z, n_x, n_tgt = (lax.axis_size(a) for a in ("z", "x", "tgt"))
-    total_src = src_rows * n_z * n_x
+    n_src, n_gather, n_tgt = (lax.axis_size(a) for a in (SRC, GATHER, "tgt"))
+    total_src = src_rows * n_src
     total_tgt = targets.shape[0] * n_tgt
     src_blocked = sources.reshape(src_blocks, BLK, features)
     tgt_blocked = targets.reshape(tgt_blocks, BLK, features)
     lists = (block_lists[:, 0, :].T, live_counts.T)
     tiles = v32(src_blocks, slots, BLK, BLK)
     row_shape, col_shape = v32(src_blocks, BLK), v32(tgt_blocks, BLK)
-    row_sends, col_sends = v32(n_tgt, src_blocks, BLK), v32(n_z, tgt_blocks, BLK)
+    row_sends, col_sends = v32(n_tgt, src_blocks, BLK), v32(1, tgt_blocks, BLK)
     row_scratch, col_scratch = v32(src_blocks, SUB, BLK), v32(tgt_blocks, SUB, BLK)
 
     tgt_vmem, z, rows, table = pl.pallas_call(
@@ -463,7 +458,6 @@
 
     tgt_vmem = in_vmem(tgt_vmem)
     block = v32(BLK + SUB, features)
-    blocks = v32(2, BLK + SUB, features)
     halves = v32(2, BLK + SUB, features // 2)
     half = v32(BLK + SUB, features // 2)
 
@@ -483,24 +477,38 @@
     col_scale, own_far, other_far = call(
         far_kernel, "far", [table, q, col_parts, tgt_vmem], [col_shape, halves, halves], SMEM
     )
+    sides = []
+    for flip in (1, 3):
+        sides.append(
+            call(
+                functools.partial(block_kernel, flip),
+                "side",
+                [table, q, in_vmem(col_scale), tgt_vmem],
+                [block, block],
+                SMEM,
+            )
+        )
     low, high = call(
         far_sum_kernel, "far_sum", [in_vmem(own_far), swap(other_far)], [half, half]
     )
-    (low, high), col_scale = lax.optimization_barrier(((low, high), col_scale))
+    (low, high), sides, col_scale = lax.optimization_barrier(((low, high), sides, col_scale))
     low, high = swap(low, 2), swap(high, 6)
-    own_side, other_side = call(
-        side_kernel, "side", [table, q, in_vmem(col_scale), tgt_vmem], [blocks, blocks], SMEM
+    own_end, other_end = call(
+        functools.partial(block_kernel, 0),
+        "end",
+        [table, q, in_vmem(col_scale), tgt_vmem],
+        [block, block],
+        SMEM,
     )
-    own_side, col_scale = lax.optimization_barrier((own_side, col_scale))
-    own_end, other_end = call(
-        end_kernel, "end", [table, q, in_vmem(col_scale), tgt_vmem], [block, block], SMEM
-    )
-    first, second = call(
-        side_sum_kernel,
-        "side_sum",
-        [in_vmem(own_side), swap(other_side), low, high],
-        [block, block],
-    )
+    first, second = [
+        call(
+            functools.partial(side_sum_kernel, way),
+            "side_sum",
+            [in_vmem(own), swap(other), received],
+            [block],
+        )[0]
+        for way, (own, other), received in ((1, sides[0], high), (0, sides[1], low))
+    ]
     mapped = call(
         finish_kernel,
         "finish",
@@ -520,7 +528,8 @@
 
 def solution(mesh):
     n_src, n_tgt = mesh.shape["src"], mesh.shape["tgt"]
-    grid = Mesh(mesh.devices.reshape(n_src // CHIPS_X, CHIPS_X, n_tgt), ("z", "x", "tgt"))
+    n_z = n_src // X_HALVES**2
+    grid = Mesh(mesh.devices.reshape(n_z, X_HALVES, X_HALVES, n_tgt), (*SRC, "tgt"))
     in_specs = (P(SRC, None), P("tgt", None), P(SRC, "tgt", None), P(SRC, "tgt"))
     out_specs = (P((*SRC, "tgt"), None), P(SRC), P("tgt"))
     return jax.shard_map(local, mesh=grid, in_specs=in_specs, out_specs=out_specs, check_vma=False)

time: 153 us -> 146 us (0.954)
  blocking collectives: 90.4 us -> 74 us
  starting transfers between devices: 6.63 us -> 14.1 us
    all_to_all x9 -> x6, blocking collectives: 90.4 us -> 74 us  [exchange(): return in_vmem(lax.all_to_all(copies, axis, 0, 0))]
    ppermute x0 -> x3, starting transfers between devices: none -> 7.02 us  [exchange_cols(): lax.ppermute(in_vmem(cols), X_AXES, pairs)]
    ppermute x0 -> x3, waiting for transfers between devices: none -> 4.55 us  [exchange_cols(): lax.ppermute(in_vmem(cols), X_AXES, pairs)]
    ppermute x7 -> x8, waiting for transfers between devices: 27.9 us -> 24.3 us  [swap(): lax.ppermute(x, 'tgt', [(t, t ^ flip) for t in range(n_tgt)])]
    ppermute x7 -> x8, starting transfers between devices: 6.63 us -> 7.12 us  [swap(): lax.ppermute(x, 'tgt', [(t, t ^ flip) for t in range(n_tgt)])]
    pallas_call x6 -> x8, Pallas kernels: 5.83 us -> 5.84 us  [call(): pl.pallas_call(kernel, in_specs=[spec] + [VMEM] * (len(operands) - 1), ou...]
  transfers between devices with their start and end apart: 7 -> 11, of which waited for: 5 -> 5; matrix products, arithmetic and copies ran while one was open for 1% -> 1% of each run, Pallas kernels for 1% -> 2%
where the time goes in v4:
time: 146 us; the launch traced here: 145 us
  blocking collectives  74 us (51%)
  waiting for transfers between devices  28.9 us (20%)
  Pallas kernels  25.3 us (17%)
  starting transfers between devices  14.1 us (10%)
    all_to_all x6, blocking collectives, exchange(): return in_vmem(lax.all_to_all(copies, axis, 0, 0))  74 us
    ppermute x8, waiting for transfers between devices, swap(): lax.ppermute(x, 'tgt', [(t, t ^ flip) for t in range(n_tgt)])  24.3 us
    pallas_call x1, Pallas kernels, local(): pl.pallas_call(functools.partial(cost_kernel, features=features), in_spec...  9.46 us
    ppermute x8, starting transfers between devices, swap(): lax.ppermute(x, 'tgt', [(t, t ^ flip) for t in range(n_tgt)])  7.12 us
    ppermute x3, starting transfers between devices, exchange_cols(): lax.ppermute(in_vmem(cols), X_AXES, pairs)  7.02 us
    pallas_call x8, Pallas kernels, call(): pl.pallas_call(kernel, in_specs=[spec] + [VMEM] * (len(operands) - 1), ou...  5.84 us
    ppermute x3, waiting for transfers between devices, exchange_cols(): lax.ppermute(in_vmem(cols), X_AXES, pairs)  4.55 us
    pallas_call x1, Pallas kernels, local(): pl.pallas_call(first_col_kernel, in_specs=[SMEM, VMEM, VMEM], out_specs=[...  3.08 us
  transfers between devices with their start and end apart: 11, of which 5 were waited for; matrix products, arithmetic and copies ran while one was open for 1% of the time, Pallas kernels for 2%

profile of v4, /device:TPU:1, one launch (start us, length us, event | category | flops | bytes accessed | tf_op | source)
XLA Modules:
  0.0 145.1 jit_solution(13012057603234633696)
XLA Ops:
  0.6 9.5 %cost.1 = (bf16[16,256,768]{2,1,0:T(8,128)(2,1)S(1)}, f32[8,4,256,256]{3,2,1,0:T(8,128)S(1)}, f32[8,8,256]{2,1,0:T(8,128)S(1)}, s32[32]{0:T(128)S(4)}) custom-call(s32[4,8]{1,0:T(4,128)} %bitcast.16, s32[1,8]{1,0:T(1,128)} %bitcast.17, bf16[8,256,768]{2,1,0:T(8,128)(2,1)} %bitcast.12, bf16[16,256,768]{2,1,0:T(8,128)(2,1)} %bitcast.13), custom_call_target="tpu_custom_call" | custom-call | tf_op jit(solution)/shard_map/cost/pallas_call | solution.py:387
  10.1 10.4 %all_to_all.30.row_parts = f32[8,8,256]{2,1,0:T(8,128)S(1)} all-to-all(f32[8,8,256]{2,1,0:T(8,128)S(1)} %get-tuple-element.43), channel_id=1, replica_groups=mesh['z'=8,'x_high'=2,'x_low'=2,'tgt'=8] {'tgt'}, dimensions={0} | all-to-all | bytes 131072 | tf_op jit(solution)/shard_map/all_to_all | solution.py:345
  20.5 3.1 %first_col.1 = (f32[8,4,256,256]{3,2,1,0:T(8,128)S(1)}, f32[8,256]{1,0:T(8,128)S(1)}, f32[1,16,256]{2,1,0:T(8,128)S(1)}) custom-call(s32[32]{0:T(128)S(4)} %get-tuple-element.41.table, f32[8,4,256,256]{3,2,1,0:T(8,128)S(1)} %get-tuple-element.42.z_ref, f32[8,8,256]{2,1,0:T(8,128)S(1)} %all_to_all.30.row_parts), custom_call_target="tpu_custom_call", output_to_operand_aliasing={{0}: (1, {})} | custom-call | tf_op jit(solution)/shard_map/first_col/pallas_call | solution.py:413
  23.6 2.4 %collective-permute-start = (f32[1,16,256]{2,1,0:T(8,128)S(1)}, f32[1,16,256]{2,1,0:T(8,128)S(1)}, u32[]{:S(2)}, u32[]{:S(2)}) collective-permute-start(f32[1,16,256]{2,1,0:T(8,128)S(1)} %get-tuple-element.44.own), channel_id=1, source_target_pairs={{0,24},{8,16},{16,8},{24,0},{1,25},{9,17},{17,9},{25,1},{2,26},{10... | collective-permute-start | bytes 49160 | tf_op jit(solution)/shard_map/ppermute | solution.py:367
  26.0 1.4 collective-permute-done.other
  27.5 17.8 %all_to_all.31.col_parts = f32[16,16,256]{2,1,0:T(8,128)S(1)} all-to-all(f32[16,16,256]{2,1,0:T(8,128)S(1)} %get-tuple-element.47), channel_id=1, replica_groups=mesh['z'=8,'x_high'=2,'x_low'=2,'tgt'=8] {'z','x_low'}, dimensions={0} | all-to-all | bytes 524288 | tf_op jit(solution)/shard_map/all_to_all | solution.py:345
  45.3 2.1 %first_row.1 = (f32[8,4,256,256]{3,2,1,0:T(8,128)S(1)}, f32[16,256]{1,0:T(8,128)S(1)}, f32[8,8,256]{2,1,0:T(8,128)S(1)}) custom-call(s32[32]{0:T(128)S(4)} %get-tuple-element.41.table, f32[8,4,256,256]{3,2,1,0:T(8,128)S(1)} %get-tuple-element.46.w_ref, f32[16,16,256]{2,1,0:T(8,128)S(1)} %all_to_all.31.col_parts), custom_call_target="tpu_custom_call", output_to_operand_aliasing={{0}: (1, {})} | custom-call | tf_op jit(solution)/shard_map/first_row/pallas_call | solution.py:425
  47.4 10.7 %all_to_all.32.row_parts = f32[8,8,256]{2,1,0:T(8,128)S(1)} all-to-all(f32[8,8,256]{2,1,0:T(8,128)S(1)} %get-tuple-element.49), channel_id=1, replica_groups=mesh['z'=8,'x_high'=2,'x_low'=2,'tgt'=8] {'tgt'}, dimensions={0} | all-to-all | bytes 131072 | tf_op jit(solution)/shard_map/all_to_all | solution.py:345
  58.1 1.7 %col_sums.2 = (f32[8,256]{1,0:T(8,128)}, f32[1,16,256]{2,1,0:T(8,128)S(1)}) custom-call(s32[32]{0:T(128)S(4)} %get-tuple-element.41.table, f32[8,4,256,256]{3,2,1,0:T(8,128)S(1)} %get-tuple-element.48.q_ref.tiles, f32[8,8,256]{2,1,0:T(8,128)S(1)} %all_to_all.32.row_parts), custom_call_target="tpu_custom_call" | custom-call | tf_op jit(solution)/shard_map/col_sums/pallas_call | solution.py:438
  59.8 2.5 %collective-permute-start.1 = (f32[1,16,256]{2,1,0:T(8,128)S(1)}, f32[1,16,256]{2,1,0:T(8,128)S(1)}, u32[]{:S(2)}, u32[]{:S(2)}) collective-permute-start(f32[1,16,256]{2,1,0:T(8,128)S(1)} %get-tuple-element.50.own), channel_id=1, source_target_pairs={{0,24},{8,16},{16,8},{24,0},{1,25},{9,17},{17,9},{25,1},{2,26},{10... | collective-permute-start | bytes 49160 | tf_op jit(solution)/shard_map/ppermute | solution.py:367
  62.3 1.3 collective-permute-done.1.other
  63.6 12.3 %all_to_all.33.col_parts = f32[16,16,256]{2,1,0:T(8,128)S(1)} all-to-all(f32[16,16,256]{2,1,0:T(8,128)S(1)} %get-tuple-element.52), channel_id=1, replica_groups=mesh['z'=8,'x_high'=2,'x_low'=2,'tgt'=8] {'z','x_low'}, dimensions={0} | all-to-all | bytes 524288 | tf_op jit(solution)/shard_map/all_to_all | solution.py:345
  75.9 1.7 %row_sums.1 = (f32[16,256]{1,0:T(8,128)}, f32[8,8,256]{2,1,0:T(8,128)S(1)}) custom-call(s32[32]{0:T(128)S(4)} %get-tuple-element.41.table, f32[8,4,256,256]{3,2,1,0:T(8,128)S(1)} %get-tuple-element.51.q_ref.tiles, f32[16,16,256]{2,1,0:T(8,128)S(1)} %all_to_all.33.col_parts), custom_call_target="tpu_custom_call" | custom-call | tf_op jit(solution)/shard_map/row_sums/pallas_call | solution.py:449
  77.6 10.6 %all_to_all.34.row_parts = f32[8,8,256]{2,1,0:T(8,128)S(1)} all-to-all(f32[8,8,256]{2,1,0:T(8,128)S(1)} %get-tuple-element.53), channel_id=1, replica_groups=mesh['z'=8,'x_high'=2,'x_low'=2,'tgt'=8] {'tgt'}, dimensions={0} | all-to-all | bytes 131072 | tf_op jit(solution)/shard_map/all_to_all | solution.py:345
  88.3 1.3 col_sums.3
  89.6 2.0 %collective-permute-start.2 = (f32[1,16,256]{2,1,0:T(8,128)S(1)}, f32[1,16,256]{2,1,0:T(8,128)S(1)}, u32[]{:S(2)}, u32[]{:S(2)}) collective-permute-start(f32[1,16,256]{2,1,0:T(8,128)S(1)} %get-tuple-element.54.own), channel_id=1, source_target_pairs={{0,24},{8,16},{16,8},{24,0},{1,25},{9,17},{17,9},{25,1},{2,26},{10... | collective-permute-start | bytes 49160 | tf_op jit(solution)/shard_map/ppermute | solution.py:367
  91.6 1.9 %collective-permute-done.2.other = f32[1,16,256]{2,1,0:T(8,128)S(1)} collective-permute-done((f32[1,16,256]{2,1,0:T(8,128)S(1)}, f32[1,16,256]{2,1,0:T(8,128)S(1)}, u32[]{:S(2)}, u32[]{:S(2)}) %collective-permute-start.2) | collective-permute-done | bytes 16416 | tf_op jit(solution)/shard_map/ppermute | solution.py:367
  93.5 12.3 %all_to_all.35.col_parts = f32[16,16,256]{2,1,0:T(8,128)S(1)} all-to-all(f32[16,16,256]{2,1,0:T(8,128)S(1)} %get-tuple-element.56), channel_id=1, replica_groups=mesh['z'=8,'x_high'=2,'x_low'=2,'tgt'=8] {'z','x_low'}, dimensions={0} | all-to-all | bytes 524288 | tf_op jit(solution)/shard_map/all_to_all | solution.py:345
  105.8 1.3 far.1
  107.1 3.5 %collective-permute-start.3 = (f32[2,264,384]{2,1,0:T(8,128)S(1)}, f32[2,264,384]{2,1,0:T(8,128)S(1)}, u32[]{:S(2)}, u32[]{:S(2)}) collective-permute-start(f32[2,264,384]{2,1,0:T(8,128)S(1)} %get-tuple-element.59), channel_id=1, source_target_pairs={{0,1},{1,0},{2,3},{3,2},{4,5},{5,4},{6,7},{7,6},{8,9},{9,8},{10,11... | collective-permute-start | bytes 2433032 | tf_op jit(solution)/shard_map/ppermute | solution.py:465
  110.6 1.0 side.3
  111.6 1.0 side.2
  112.6 0.0 collective-permute-done.3.other
  112.6 0.1 far_sum.1
  112.7 0.0 copy-start
  112.7 0.4 collective-permute-start.7
  113.1 0.2 collective-permute-start.4
  113.3 0.2 collective-permute-start.8
  113.6 0.8 collective-permute-start.5
  114.3 1.0 end.1
  115.3 0.9 collective-permute-start.10
  116.3 7.7 %collective-permute-done.8.received = f32[264,384]{1,0:T(8,128)S(1)} collective-permute-done((f32[264,384]{1,0:T(8,128)S(1)}, f32[264,384]{1,0:T(8,128)S(1)}, u32[]{:S(2)}, u32[]{:S(2)}) %collective-permute-start.8) | collective-permute-done | bytes 405536 | tf_op jit(solution)/shard_map/ppermute | solution.py:465
  124.0 0.0 collective-permute-done.7.other
  124.0 0.1 side_sum.3
  124.1 1.0 collective-permute-start.9
  125.1 0.0 collective-permute-done.5.received
  125.2 0.0 collective-permute-done.4.other
  125.2 0.1 side_sum.2
  125.3 0.1 collective-permute-start.6
  125.4 0.0 copy-done
  125.4 0.7 multiply_reduce_fusion
  126.1 0.6 multiply_add_fusion
  126.7 0.6 copy.13
  127.4 0.0 collective-permute-done.10.other
  127.4 16.6 %collective-permute-done.9.second = f32[264,768]{1,0:T(8,128)S(1)} collective-permute-done((f32[264,768]{1,0:T(8,128)S(1)}, f32[264,768]{1,0:T(8,128)S(1)}, u32[]{:S(2)}, u32[]{:S(2)}) %collective-permute-start.9) | collective-permute-done | bytes 811040 | tf_op jit(solution)/shard_map/ppermute | solution.py:465
  143.9 0.0 collective-permute-done.6.first
  143.9 1.2 finish.1
  (6 shorter events, 0.1 us)
Async XLA Ops:
  23.6 3.9 %collective-permute-start = (f32[1,16,256]{2,1,0:T(8,128)S(1)}, f32[1,16,256]{2,1,0:T(8,128)S(1)}, u32[]{:S(2)}, u32[]{:S(2)}) collective-permute-start(f32[1,16,256]{2,1,0:T(8,128)S(1)} %get-tuple-element.44.own), channel_id=1, source_target_pairs={{0,24},{8,16},{16,8},{24,0},{1,25},{9,17},{17,9},{25,1},{2,26},{10... | collective-permute-start | bytes 49160 | tf_op jit(solution)/shard_map/ppermute | solution.py:367
  59.8 3.8 %collective-permute-start.1 = (f32[1,16,256]{2,1,0:T(8,128)S(1)}, f32[1,16,256]{2,1,0:T(8,128)S(1)}, u32[]{:S(2)}, u32[]{:S(2)}) collective-permute-start(f32[1,16,256]{2,1,0:T(8,128)S(1)} %get-tuple-element.50.own), channel_id=1, source_target_pairs={{0,24},{8,16},{16,8},{24,0},{1,25},{9,17},{17,9},{25,1},{2,26},{10... | collective-permute-start | bytes 49160 | tf_op jit(solution)/shard_map/ppermute | solution.py:367
  89.6 3.9 %collective-permute-start.2 = (f32[1,16,256]{2,1,0:T(8,128)S(1)}, f32[1,16,256]{2,1,0:T(8,128)S(1)}, u32[]{:S(2)}, u32[]{:S(2)}) collective-permute-start(f32[1,16,256]{2,1,0:T(8,128)S(1)} %get-tuple-element.54.own), channel_id=1, source_target_pairs={{0,24},{8,16},{16,8},{24,0},{1,25},{9,17},{17,9},{25,1},{2,26},{10... | collective-permute-start | bytes 49160 | tf_op jit(solution)/shard_map/ppermute | solution.py:367
  107.1 5.5 %collective-permute-start.3 = (f32[2,264,384]{2,1,0:T(8,128)S(1)}, f32[2,264,384]{2,1,0:T(8,128)S(1)}, u32[]{:S(2)}, u32[]{:S(2)}) collective-permute-start(f32[2,264,384]{2,1,0:T(8,128)S(1)} %get-tuple-element.59), channel_id=1, source_target_pairs={{0,1},{1,0},{2,3},{3,2},{4,5},{5,4},{6,7},{7,6},{8,9},{9,8},{10,11... | collective-permute-start | bytes 2433032 | tf_op jit(solution)/shard_map/ppermute | solution.py:465
  112.7 12.7 %copy-start = (bf16[2048,768]{1,0:T(8,128)(2,1)S(1)}, bf16[2048,768]{1,0:T(8,128)(2,1)}, u32[]{:S(2)}) copy-start(bf16[2048,768]{1,0:T(8,128)(2,1)} %param.4) | copy-start | bytes 9437188
  112.7 11.3 %collective-permute-start.7 = (f32[264,768]{1,0:T(8,128)S(1)}, f32[264,768]{1,0:T(8,128)S(1)}, u32[]{:S(2)}, u32[]{:S(2)}) collective-permute-start(f32[264,768]{1,0:T(8,128)S(1)} %get-tuple-element.71), channel_id=1, source_target_pairs={{0,1},{1,0},{2,3},{3,2},{4,5},{5,4},{6,7},{7,6},{8,9},{9,8},{10,11... | collective-permute-start | bytes 2433032 | tf_op jit(solution)/shard_map/ppermute | solution.py:465
  113.1 12.1 %collective-permute-start.4 = (f32[264,768]{1,0:T(8,128)S(1)}, f32[264,768]{1,0:T(8,128)S(1)}, u32[]{:S(2)}, u32[]{:S(2)}) collective-permute-start(f32[264,768]{1,0:T(8,128)S(1)} %get-tuple-element.68), channel_id=1, source_target_pairs={{0,1},{1,0},{2,3},{3,2},{4,5},{5,4},{6,7},{7,6},{8,9},{9,8},{10,11... | collective-permute-start | bytes 2433032 | tf_op jit(solution)/shard_map/ppermute | solution.py:465
  113.3 10.7 %collective-permute-start.8 = (f32[264,384]{1,0:T(8,128)S(1)}, f32[264,384]{1,0:T(8,128)S(1)}, u32[]{:S(2)}, u32[]{:S(2)}) collective-permute-start(f32[264,384]{1,0:T(8,128)S(1)} %get-tuple-element.72), channel_id=1, source_target_pairs={{0,2},{1,3},{2,0},{3,1},{4,6},{5,7},{6,4},{7,5},{8,10},{9,11},{10,... | collective-permute-start | bytes 1216520 | tf_op jit(solution)/shard_map/ppermute | solution.py:465
  113.6 11.6 %collective-permute-start.5 = (f32[264,384]{1,0:T(8,128)S(1)}, f32[264,384]{1,0:T(8,128)S(1)}, u32[]{:S(2)}, u32[]{:S(2)}) collective-permute-start(f32[264,384]{1,0:T(8,128)S(1)} %get-tuple-element.69), channel_id=1, source_target_pairs={{0,6},{1,7},{2,4},{3,5},{4,2},{5,3},{6,0},{7,1},{8,14},{9,15},{10,... | collective-permute-start | bytes 1216520 | tf_op jit(solution)/shard_map/ppermute | solution.py:465
  115.3 12.0 %collective-permute-start.10 = (f32[264,768]{1,0:T(8,128)S(1)}, f32[264,768]{1,0:T(8,128)S(1)}, u32[]{:S(2)}, u32[]{:S(2)}) collective-permute-start(f32[264,768]{1,0:T(8,128)S(1)} %get-tuple-element.75), channel_id=1, source_target_pairs={{0,1},{1,0},{2,3},{3,2},{4,5},{5,4},{6,7},{7,6},{8,9},{9,8},{10,11... | collective-permute-start | bytes 2433032 | tf_op jit(solution)/shard_map/ppermute | solution.py:465
  124.1 19.8 %collective-permute-start.9 = (f32[264,768]{1,0:T(8,128)S(1)}, f32[264,768]{1,0:T(8,128)S(1)}, u32[]{:S(2)}, u32[]{:S(2)}) collective-permute-start(f32[264,768]{1,0:T(8,128)S(1)} %side_sum.3), channel_id=1, source_target_pairs={{0,6},{1,7},{2,4},{3,5},{4,2},{5,3},{6,0},{7,1},{8,14},{9,15},{10,... | collective-permute-start | bytes 2433032 | tf_op jit(solution)/shard_map/ppermute | solution.py:465
  125.3 18.6 %collective-permute-start.6 = (f32[264,768]{1,0:T(8,128)S(1)}, f32[264,768]{1,0:T(8,128)S(1)}, u32[]{:S(2)}, u32[]{:S(2)}) collective-permute-start(f32[264,768]{1,0:T(8,128)S(1)} %side_sum.2), channel_id=1, source_target_pairs={{0,2},{1,3},{2,0},{3,1},{4,6},{5,7},{6,4},{7,5},{8,10},{9,11},{10,... | collective-permute-start | bytes 2433032 | tf_op jit(solution)/shard_map/ppermute | solution.py:465

commit v5 on v4

--- a/solution.py
+++ b/solution.py
@@ -191,9 +191,10 @@
     spread(rows, totals, rows.shape[0])
 
 
-def first_col_kernel(table, z_ref, row_parts, w_ref, row_lse, cols, peaks, sums):
-    src_blocks, slots, tgt_blocks = z_ref.shape[0], z_ref.shape[1], peaks.shape[0]
-    row_lse[...] = merge_lse(row_parts[...])
+def first_col_kernel(table, z_ref, row_parts, w_ref, cols, peaks, sums):
+    src_blocks, slots, tgt_blocks = row_parts.shape[1], z_ref.shape[1], peaks.shape[0]
+    row_lse = w_ref.at[src_blocks, 0]
+    row_lse[:src_blocks, :] = merge_lse(row_parts[...])
     peaks[...] = jnp.full(peaks.shape, NEGATIVE, jnp.float32)
     sums[...] = jnp.zeros(sums.shape, jnp.float32)
 
@@ -229,20 +230,22 @@
         totals[b] = jnp.broadcast_to(lane_total(total), (SUB, BLK))
 
 
-def first_row_kernel(table, w_ref, col_parts, q_ref, col_lse, rows, totals):
-    col_lse[...] = merge_lse(col_parts[...])
+def first_row_kernel(table, w_ref, col_parts, q_ref, rows, totals):
+    src_blocks = totals.shape[0]
+    col_lse = q_ref.at[src_blocks, 1]
+    col_lse[: col_parts.shape[1], :] = merge_lse(col_parts[...])
 
     def tile(b, k, t):
         q = jnp.exp2(w_ref[b, k] - col_lse[pl.ds(t, 1), :])
         q_ref[b, k] = q
         return q
 
-    row_totals(table, tile, totals, w_ref.shape[0], w_ref.shape[1])
+    row_totals(table, tile, totals, src_blocks, w_ref.shape[1])
     spread(rows, totals, rows.shape[0])
 
 
 def col_kernel(table, q_ref, row_parts, row_scale, cols, sums, *, share):
-    src_blocks, slots, tgt_blocks = q_ref.shape[0], q_ref.shape[1], sums.shape[0]
+    src_blocks, slots, tgt_blocks = row_scale.shape[0], q_ref.shape[1], sums.shape[0]
     row_scale[...] = share / add_parts(row_parts[...])
     sums[...] = jnp.zeros(sums.shape, jnp.float32)
 
@@ -258,13 +261,17 @@
     spread(cols, sums, cols.shape[0])
 
 
-def row_kernel(table, q_ref, col_parts, col_scale, rows, totals):
+def inner_col_kernel(table, q_ref, row_parts, cols, sums, row_scale, *, share):
+    col_kernel(table, q_ref, row_parts, row_scale, cols, sums, share=share)
+
+
+def row_kernel(table, q_ref, col_parts, rows, totals, col_scale):
     col_scale[...] = 1.0 / add_parts(col_parts[...])
 
     def tile(b, k, t):
         return q_ref[b, k] * col_scale[pl.ds(t, 1), :]
 
-    row_totals(table, tile, totals, q_ref.shape[0], q_ref.shape[1])
+    row_totals(table, tile, totals, totals.shape[0], q_ref.shape[1])
     spread(rows, totals, rows.shape[0])
 
 
@@ -284,26 +291,30 @@
     rows = [(t, w.astype(jnp.bfloat16)) for t, w in weights]
     total = functools.reduce(jnp.add, [fold_lanes(w, jnp.add) for _, w in weights])
     mass = jnp.broadcast_to(lane_total(total), (SUB, BLK))
+    terms = [jnp.dot(w, tgt[t], preferred_element_type=jnp.float32) for t, w in rows]
+    result = functools.reduce(jnp.add, terms)
     for n, out in enumerate(outs):
-        columns = slice(n * width, (n + 1) * width)
-        terms = [
-            jnp.dot(w, tgt[t, :, columns], preferred_element_type=jnp.float32) for t, w in rows
-        ]
-        out[:BLK, :] = functools.reduce(jnp.add, terms)
+        out[:BLK, :] = result[:, n * width : (n + 1) * width]
         out[BLK:, :BLK] = mass
         out[BLK:, BLK:] = jnp.zeros((SUB, width - BLK), jnp.float32)
 
 
 def far_kernel(table, q_ref, col_parts, tgt, col_scale, own, other):
     col_scale[...] = 1.0 / add_parts(col_parts[...])
+    block_kernel(2, table, q_ref, col_scale, tgt, own, other)
+
+
+def block_kernel(flip, table, q_ref, col_scale, tgt, own, other):
     for sibling, out in ((True, other), (False, own)):
         halves = [out.at[0], out.at[1]]
-        project(table, q_ref, col_scale, tgt, block_at(2, sibling), halves, out.shape[2])
-
-
-def block_kernel(flip, table, q_ref, col_scale, tgt, own, other):
-    for sibling, out in ((True, other), (False, own)):
-        project(table, q_ref, col_scale, tgt, block_at(flip, sibling), [out], out.shape[1])
+        project(table, q_ref, col_scale, tgt, block_at(flip, sibling), halves, out.shape[2])
+
+
+def end_kernel(table, q_ref, col_scale, tgt, own, other, row_lse, col_lse):
+    block_kernel(0, table, q_ref, col_scale, tgt, own, other)
+    aux = q_ref.at[row_lse.shape[0]]
+    row_lse[...] = aux[0, : row_lse.shape[0], :]
+    col_lse[...] = aux[1, : col_lse.shape[0], :]
 
 
 def far_sum_kernel(own, other, low, high):
@@ -311,18 +322,35 @@
     high[...] = own[1] + other[1]
 
 
-def side_sum_kernel(way, own, other, received, out):
-    width = received.shape[1]
-    for n in range(2):
-        columns = slice(n * width, (n + 1) * width)
-        total = own[:, columns] + other[:, columns]
-        out[:, columns] = total + received[...] if n == way else total
-
-
-def finish_kernel(first, second, own, other, out):
-    mass = (first[BLK:] + second[BLK:] + own[BLK:] + other[BLK:])[0:1, :BLK]
-    total = first[:BLK] + second[:BLK] + own[:BLK] + other[:BLK]
-    out[...] = total * to_sublanes(1.0 / mass)
+def near_sum_kernel(own_first, other_first, own_second, other_second, low, high):
+    low[...] = own_first[0] + other_first[0]
+    high[...] = own_second[1] + other_second[1]
+
+
+def relay_sum_kernel(way, own, other, received, out):
+    out[...] = own[way] + other[way] + received[...]
+
+
+def near_kernel(low, high, out):
+    out[0] = low[...]
+    out[1] = high[...]
+
+
+def finish_kernel(near, own, other, relay_low, relay_high, out_hbm, out, sems):
+    mass = near[0, BLK:] + own[0, BLK:] + other[0, BLK:] + relay_low[BLK:]
+    scale = to_sublanes(1.0 / mass[0:1, :BLK])
+    width = relay_low.shape[1]
+    rows = BLK // sems.shape[0]
+    copies = []
+    for n in range(sems.shape[0]):
+        part = pl.ds(n * rows, rows)
+        for way, relay in enumerate((relay_low, relay_high)):
+            total = near[way, part] + own[way, part] + other[way, part] + relay[part]
+            out[part, way * width : (way + 1) * width] = total * scale[n * rows : (n + 1) * rows]
+        copies.append(pltpu.make_async_copy(out.at[part], out_hbm.at[part], sems.at[n]))
+        copies[-1].start()
+    for copy in copies:
+        copy.wait()
 
 
 def in_vmem(x):
@@ -379,7 +407,7 @@
     src_blocked = sources.reshape(src_blocks, BLK, features)
     tgt_blocked = targets.reshape(tgt_blocks, BLK, features)
     lists = (block_lists[:, 0, :].T, live_counts.T)
-    tiles = v32(src_blocks, slots, BLK, BLK)
+    tiles = v32(src_blocks + 1, slots, BLK, BLK)
     row_shape, col_shape = v32(src_blocks, BLK), v32(tgt_blocks, BLK)
     row_sends, col_sends = v32(n_tgt, src_blocks, BLK), v32(1, tgt_blocks, BLK)
     row_scratch, col_scratch = v32(src_blocks, SUB, BLK), v32(tgt_blocks, SUB, BLK)
@@ -410,11 +438,11 @@
     )(*[in_hbm(x) for x in (*lists, src_blocked, tgt_blocked)])
     table = pltpu.with_memory_space_constraint(table, pltpu.SMEM)
 
-    w, row_lse, cols = pl.pallas_call(
+    w, cols = pl.pallas_call(
         first_col_kernel,
         in_specs=[SMEM, VMEM, VMEM],
-        out_specs=[VMEM, VMEM, VMEM],
-        out_shape=[tiles, f32(src_blocks, BLK), col_sends],
+        out_specs=[VMEM, VMEM],
+        out_shape=[tiles, col_sends],
         scratch_shapes=[col_scratch, col_scratch],
         input_output_aliases={1: 0},
         compiler_params=PARAMS,
@@ -422,11 +450,11 @@
     )(table, in_vmem(z), exchange(rows, "tgt"))
 
     col_parts, w = exchange_cols(cols, merge_lse, in_vmem(w))
-    q, col_lse, rows = pl.pallas_call(
+    q, rows = pl.pallas_call(
         first_row_kernel,
         in_specs=[SMEM, VMEM, VMEM],
-        out_specs=[VMEM, VMEM, VMEM],
-        out_shape=[tiles, f32(tgt_blocks, BLK), row_sends],
+        out_specs=[VMEM, VMEM],
+        out_shape=[tiles, row_sends],
         scratch_shapes=[row_scratch],
         input_output_aliases={1: 0},
         compiler_params=PARAMS,
@@ -435,42 +463,49 @@
     q = in_vmem(q)
 
     for sweep in range(1, ITERS):
-        row_scale, cols = pl.pallas_call(
-            functools.partial(col_kernel, share=total_tgt / total_src),
+        last = sweep == ITERS - 1
+        *scales, cols = pl.pallas_call(
+            functools.partial(
+                col_kernel if last else inner_col_kernel, share=total_tgt / total_src
+            ),
             in_specs=[SMEM, VMEM, VMEM],
-            out_specs=[VMEM, VMEM],
-            out_shape=[row_shape, col_sends],
-            scratch_shapes=[col_scratch],
+            out_specs=[VMEM] * (1 + last),
+            out_shape=[row_shape] * last + [col_sends],
+            scratch_shapes=[col_scratch] + [row_shape] * (not last),
             compiler_params=PARAMS,
             name="col_sums",
         )(table, q, exchange(rows, "tgt"))
         col_parts, q = exchange_cols(cols, add_parts, q)
-        if sweep < ITERS - 1:
-            col_scale, rows = pl.pallas_call(
+        if not last:
+            rows = pl.pallas_call(
                 row_kernel,
                 in_specs=[SMEM, VMEM, VMEM],
-                out_specs=[VMEM, VMEM],
-                out_shape=[col_shape, row_sends],
-                scratch_shapes=[row_scratch],
+                out_specs=VMEM,
+                out_shape=row_sends,
+                scratch_shapes=[row_scratch, col_shape],
                 compiler_params=PARAMS,
                 name="row_sums",
             )(table, q, col_parts)
+    (row_scale,) = scales
 
     tgt_vmem = in_vmem(tgt_vmem)
-    block = v32(BLK + SUB, features)
     halves = v32(2, BLK + SUB, features // 2)
     half = v32(BLK + SUB, features // 2)
 
+    def send(x, flip):
+        return lax.ppermute(x, "tgt", [(t, t ^ flip) for t in range(n_tgt)])
+
     def swap(x, flip=1):
-        return in_vmem(lax.ppermute(x, "tgt", [(t, t ^ flip) for t in range(n_tgt)]))
-
-    def call(kernel, name, operands, out_shape, spec=VMEM):
+        return in_vmem(send(x, flip))
+
+    def call(kernel, name, operands, out_shape, spec=VMEM, cost=None):
         return pl.pallas_call(
             kernel,
             in_specs=[spec] + [VMEM] * (len(operands) - 1),
             out_specs=[VMEM] * len(out_shape),
             out_shape=out_shape,
             compiler_params=PARAMS,
+            cost_estimate=cost,
             name=name,
         )(*operands)
 
@@ -484,7 +519,7 @@
                 functools.partial(block_kernel, flip),
                 "side",
                 [table, q, in_vmem(col_scale), tgt_vmem],
-                [block, block],
+                [halves, halves],
                 SMEM,
             )
         )
@@ -493,30 +528,48 @@
     )
     (low, high), sides, col_scale = lax.optimization_barrier(((low, high), sides, col_scale))
     low, high = swap(low, 2), swap(high, 6)
-    own_end, other_end = call(
-        functools.partial(block_kernel, 0),
+    own_end, other_end, row_lse, col_lse = call(
+        end_kernel,
         "end",
         [table, q, in_vmem(col_scale), tgt_vmem],
-        [block, block],
+        [halves, halves, f32(src_blocks, BLK), f32(tgt_blocks, BLK)],
         SMEM,
     )
-    first, second = [
-        call(
-            functools.partial(side_sum_kernel, way),
-            "side_sum",
-            [in_vmem(own), swap(other), received],
-            [block],
-        )[0]
-        for way, (own, other), received in ((1, sides[0], high), (0, sides[1], low))
-    ]
-    mapped = call(
+    sides = [(own, swap(other)) for own, other in sides]
+    (own_first, other_first), (own_second, other_second) = sides
+    near_low, near_high = call(
+        near_sum_kernel,
+        "near_sum",
+        [in_vmem(own_first), other_first, in_vmem(own_second), other_second],
+        [half, half],
+    )
+    near = call(
+        near_kernel,
+        "near",
+        [swap(near_low, 2), swap(near_high, 6)],
+        [halves],
+        cost=pl.CostEstimate(flops=3 * 10**9, bytes_accessed=0, transcendentals=0),
+    )[0]
+
+    def relay(way, own, other, received, flip):
+        kernel = functools.partial(relay_sum_kernel, way)
+        total = call(kernel, "relay_sum", [in_vmem(own), other, received], [half])[0]
+        return swap(total, flip)
+
+    relay_high = relay(1, own_first, other_first, high, 2)
+    relay_low = relay(0, own_second, other_second, low, 6)
+    mapped = pl.pallas_call(
         finish_kernel,
-        "finish",
-        [swap(first, 2), swap(second, 6), in_vmem(own_end), swap(other_end)],
-        [f32(BLK, features)],
-    )[0]
-
-    src_square = jnp.sum(jnp.square(sources.astype(jnp.float32)), -1)
+        in_specs=[VMEM] * 5,
+        out_specs=HBM,
+        out_shape=f32(BLK, features),
+        scratch_shapes=[v32(BLK, features), pltpu.SemaphoreType.DMA((4,))],
+        compiler_params=PARAMS,
+        name="finish",
+    )(in_vmem(near), in_vmem(own_end), swap(other_end), relay_low, relay_high)
+
+    late_sources, _ = lax.optimization_barrier((sources, near))
+    src_square = jnp.sum(jnp.square(late_sources.astype(jnp.float32)), -1)
     row_potential = (
         EPSILON * (jnp.log(row_scale) - LN2 * row_lse - math.log(total_src))
     ).reshape(src_rows) + src_square / features

time: 146 us -> 144 us (0.986)
  waiting for transfers between devices: 28.9 us -> 26.4 us
  starting transfers between devices: 14.1 us -> 16.5 us
  Pallas kernels: 25.3 us -> 23.8 us
    ppermute x8 -> x10, waiting for transfers between devices: 24.3 us -> 21.5 us  [send(): return lax.ppermute(x, 'tgt', [(t, t ^ flip) for t in range(n_tgt)])]
    ppermute x8 -> x10, starting transfers between devices: 7.12 us -> 9.79 us  [send(): return lax.ppermute(x, 'tgt', [(t, t ^ flip) for t in range(n_tgt)])]
    pallas_call x8 -> x9, Pallas kernels: 5.84 us -> 4.45 us  [call(): pl.pallas_call(kernel, in_specs=[spec] + [VMEM] * (len(operands) - 1), ou...]
    pallas_call x3 -> x4, Pallas kernels: 4.78 us -> 4.98 us  [the longest x2 2.63 us: local(): pl.pallas_call(functools.partial(col_kernel if last else inner_col_kernel...]
  transfers between devices with their start and end apart: 11 -> 13, of which waited for: 5 -> 9; matrix products, arithmetic and copies ran while one was open for 1% -> 1% of each run, Pallas kernels for 2% -> 2%
where the time goes in v5:
time: 144 us
  blocking collectives  74.3 us (52%)
  waiting for transfers between devices  26.4 us (18%)
  Pallas kernels  23.8 us (17%)
  starting transfers between devices  16.5 us (11%)
    all_to_all x6, blocking collectives, exchange(): return in_vmem(lax.all_to_all(copies, axis, 0, 0))  74.3 us
    ppermute x10, waiting for transfers between devices, send(): return lax.ppermute(x, 'tgt', [(t, t ^ flip) for t in range(n_tgt)])  21.5 us
    ppermute x10, starting transfers between devices, send(): return lax.ppermute(x, 'tgt', [(t, t ^ flip) for t in range(n_tgt)])  9.79 us
    pallas_call x1, Pallas kernels, local(): pl.pallas_call(functools.partial(cost_kernel, features=features), in_spec...  9.12 us
    ppermute x3, starting transfers between devices, exchange_cols(): lax.ppermute(in_vmem(cols), X_AXES, pairs)  6.75 us
    ppermute x3, waiting for transfers between devices, exchange_cols(): lax.ppermute(in_vmem(cols), X_AXES, pairs)  4.91 us
    pallas_call x9, Pallas kernels, call(): pl.pallas_call(kernel, in_specs=[spec] + [VMEM] * (len(operands) - 1), ou...  4.45 us
    pallas_call x1, Pallas kernels, local(): pl.pallas_call(first_col_kernel, in_specs=[SMEM, VMEM, VMEM], out_specs=[...  3.07 us
  transfers between devices with their start and end apart: 13, of which 9 were waited for; matrix products, arithmetic and copies ran while one was open for 1% of the time, Pallas kernels for 2%

profile of v5, /device:TPU:1, one launch (start us, length us, event | category | flops | bytes accessed | tf_op | source)
XLA Modules:
  0.0 144.0 jit_solution(13721102517524376968)
XLA Ops:
  0.6 9.1 %cost.1 = (bf16[16,256,768]{2,1,0:T(8,128)(2,1)S(1)}, f32[9,4,256,256]{3,2,1,0:T(8,128)S(1)}, f32[8,8,256]{2,1,0:T(8,128)S(1)}, s32[32]{0:T(128)S(4)}) custom-call(s32[4,8]{1,0:T(4,128)} %bitcast.16, s32[1,8]{1,0:T(1,128)} %bitcast.17, bf16[8,256,768]{2,1,0:T(8,128)(2,1)} %bitcast.12, bf16[16,256,768]{2,1,0:T(8,128)(2,1)} %bitcast.13), custom_call_target="tpu_custom_call" | custom-call | tf_op jit(solution)/shard_map/cost/pallas_call | solution.py:415
  9.8 10.7 %all_to_all.30.row_parts = f32[8,8,256]{2,1,0:T(8,128)S(1)} all-to-all(f32[8,8,256]{2,1,0:T(8,128)S(1)} %get-tuple-element.44), channel_id=1, replica_groups=mesh['z'=8,'x_high'=2,'x_low'=2,'tgt'=8] {'tgt'}, dimensions={0} | all-to-all | bytes 131072 | tf_op jit(solution)/shard_map/all_to_all | solution.py:373
  20.5 3.1 %first_col.1 = (f32[9,4,256,256]{3,2,1,0:T(8,128)S(1)}, f32[1,16,256]{2,1,0:T(8,128)S(1)}) custom-call(s32[32]{0:T(128)S(4)} %get-tuple-element.42.table, f32[9,4,256,256]{3,2,1,0:T(8,128)S(1)} %get-tuple-element.43.z_ref, f32[8,8,256]{2,1,0:T(8,128)S(1)} %all_to_all.30.row_parts), custom_call_target="tpu_custom_call", output_to_operand_aliasing={{0}: (1, {})} | custom-call | tf_op jit(solution)/shard_map/first_col/pallas_call | solution.py:441
  23.6 2.5 %collective-permute-start = (f32[1,16,256]{2,1,0:T(8,128)S(1)}, f32[1,16,256]{2,1,0:T(8,128)S(1)}, u32[]{:S(2)}, u32[]{:S(2)}) collective-permute-start(f32[1,16,256]{2,1,0:T(8,128)S(1)} %get-tuple-element.45.own), channel_id=1, source_target_pairs={{0,24},{8,16},{16,8},{24,0},{1,25},{9,17},{17,9},{25,1},{2,26},{10... | collective-permute-start | bytes 49160 | tf_op jit(solution)/shard_map/ppermute | solution.py:395
  26.0 1.4 collective-permute-done.other
  27.5 17.6 %all_to_all.31.col_parts = f32[16,16,256]{2,1,0:T(8,128)S(1)} all-to-all(f32[16,16,256]{2,1,0:T(8,128)S(1)} %get-tuple-element.48), channel_id=1, replica_groups=mesh['z'=8,'x_high'=2,'x_low'=2,'tgt'=8] {'z','x_low'}, dimensions={0} | all-to-all | bytes 524288 | tf_op jit(solution)/shard_map/all_to_all | solution.py:373
  45.1 2.1 %first_row.1 = (f32[9,4,256,256]{3,2,1,0:T(8,128)S(1)}, f32[8,8,256]{2,1,0:T(8,128)S(1)}) custom-call(s32[32]{0:T(128)S(4)} %get-tuple-element.42.table, f32[9,4,256,256]{3,2,1,0:T(8,128)S(1)} %get-tuple-element.47.w_ref, f32[16,16,256]{2,1,0:T(8,128)S(1)} %all_to_all.31.col_parts), custom_call_target="tpu_custom_call", output_to_operand_aliasing={{0}: (1, {})} | custom-call | tf_op jit(solution)/shard_map/first_row/pallas_call | solution.py:453
  47.2 10.7 %all_to_all.32.row_parts = f32[8,8,256]{2,1,0:T(8,128)S(1)} all-to-all(f32[8,8,256]{2,1,0:T(8,128)S(1)} %get-tuple-element.50), channel_id=1, replica_groups=mesh['z'=8,'x_high'=2,'x_low'=2,'tgt'=8] {'tgt'}, dimensions={0} | all-to-all | bytes 131072 | tf_op jit(solution)/shard_map/all_to_all | solution.py:373
  58.0 1.3 col_sums.2.own
  59.3 2.4 %collective-permute-start.1 = (f32[1,16,256]{2,1,0:T(8,128)S(1)}, f32[1,16,256]{2,1,0:T(8,128)S(1)}, u32[]{:S(2)}, u32[]{:S(2)}) collective-permute-start(f32[1,16,256]{2,1,0:T(8,128)S(1)} %col_sums.2.own), channel_id=1, source_target_pairs={{0,24},{8,16},{16,8},{24,0},{1,25},{9,17},{17,9},{25,1},{2,26},{10... | collective-permute-start | bytes 49160 | tf_op jit(solution)/shard_map/ppermute | solution.py:395
  61.7 1.4 %collective-permute-done.1.other = f32[1,16,256]{2,1,0:T(8,128)S(1)} collective-permute-done((f32[1,16,256]{2,1,0:T(8,128)S(1)}, f32[1,16,256]{2,1,0:T(8,128)S(1)}, u32[]{:S(2)}, u32[]{:S(2)}) %collective-permute-start.1) | collective-permute-done | bytes 16416 | tf_op jit(solution)/shard_map/ppermute | solution.py:395
  63.2 12.3 %all_to_all.33.col_parts = f32[16,16,256]{2,1,0:T(8,128)S(1)} all-to-all(f32[16,16,256]{2,1,0:T(8,128)S(1)} %get-tuple-element.52), channel_id=1, replica_groups=mesh['z'=8,'x_high'=2,'x_low'=2,'tgt'=8] {'z','x_low'}, dimensions={0} | all-to-all | bytes 524288 | tf_op jit(solution)/shard_map/all_to_all | solution.py:373
  75.5 1.2 row_sums.1
  76.7 10.6 %all_to_all.34.row_parts = f32[8,8,256]{2,1,0:T(8,128)S(1)} all-to-all(f32[8,8,256]{2,1,0:T(8,128)S(1)} %row_sums.1), channel_id=1, replica_groups=mesh['z'=8,'x_high'=2,'x_low'=2,'tgt'=8] {'tgt'}, dimensions={0} | all-to-all | bytes 131072 | tf_op jit(solution)/shard_map/all_to_all | solution.py:373
  87.3 1.3 col_sums.3
  88.7 1.9 %collective-permute-start.2 = (f32[1,16,256]{2,1,0:T(8,128)S(1)}, f32[1,16,256]{2,1,0:T(8,128)S(1)}, u32[]{:S(2)}, u32[]{:S(2)}) collective-permute-start(f32[1,16,256]{2,1,0:T(8,128)S(1)} %get-tuple-element.53.own), channel_id=1, source_target_pairs={{0,24},{8,16},{16,8},{24,0},{1,25},{9,17},{17,9},{25,1},{2,26},{10... | collective-permute-start | bytes 49160 | tf_op jit(solution)/shard_map/ppermute | solution.py:395
  90.5 2.0 %collective-permute-done.2.other = f32[1,16,256]{2,1,0:T(8,128)S(1)} collective-permute-done((f32[1,16,256]{2,1,0:T(8,128)S(1)}, f32[1,16,256]{2,1,0:T(8,128)S(1)}, u32[]{:S(2)}, u32[]{:S(2)}) %collective-permute-start.2) | collective-permute-done | bytes 16416 | tf_op jit(solution)/shard_map/ppermute | solution.py:395
  92.6 12.3 %all_to_all.35.col_parts = f32[16,16,256]{2,1,0:T(8,128)S(1)} all-to-all(f32[16,16,256]{2,1,0:T(8,128)S(1)} %get-tuple-element.55), channel_id=1, replica_groups=mesh['z'=8,'x_high'=2,'x_low'=2,'tgt'=8] {'z','x_low'}, dimensions={0} | all-to-all | bytes 524288 | tf_op jit(solution)/shard_map/all_to_all | solution.py:373
  104.8 1.0 far.1
  105.9 3.5 %collective-permute-start.3 = (f32[2,264,384]{2,1,0:T(8,128)S(1)}, f32[2,264,384]{2,1,0:T(8,128)S(1)}, u32[]{:S(2)}, u32[]{:S(2)}) collective-permute-start(f32[2,264,384]{2,1,0:T(8,128)S(1)} %get-tuple-element.58), channel_id=1, source_target_pairs={{0,1},{1,0},{2,3},{3,2},{4,5},{5,4},{6,7},{7,6},{8,9},{9,8},{10,11... | collective-permute-start | bytes 2433032 | tf_op jit(solution)/shard_map/ppermute | solution.py:496
  109.4 1.0 side.3
  110.4 1.0 side.2
  111.4 0.1 far_sum.1
  111.5 0.4 collective-permute-start.4
  111.9 0.2 collective-permute-start.5
  112.1 1.0 end.1
  113.1 0.0 copy-start
  113.1 0.6 collective-permute-start.9
  113.7 0.7 collective-permute-start.11
  114.4 0.7 collective-permute-done.5.other_second.other
  115.1 0.1 near_sum.1
  115.2 0.4 collective-permute-start.6
  115.6 1.6 %collective-permute-start.7 = (f32[264,384]{1,0:T(8,128)S(1)}, f32[264,384]{1,0:T(8,128)S(1)}, u32[]{:S(2)}, u32[]{:S(2)}) collective-permute-start(f32[264,384]{1,0:T(8,128)S(1)} %get-tuple-element.71), channel_id=1, source_target_pairs={{0,6},{1,7},{2,4},{3,5},{4,2},{5,3},{6,0},{7,1},{8,14},{9,15},{10,... | collective-permute-start | bytes 1216520 | tf_op jit(solution)/shard_map/ppermute | solution.py:496
  117.2 0.6 copy.13
  117.8 1.4 collective-permute-start.8
  119.2 6.1 %collective-permute-done.11.received = f32[264,384]{1,0:T(8,128)S(1)} collective-permute-done((f32[264,384]{1,0:T(8,128)S(1)}, f32[264,384]{1,0:T(8,128)S(1)}, u32[]{:S(2)}, u32[]{:S(2)}) %collective-permute-start.11) | collective-permute-done | bytes 405536 | tf_op jit(solution)/shard_map/ppermute | solution.py:496
  125.3 0.1 relay_sum.3
  125.4 0.1 collective-permute-start.12
  125.5 0.1 relay_sum.2
  125.6 0.9 collective-permute-start.10
  126.5 6.3 %collective-permute-done.6.low = f32[264,384]{1,0:T(8,128)S(1)} collective-permute-done((f32[264,384]{1,0:T(8,128)S(1)}, f32[264,384]{1,0:T(8,128)S(1)}, u32[]{:S(2)}, u32[]{:S(2)}) %collective-permute-start.6) | collective-permute-done | bytes 405536 | tf_op jit(solution)/shard_map/ppermute | solution.py:496
  132.8 1.2 collective-permute-done.7.high
  134.0 0.1 near.1
  134.0 0.7 multiply_reduce_fusion
  134.7 0.6 multiply_add_fusion
  135.3 6.1 %collective-permute-done.12.relay_high = f32[264,384]{1,0:T(8,128)S(1)} collective-permute-done((f32[264,384]{1,0:T(8,128)S(1)}, f32[264,384]{1,0:T(8,128)S(1)}, u32[]{:S(2)}, u32[]{:S(2)}) %collective-permute-start.12) | collective-permute-done | bytes 405536 | tf_op jit(solution)/shard_map/ppermute | solution.py:496
  141.5 1.2 collective-permute-done.10.relay_low
  142.7 1.1 finish.1
  (11 shorter events, 0.1 us)
Async XLA Ops:
  23.6 3.9 %collective-permute-start = (f32[1,16,256]{2,1,0:T(8,128)S(1)}, f32[1,16,256]{2,1,0:T(8,128)S(1)}, u32[]{:S(2)}, u32[]{:S(2)}) collective-permute-start(f32[1,16,256]{2,1,0:T(8,128)S(1)} %get-tuple-element.45.own), channel_id=1, source_target_pairs={{0,24},{8,16},{16,8},{24,0},{1,25},{9,17},{17,9},{25,1},{2,26},{10... | collective-permute-start | bytes 49160 | tf_op jit(solution)/shard_map/ppermute | solution.py:395
  59.3 3.9 %collective-permute-start.1 = (f32[1,16,256]{2,1,0:T(8,128)S(1)}, f32[1,16,256]{2,1,0:T(8,128)S(1)}, u32[]{:S(2)}, u32[]{:S(2)}) collective-permute-start(f32[1,16,256]{2,1,0:T(8,128)S(1)} %col_sums.2.own), channel_id=1, source_target_pairs={{0,24},{8,16},{16,8},{24,0},{1,25},{9,17},{17,9},{25,1},{2,26},{10... | collective-permute-start | bytes 49160 | tf_op jit(solution)/shard_map/ppermute | solution.py:395
  88.7 3.9 %collective-permute-start.2 = (f32[1,16,256]{2,1,0:T(8,128)S(1)}, f32[1,16,256]{2,1,0:T(8,128)S(1)}, u32[]{:S(2)}, u32[]{:S(2)}) collective-permute-start(f32[1,16,256]{2,1,0:T(8,128)S(1)} %get-tuple-element.53.own), channel_id=1, source_target_pairs={{0,24},{8,16},{16,8},{24,0},{1,25},{9,17},{17,9},{25,1},{2,26},{10... | collective-permute-start | bytes 49160 | tf_op jit(solution)/shard_map/ppermute | solution.py:395
  105.9 5.5 %collective-permute-start.3 = (f32[2,264,384]{2,1,0:T(8,128)S(1)}, f32[2,264,384]{2,1,0:T(8,128)S(1)}, u32[]{:S(2)}, u32[]{:S(2)}) collective-permute-start(f32[2,264,384]{2,1,0:T(8,128)S(1)} %get-tuple-element.58), channel_id=1, source_target_pairs={{0,1},{1,0},{2,3},{3,2},{4,5},{5,4},{6,7},{7,6},{8,9},{9,8},{10,11... | collective-permute-start | bytes 2433032 | tf_op jit(solution)/shard_map/ppermute | solution.py:496
  111.5 2.9 %collective-permute-start.4 = (f32[2,264,384]{2,1,0:T(8,128)S(1)}, f32[2,264,384]{2,1,0:T(8,128)S(1)}, u32[]{:S(2)}, u32[]{:S(2)}) collective-permute-start(f32[2,264,384]{2,1,0:T(8,128)S(1)} %get-tuple-element.67), channel_id=1, source_target_pairs={{0,1},{1,0},{2,3},{3,2},{4,5},{5,4},{6,7},{7,6},{8,9},{9,8},{10,11... | collective-permute-start | bytes 2433032 | tf_op jit(solution)/shard_map/ppermute | solution.py:496
  111.9 3.2 %collective-permute-start.5 = (f32[2,264,384]{2,1,0:T(8,128)S(1)}, f32[2,264,384]{2,1,0:T(8,128)S(1)}, u32[]{:S(2)}, u32[]{:S(2)}) collective-permute-start(f32[2,264,384]{2,1,0:T(8,128)S(1)} %get-tuple-element.69), channel_id=1, source_target_pairs={{0,1},{1,0},{2,3},{3,2},{4,5},{5,4},{6,7},{7,6},{8,9},{9,8},{10,11... | collective-permute-start | bytes 2433032 | tf_op jit(solution)/shard_map/ppermute | solution.py:496
  113.1 20.9 %copy-start = (bf16[2048,768]{1,0:T(8,128)(2,1)S(1)}, bf16[2048,768]{1,0:T(8,128)(2,1)}, u32[]{:S(2)}) copy-start(bf16[2048,768]{1,0:T(8,128)(2,1)} %param.4) | copy-start | bytes 9437188
  113.1 12.3 %collective-permute-start.9 = (f32[264,384]{1,0:T(8,128)S(1)}, f32[264,384]{1,0:T(8,128)S(1)}, u32[]{:S(2)}, u32[]{:S(2)}) collective-permute-start(f32[264,384]{1,0:T(8,128)S(1)} %get-tuple-element.75), channel_id=1, source_target_pairs={{0,2},{1,3},{2,0},{3,1},{4,6},{5,7},{6,4},{7,5},{8,10},{9,11},{10,... | collective-permute-start | bytes 1216520 | tf_op jit(solution)/shard_map/ppermute | solution.py:496
  113.7 11.6 %collective-permute-start.11 = (f32[264,384]{1,0:T(8,128)S(1)}, f32[264,384]{1,0:T(8,128)S(1)}, u32[]{:S(2)}, u32[]{:S(2)}) collective-permute-start(f32[264,384]{1,0:T(8,128)S(1)} %get-tuple-element.76), channel_id=1, source_target_pairs={{0,6},{1,7},{2,4},{3,5},{4,2},{5,3},{6,0},{7,1},{8,14},{9,15},{10,... | collective-permute-start | bytes 1216520 | tf_op jit(solution)/shard_map/ppermute | solution.py:496
  115.2 17.6 %collective-permute-start.6 = (f32[264,384]{1,0:T(8,128)S(1)}, f32[264,384]{1,0:T(8,128)S(1)}, u32[]{:S(2)}, u32[]{:S(2)}) collective-permute-start(f32[264,384]{1,0:T(8,128)S(1)} %get-tuple-element.70), channel_id=1, source_target_pairs={{0,2},{1,3},{2,0},{3,1},{4,6},{5,7},{6,4},{7,5},{8,10},{9,11},{10,... | collective-permute-start | bytes 1216520 | tf_op jit(solution)/shard_map/ppermute | solution.py:496
  115.6 18.4 %collective-permute-start.7 = (f32[264,384]{1,0:T(8,128)S(1)}, f32[264,384]{1,0:T(8,128)S(1)}, u32[]{:S(2)}, u32[]{:S(2)}) collective-permute-start(f32[264,384]{1,0:T(8,128)S(1)} %get-tuple-element.71), channel_id=1, source_target_pairs={{0,6},{1,7},{2,4},{3,5},{4,2},{5,3},{6,0},{7,1},{8,14},{9,15},{10,... | collective-permute-start | bytes 1216520 | tf_op jit(solution)/shard_map/ppermute | solution.py:496
  117.8 17.5 %collective-permute-start.8 = (f32[2,264,384]{2,1,0:T(8,128)S(1)}, f32[2,264,384]{2,1,0:T(8,128)S(1)}, u32[]{:S(2)}, u32[]{:S(2)}) collective-permute-start(f32[2,264,384]{2,1,0:T(8,128)S(1)} %get-tuple-element.74), channel_id=1, source_target_pairs={{0,1},{1,0},{2,3},{3,2},{4,5},{5,4},{6,7},{7,6},{8,9},{9,8},{10,11... | collective-permute-start | bytes 2433032 | tf_op jit(solution)/shard_map/ppermute | solution.py:496
  125.4 16.1 %collective-permute-start.12 = (f32[264,384]{1,0:T(8,128)S(1)}, f32[264,384]{1,0:T(8,128)S(1)}, u32[]{:S(2)}, u32[]{:S(2)}) collective-permute-start(f32[264,384]{1,0:T(8,128)S(1)} %relay_sum.3), channel_id=1, source_target_pairs={{0,2},{1,3},{2,0},{3,1},{4,6},{5,7},{6,4},{7,5},{8,10},{9,11},{10,... | collective-permute-start | bytes 1216520 | tf_op jit(solution)/shard_map/ppermute | solution.py:496
  125.6 17.1 %collective-permute-start.10 = (f32[264,384]{1,0:T(8,128)S(1)}, f32[264,384]{1,0:T(8,128)S(1)}, u32[]{:S(2)}, u32[]{:S(2)}) collective-permute-start(f32[264,384]{1,0:T(8,128)S(1)} %relay_sum.2), channel_id=1, source_target_pairs={{0,6},{1,7},{2,4},{3,5},{4,2},{5,3},{6,0},{7,1},{8,14},{9,15},{10,... | collective-permute-start | bytes 1216520 | tf_op jit(solution)/shard_map/ppermute | solution.py:496

commit v6 on v5

--- a/solution.py
+++ b/solution.py
@@ -568,7 +568,8 @@
         name="finish",
     )(in_vmem(near), in_vmem(own_end), swap(other_end), relay_low, relay_high)
 
-    late_sources, _ = lax.optimization_barrier((sources, near))
+    late = (sources, row_lse, col_lse, near)
+    late_sources, row_lse, col_lse, _ = lax.optimization_barrier(late)
     src_square = jnp.sum(jnp.square(late_sources.astype(jnp.float32)), -1)
     row_potential = (
         EPSILON * (jnp.log(row_scale) - LN2 * row_lse - math.log(total_src))

time: 144 us -> 143 us (level)
    ppermute x10, starting transfers between devices: 9.79 us -> 8.18 us  [send(): return lax.ppermute(x, 'tgt', [(t, t ^ flip) for t in range(n_tgt)])]
  transfers between devices with their start and end apart: 13 -> 13, of which waited for: 9 -> 10; matrix products, arithmetic and copies ran while one was open for 1% -> 1% of each run, Pallas kernels for 2% -> 2%
where the time goes in v6:
time: 143 us
  blocking collectives  74.3 us (52%)
  waiting for transfers between devices  26.5 us (19%)
  Pallas kernels  23.9 us (17%)
  starting transfers between devices  15.1 us (11%)
    all_to_all x6, blocking collectives, exchange(): return in_vmem(lax.all_to_all(copies, axis, 0, 0))  74.3 us
    ppermute x10, waiting for transfers between devices, send(): return lax.ppermute(x, 'tgt', [(t, t ^ flip) for t in range(n_tgt)])  21.8 us
    pallas_call x1, Pallas kernels, local(): pl.pallas_call(functools.partial(cost_kernel, features=features), in_spec...  9.12 us
    ppermute x10, starting transfers between devices, send(): return lax.ppermute(x, 'tgt', [(t, t ^ flip) for t in range(n_tgt)])  8.18 us
    ppermute x3, starting transfers between devices, exchange_cols(): lax.ppermute(in_vmem(cols), X_AXES, pairs)  6.92 us
    ppermute x3, waiting for transfers between devices, exchange_cols(): lax.ppermute(in_vmem(cols), X_AXES, pairs)  4.74 us
    pallas_call x9, Pallas kernels, call(): pl.pallas_call(kernel, in_specs=[spec] + [VMEM] * (len(operands) - 1), ou...  4.47 us
    pallas_call x1, Pallas kernels, local(): pl.pallas_call(first_col_kernel, in_specs=[SMEM, VMEM, VMEM], out_specs=[...  3.07 us
  transfers between devices with their start and end apart: 13, of which 10 were waited for; matrix products, arithmetic and copies ran while one was open for 1% of the time, Pallas kernels for 2%

profile of v6, /device:TPU:1, one launch (start us, length us, event | category | flops | bytes accessed | tf_op | source)
XLA Modules:
  0.0 142.8 jit_solution(13449600822565184800)
XLA Ops:
  0.6 9.1 %cost.1 = (bf16[16,256,768]{2,1,0:T(8,128)(2,1)S(1)}, f32[9,4,256,256]{3,2,1,0:T(8,128)S(1)}, f32[8,8,256]{2,1,0:T(8,128)S(1)}, s32[32]{0:T(128)S(4)}) custom-call(s32[4,8]{1,0:T(4,128)} %bitcast.16, s32[1,8]{1,0:T(1,128)} %bitcast.17, bf16[8,256,768]{2,1,0:T(8,128)(2,1)} %bitcast.12, bf16[16,256,768]{2,1,0:T(8,128)(2,1)} %bitcast.13), custom_call_target="tpu_custom_call" | custom-call | tf_op jit(solution)/shard_map/cost/pallas_call | solution.py:415
  9.8 10.9 %all_to_all.30.row_parts = f32[8,8,256]{2,1,0:T(8,128)S(1)} all-to-all(f32[8,8,256]{2,1,0:T(8,128)S(1)} %get-tuple-element.46), channel_id=1, replica_groups=mesh['z'=8,'x_high'=2,'x_low'=2,'tgt'=8] {'tgt'}, dimensions={0} | all-to-all | bytes 131072 | tf_op jit(solution)/shard_map/all_to_all | solution.py:373
  20.7 3.1 %first_col.1 = (f32[9,4,256,256]{3,2,1,0:T(8,128)S(1)}, f32[1,16,256]{2,1,0:T(8,128)S(1)}) custom-call(s32[32]{0:T(128)S(4)} %get-tuple-element.44.table, f32[9,4,256,256]{3,2,1,0:T(8,128)S(1)} %get-tuple-element.45.z_ref, f32[8,8,256]{2,1,0:T(8,128)S(1)} %all_to_all.30.row_parts), custom_call_target="tpu_custom_call", output_to_operand_aliasing={{0}: (1, {})} | custom-call | tf_op jit(solution)/shard_map/first_col/pallas_call | solution.py:441
  23.7 2.6 %collective-permute-start = (f32[1,16,256]{2,1,0:T(8,128)S(1)}, f32[1,16,256]{2,1,0:T(8,128)S(1)}, u32[]{:S(2)}, u32[]{:S(2)}) collective-permute-start(f32[1,16,256]{2,1,0:T(8,128)S(1)} %get-tuple-element.47.own), channel_id=1, source_target_pairs={{0,24},{8,16},{16,8},{24,0},{1,25},{9,17},{17,9},{25,1},{2,26},{10... | collective-permute-start | bytes 49160 | tf_op jit(solution)/shard_map/ppermute | solution.py:395
  26.3 1.3 collective-permute-done.other
  27.6 17.5 %all_to_all.31.col_parts = f32[16,16,256]{2,1,0:T(8,128)S(1)} all-to-all(f32[16,16,256]{2,1,0:T(8,128)S(1)} %get-tuple-element.50), channel_id=1, replica_groups=mesh['z'=8,'x_high'=2,'x_low'=2,'tgt'=8] {'z','x_low'}, dimensions={0} | all-to-all | bytes 524288 | tf_op jit(solution)/shard_map/all_to_all | solution.py:373
  45.1 2.1 %first_row.1 = (f32[9,4,256,256]{3,2,1,0:T(8,128)S(1)}, f32[8,8,256]{2,1,0:T(8,128)S(1)}) custom-call(s32[32]{0:T(128)S(4)} %get-tuple-element.44.table, f32[9,4,256,256]{3,2,1,0:T(8,128)S(1)} %get-tuple-element.49.w_ref, f32[16,16,256]{2,1,0:T(8,128)S(1)} %all_to_all.31.col_parts), custom_call_target="tpu_custom_call", output_to_operand_aliasing={{0}: (1, {})} | custom-call | tf_op jit(solution)/shard_map/first_row/pallas_call | solution.py:453
  47.3 10.8 %all_to_all.32.row_parts = f32[8,8,256]{2,1,0:T(8,128)S(1)} all-to-all(f32[8,8,256]{2,1,0:T(8,128)S(1)} %get-tuple-element.52), channel_id=1, replica_groups=mesh['z'=8,'x_high'=2,'x_low'=2,'tgt'=8] {'tgt'}, dimensions={0} | all-to-all | bytes 131072 | tf_op jit(solution)/shard_map/all_to_all | solution.py:373
  58.0 1.3 col_sums.2.own
  59.4 2.5 %collective-permute-start.1 = (f32[1,16,256]{2,1,0:T(8,128)S(1)}, f32[1,16,256]{2,1,0:T(8,128)S(1)}, u32[]{:S(2)}, u32[]{:S(2)}) collective-permute-start(f32[1,16,256]{2,1,0:T(8,128)S(1)} %col_sums.2.own), channel_id=1, source_target_pairs={{0,24},{8,16},{16,8},{24,0},{1,25},{9,17},{17,9},{25,1},{2,26},{10... | collective-permute-start | bytes 49160 | tf_op jit(solution)/shard_map/ppermute | solution.py:395
  61.8 1.4 collective-permute-done.1.other
  63.3 12.3 %all_to_all.33.col_parts = f32[16,16,256]{2,1,0:T(8,128)S(1)} all-to-all(f32[16,16,256]{2,1,0:T(8,128)S(1)} %get-tuple-element.54), channel_id=1, replica_groups=mesh['z'=8,'x_high'=2,'x_low'=2,'tgt'=8] {'z','x_low'}, dimensions={0} | all-to-all | bytes 524288 | tf_op jit(solution)/shard_map/all_to_all | solution.py:373
  75.6 1.2 row_sums.1
  76.8 10.6 %all_to_all.34.row_parts = f32[8,8,256]{2,1,0:T(8,128)S(1)} all-to-all(f32[8,8,256]{2,1,0:T(8,128)S(1)} %row_sums.1), channel_id=1, replica_groups=mesh['z'=8,'x_high'=2,'x_low'=2,'tgt'=8] {'tgt'}, dimensions={0} | all-to-all | bytes 131072 | tf_op jit(solution)/shard_map/all_to_all | solution.py:373
  87.4 1.3 col_sums.3
  88.8 1.8 %collective-permute-start.2 = (f32[1,16,256]{2,1,0:T(8,128)S(1)}, f32[1,16,256]{2,1,0:T(8,128)S(1)}, u32[]{:S(2)}, u32[]{:S(2)}) collective-permute-start(f32[1,16,256]{2,1,0:T(8,128)S(1)} %get-tuple-element.55.own), channel_id=1, source_target_pairs={{0,24},{8,16},{16,8},{24,0},{1,25},{9,17},{17,9},{25,1},{2,26},{10... | collective-permute-start | bytes 49160 | tf_op jit(solution)/shard_map/ppermute | solution.py:395
  90.6 2.1 %collective-permute-done.2.other = f32[1,16,256]{2,1,0:T(8,128)S(1)} collective-permute-done((f32[1,16,256]{2,1,0:T(8,128)S(1)}, f32[1,16,256]{2,1,0:T(8,128)S(1)}, u32[]{:S(2)}, u32[]{:S(2)}) %collective-permute-start.2) | collective-permute-done | bytes 16416 | tf_op jit(solution)/shard_map/ppermute | solution.py:395
  92.7 12.3 %all_to_all.35.col_parts = f32[16,16,256]{2,1,0:T(8,128)S(1)} all-to-all(f32[16,16,256]{2,1,0:T(8,128)S(1)} %get-tuple-element.57), channel_id=1, replica_groups=mesh['z'=8,'x_high'=2,'x_low'=2,'tgt'=8] {'z','x_low'}, dimensions={0} | all-to-all | bytes 524288 | tf_op jit(solution)/shard_map/all_to_all | solution.py:373
  105.0 1.0 far.1
  106.0 3.5 %collective-permute-start.3 = (f32[2,264,384]{2,1,0:T(8,128)S(1)}, f32[2,264,384]{2,1,0:T(8,128)S(1)}, u32[]{:S(2)}, u32[]{:S(2)}) collective-permute-start(f32[2,264,384]{2,1,0:T(8,128)S(1)} %get-tuple-element.60), channel_id=1, source_target_pairs={{0,1},{1,0},{2,3},{3,2},{4,5},{5,4},{6,7},{7,6},{8,9},{9,8},{10,11... | collective-permute-start | bytes 2433032 | tf_op jit(solution)/shard_map/ppermute | solution.py:496
  109.5 1.0 side.3
  110.5 1.0 side.2
  111.5 0.1 far_sum.1
  111.7 0.4 collective-permute-start.4
  112.0 0.2 collective-permute-start.5
  112.2 0.3 collective-permute-start.9
  112.5 0.7 collective-permute-start.11
  113.2 0.9 collective-permute-done.4.other_first.other
  114.1 1.2 collective-permute-done.5.other_second.other
  115.2 0.1 near_sum.1
  115.3 0.3 collective-permute-start.6
  115.7 0.7 collective-permute-start.7
  116.4 1.0 end.1
  117.4 1.1 collective-permute-start.8
  118.5 5.6 %collective-permute-done.11.received = f32[264,384]{1,0:T(8,128)S(1)} collective-permute-done((f32[264,384]{1,0:T(8,128)S(1)}, f32[264,384]{1,0:T(8,128)S(1)}, u32[]{:S(2)}, u32[]{:S(2)}) %collective-permute-start.11) | collective-permute-done | bytes 405536 | tf_op jit(solution)/shard_map/ppermute | solution.py:496
  124.1 0.1 relay_sum.3
  124.2 0.1 collective-permute-start.12
  124.3 0.1 relay_sum.2
  124.4 0.9 collective-permute-start.10
  125.3 6.4 %collective-permute-done.6.low = f32[264,384]{1,0:T(8,128)S(1)} collective-permute-done((f32[264,384]{1,0:T(8,128)S(1)}, f32[264,384]{1,0:T(8,128)S(1)}, u32[]{:S(2)}, u32[]{:S(2)}) %collective-permute-start.6) | collective-permute-done | bytes 405536 | tf_op jit(solution)/shard_map/ppermute | solution.py:496
  131.6 1.1 collective-permute-done.7.high
  132.8 0.1 near.1
  132.9 0.6 copy.13
  133.5 0.7 multiply_reduce_fusion
  134.2 0.6 multiply_add_fusion
  134.8 5.5 %collective-permute-done.12.relay_high = f32[264,384]{1,0:T(8,128)S(1)} collective-permute-done((f32[264,384]{1,0:T(8,128)S(1)}, f32[264,384]{1,0:T(8,128)S(1)}, u32[]{:S(2)}, u32[]{:S(2)}) %collective-permute-start.12) | collective-permute-done | bytes 405536 | tf_op jit(solution)/shard_map/ppermute | solution.py:496
  140.3 1.1 collective-permute-done.10.relay_low
  141.5 1.1 finish.1
  (11 shorter events, 0.1 us)
Async XLA Ops:
  23.7 3.9 %collective-permute-start = (f32[1,16,256]{2,1,0:T(8,128)S(1)}, f32[1,16,256]{2,1,0:T(8,128)S(1)}, u32[]{:S(2)}, u32[]{:S(2)}) collective-permute-start(f32[1,16,256]{2,1,0:T(8,128)S(1)} %get-tuple-element.47.own), channel_id=1, source_target_pairs={{0,24},{8,16},{16,8},{24,0},{1,25},{9,17},{17,9},{25,1},{2,26},{10... | collective-permute-start | bytes 49160 | tf_op jit(solution)/shard_map/ppermute | solution.py:395
  59.4 3.9 %collective-permute-start.1 = (f32[1,16,256]{2,1,0:T(8,128)S(1)}, f32[1,16,256]{2,1,0:T(8,128)S(1)}, u32[]{:S(2)}, u32[]{:S(2)}) collective-permute-start(f32[1,16,256]{2,1,0:T(8,128)S(1)} %col_sums.2.own), channel_id=1, source_target_pairs={{0,24},{8,16},{16,8},{24,0},{1,25},{9,17},{17,9},{25,1},{2,26},{10... | collective-permute-start | bytes 49160 | tf_op jit(solution)/shard_map/ppermute | solution.py:395
  88.8 3.9 %collective-permute-start.2 = (f32[1,16,256]{2,1,0:T(8,128)S(1)}, f32[1,16,256]{2,1,0:T(8,128)S(1)}, u32[]{:S(2)}, u32[]{:S(2)}) collective-permute-start(f32[1,16,256]{2,1,0:T(8,128)S(1)} %get-tuple-element.55.own), channel_id=1, source_target_pairs={{0,24},{8,16},{16,8},{24,0},{1,25},{9,17},{17,9},{25,1},{2,26},{10... | collective-permute-start | bytes 49160 | tf_op jit(solution)/shard_map/ppermute | solution.py:395
  106.0 5.5 %collective-permute-start.3 = (f32[2,264,384]{2,1,0:T(8,128)S(1)}, f32[2,264,384]{2,1,0:T(8,128)S(1)}, u32[]{:S(2)}, u32[]{:S(2)}) collective-permute-start(f32[2,264,384]{2,1,0:T(8,128)S(1)} %get-tuple-element.60), channel_id=1, source_target_pairs={{0,1},{1,0},{2,3},{3,2},{4,5},{5,4},{6,7},{7,6},{8,9},{9,8},{10,11... | collective-permute-start | bytes 2433032 | tf_op jit(solution)/shard_map/ppermute | solution.py:496
  111.7 2.4 %collective-permute-start.4 = (f32[2,264,384]{2,1,0:T(8,128)S(1)}, f32[2,264,384]{2,1,0:T(8,128)S(1)}, u32[]{:S(2)}, u32[]{:S(2)}) collective-permute-start(f32[2,264,384]{2,1,0:T(8,128)S(1)} %get-tuple-element.69), channel_id=1, source_target_pairs={{0,1},{1,0},{2,3},{3,2},{4,5},{5,4},{6,7},{7,6},{8,9},{9,8},{10,11... | collective-permute-start | bytes 2433032 | tf_op jit(solution)/shard_map/ppermute | solution.py:496
  112.0 3.2 %collective-permute-start.5 = (f32[2,264,384]{2,1,0:T(8,128)S(1)}, f32[2,264,384]{2,1,0:T(8,128)S(1)}, u32[]{:S(2)}, u32[]{:S(2)}) collective-permute-start(f32[2,264,384]{2,1,0:T(8,128)S(1)} %get-tuple-element.71), channel_id=1, source_target_pairs={{0,1},{1,0},{2,3},{3,2},{4,5},{5,4},{6,7},{7,6},{8,9},{9,8},{10,11... | collective-permute-start | bytes 2433032 | tf_op jit(solution)/shard_map/ppermute | solution.py:496
  112.2 12.0 %collective-permute-start.9 = (f32[264,384]{1,0:T(8,128)S(1)}, f32[264,384]{1,0:T(8,128)S(1)}, u32[]{:S(2)}, u32[]{:S(2)}) collective-permute-start(f32[264,384]{1,0:T(8,128)S(1)} %get-tuple-element.77), channel_id=1, source_target_pairs={{0,2},{1,3},{2,0},{3,1},{4,6},{5,7},{6,4},{7,5},{8,10},{9,11},{10,... | collective-permute-start | bytes 1216520 | tf_op jit(solution)/shard_map/ppermute | solution.py:496
  112.5 11.6 %collective-permute-start.11 = (f32[264,384]{1,0:T(8,128)S(1)}, f32[264,384]{1,0:T(8,128)S(1)}, u32[]{:S(2)}, u32[]{:S(2)}) collective-permute-start(f32[264,384]{1,0:T(8,128)S(1)} %get-tuple-element.78), channel_id=1, source_target_pairs={{0,6},{1,7},{2,4},{3,5},{4,2},{5,3},{6,0},{7,1},{8,14},{9,15},{10,... | collective-permute-start | bytes 1216520 | tf_op jit(solution)/shard_map/ppermute | solution.py:496
  115.3 16.3 %collective-permute-start.6 = (f32[264,384]{1,0:T(8,128)S(1)}, f32[264,384]{1,0:T(8,128)S(1)}, u32[]{:S(2)}, u32[]{:S(2)}) collective-permute-start(f32[264,384]{1,0:T(8,128)S(1)} %get-tuple-element.72), channel_id=1, source_target_pairs={{0,2},{1,3},{2,0},{3,1},{4,6},{5,7},{6,4},{7,5},{8,10},{9,11},{10,... | collective-permute-start | bytes 1216520 | tf_op jit(solution)/shard_map/ppermute | solution.py:496
  115.7 17.1 %collective-permute-start.7 = (f32[264,384]{1,0:T(8,128)S(1)}, f32[264,384]{1,0:T(8,128)S(1)}, u32[]{:S(2)}, u32[]{:S(2)}) collective-permute-start(f32[264,384]{1,0:T(8,128)S(1)} %get-tuple-element.73), channel_id=1, source_target_pairs={{0,6},{1,7},{2,4},{3,5},{4,2},{5,3},{6,0},{7,1},{8,14},{9,15},{10,... | collective-permute-start | bytes 1216520 | tf_op jit(solution)/shard_map/ppermute | solution.py:496
  117.4 16.1 %copy-start = (bf16[2048,768]{1,0:T(8,128)(2,1)S(1)}, bf16[2048,768]{1,0:T(8,128)(2,1)}, u32[]{:S(2)}) copy-start(bf16[2048,768]{1,0:T(8,128)(2,1)} %param.4) | copy-start | bytes 9437188
  117.4 17.4 %collective-permute-start.8 = (f32[2,264,384]{2,1,0:T(8,128)S(1)}, f32[2,264,384]{2,1,0:T(8,128)S(1)}, u32[]{:S(2)}, u32[]{:S(2)}) collective-permute-start(f32[2,264,384]{2,1,0:T(8,128)S(1)} %get-tuple-element.76), channel_id=1, source_target_pairs={{0,1},{1,0},{2,3},{3,2},{4,5},{5,4},{6,7},{7,6},{8,9},{9,8},{10,11... | collective-permute-start | bytes 2433032 | tf_op jit(solution)/shard_map/ppermute | solution.py:496
  124.2 16.2 %collective-permute-start.12 = (f32[264,384]{1,0:T(8,128)S(1)}, f32[264,384]{1,0:T(8,128)S(1)}, u32[]{:S(2)}, u32[]{:S(2)}) collective-permute-start(f32[264,384]{1,0:T(8,128)S(1)} %relay_sum.3), channel_id=1, source_target_pairs={{0,2},{1,3},{2,0},{3,1},{4,6},{5,7},{6,4},{7,5},{8,10},{9,11},{10,... | collective-permute-start | bytes 1216520 | tf_op jit(solution)/shard_map/ppermute | solution.py:496
  124.4 17.1 %collective-permute-start.10 = (f32[264,384]{1,0:T(8,128)S(1)}, f32[264,384]{1,0:T(8,128)S(1)}, u32[]{:S(2)}, u32[]{:S(2)}) collective-permute-start(f32[264,384]{1,0:T(8,128)S(1)} %relay_sum.2), channel_id=1, source_target_pairs={{0,6},{1,7},{2,4},{3,5},{4,2},{5,3},{6,0},{7,1},{8,14},{9,15},{10,... | collective-permute-start | bytes 1216520 | tf_op jit(solution)/shard_map/ppermute | solution.py:496

commit v7 on v6

--- a/solution.py
+++ b/solution.py
@@ -198,7 +198,7 @@
     peaks[...] = jnp.full(peaks.shape, NEGATIVE, jnp.float32)
     sums[...] = jnp.zeros(sums.shape, jnp.float32)
 
-    @pl.loop(0, src_blocks)
+    @pl.loop(0, src_blocks, unroll=2)
     def _(b):
         shift = along_rows(row_lse[pl.ds(b, 1), :])
         for k in range(slots):
@@ -220,7 +220,7 @@
 
 
 def row_totals(table, tile, totals, src_blocks, slots):
-    @pl.loop(0, src_blocks)
+    @pl.loop(0, src_blocks, unroll=2)
     def _(b):
         total = None
         for k in range(slots):
@@ -249,7 +249,7 @@
     row_scale[...] = share / add_parts(row_parts[...])
     sums[...] = jnp.zeros(sums.shape, jnp.float32)
 
-    @pl.loop(0, src_blocks)
+    @pl.loop(0, src_blocks, unroll=2)
     def _(b):
         scale = along_rows(row_scale[pl.ds(b, 1), :])
         for k in range(slots):

time: 143 us -> 141 us (0.986)
  Pallas kernels: 23.9 us -> 22.3 us
where the time goes in v7:
time: 141 us
  blocking collectives  74.2 us (53%)
  waiting for transfers between devices  26 us (18%)
  Pallas kernels  22.3 us (16%)
  starting transfers between devices  15.8 us (11%)
    all_to_all x6, blocking collectives, exchange(): return in_vmem(lax.all_to_all(copies, axis, 0, 0))  74.2 us
    ppermute x10, waiting for transfers between devices, send(): return lax.ppermute(x, 'tgt', [(t, t ^ flip) for t in range(n_tgt)])  21.8 us
    pallas_call x1, Pallas kernels, local(): pl.pallas_call(functools.partial(cost_kernel, features=features), in_spec...  9.12 us
    ppermute x10, starting transfers between devices, send(): return lax.ppermute(x, 'tgt', [(t, t ^ flip) for t in range(n_tgt)])  8.24 us
    ppermute x3, starting transfers between devices, exchange_cols(): lax.ppermute(in_vmem(cols), X_AXES, pairs)  7.53 us
    pallas_call x9, Pallas kernels, call(): pl.pallas_call(kernel, in_specs=[spec] + [VMEM] * (len(operands) - 1), ou...  4.46 us
    ppermute x3, waiting for transfers between devices, exchange_cols(): lax.ppermute(in_vmem(cols), X_AXES, pairs)  4.16 us
  transfers between devices with their start and end apart: 13, of which 10 were waited for; matrix products, arithmetic and copies ran while one was open for 1% of the time, Pallas kernels for 2%

profile of v7, /device:TPU:1, one launch (start us, length us, event | category | flops | bytes accessed | tf_op | source)
XLA Modules:
  0.0 141.2 jit_solution(618633907573698417)
XLA Ops:
  0.6 9.1 %cost.1 = (bf16[16,256,768]{2,1,0:T(8,128)(2,1)S(1)}, f32[9,4,256,256]{3,2,1,0:T(8,128)S(1)}, f32[8,8,256]{2,1,0:T(8,128)S(1)}, s32[32]{0:T(128)S(4)}) custom-call(s32[4,8]{1,0:T(4,128)} %bitcast.16, s32[1,8]{1,0:T(1,128)} %bitcast.17, bf16[8,256,768]{2,1,0:T(8,128)(2,1)} %bitcast.12, bf16[16,256,768]{2,1,0:T(8,128)(2,1)} %bitcast.13), custom_call_target="tpu_custom_call" | custom-call | tf_op jit(solution)/shard_map/cost/pallas_call | solution.py:415
  9.8 10.6 %all_to_all.30.row_parts = f32[8,8,256]{2,1,0:T(8,128)S(1)} all-to-all(f32[8,8,256]{2,1,0:T(8,128)S(1)} %get-tuple-element.46), channel_id=1, replica_groups=mesh['z'=8,'x_high'=2,'x_low'=2,'tgt'=8] {'tgt'}, dimensions={0} | all-to-all | bytes 131072 | tf_op jit(solution)/shard_map/all_to_all | solution.py:373
  20.4 2.8 %first_col.1 = (f32[9,4,256,256]{3,2,1,0:T(8,128)S(1)}, f32[1,16,256]{2,1,0:T(8,128)S(1)}) custom-call(s32[32]{0:T(128)S(4)} %get-tuple-element.44.table, f32[9,4,256,256]{3,2,1,0:T(8,128)S(1)} %get-tuple-element.45.z_ref, f32[8,8,256]{2,1,0:T(8,128)S(1)} %all_to_all.30.row_parts), custom_call_target="tpu_custom_call", output_to_operand_aliasing={{0}: (1, {})} | custom-call | tf_op jit(solution)/shard_map/first_col/pallas_call | solution.py:441
  23.2 2.8 %collective-permute-start = (f32[1,16,256]{2,1,0:T(8,128)S(1)}, f32[1,16,256]{2,1,0:T(8,128)S(1)}, u32[]{:S(2)}, u32[]{:S(2)}) collective-permute-start(f32[1,16,256]{2,1,0:T(8,128)S(1)} %get-tuple-element.47.own), channel_id=1, source_target_pairs={{0,24},{8,16},{16,8},{24,0},{1,25},{9,17},{17,9},{25,1},{2,26},{10... | collective-permute-start | bytes 49160 | tf_op jit(solution)/shard_map/ppermute | solution.py:395
  26.0 1.1 collective-permute-done.other
  27.1 17.7 %all_to_all.31.col_parts = f32[16,16,256]{2,1,0:T(8,128)S(1)} all-to-all(f32[16,16,256]{2,1,0:T(8,128)S(1)} %get-tuple-element.50), channel_id=1, replica_groups=mesh['z'=8,'x_high'=2,'x_low'=2,'tgt'=8] {'z','x_low'}, dimensions={0} | all-to-all | bytes 524288 | tf_op jit(solution)/shard_map/all_to_all | solution.py:373
  44.9 1.8 %first_row.1 = (f32[9,4,256,256]{3,2,1,0:T(8,128)S(1)}, f32[8,8,256]{2,1,0:T(8,128)S(1)}) custom-call(s32[32]{0:T(128)S(4)} %get-tuple-element.44.table, f32[9,4,256,256]{3,2,1,0:T(8,128)S(1)} %get-tuple-element.49.w_ref, f32[16,16,256]{2,1,0:T(8,128)S(1)} %all_to_all.31.col_parts), custom_call_target="tpu_custom_call", output_to_operand_aliasing={{0}: (1, {})} | custom-call | tf_op jit(solution)/shard_map/first_row/pallas_call | solution.py:453
  46.7 10.7 %all_to_all.32.row_parts = f32[8,8,256]{2,1,0:T(8,128)S(1)} all-to-all(f32[8,8,256]{2,1,0:T(8,128)S(1)} %get-tuple-element.52), channel_id=1, replica_groups=mesh['z'=8,'x_high'=2,'x_low'=2,'tgt'=8] {'tgt'}, dimensions={0} | all-to-all | bytes 131072 | tf_op jit(solution)/shard_map/all_to_all | solution.py:373
  57.4 1.0 col_sums.2.own
  58.4 2.7 %collective-permute-start.1 = (f32[1,16,256]{2,1,0:T(8,128)S(1)}, f32[1,16,256]{2,1,0:T(8,128)S(1)}, u32[]{:S(2)}, u32[]{:S(2)}) collective-permute-start(f32[1,16,256]{2,1,0:T(8,128)S(1)} %col_sums.2.own), channel_id=1, source_target_pairs={{0,24},{8,16},{16,8},{24,0},{1,25},{9,17},{17,9},{25,1},{2,26},{10... | collective-permute-start | bytes 49160 | tf_op jit(solution)/shard_map/ppermute | solution.py:395
  61.1 1.2 collective-permute-done.1.other
  62.3 12.3 %all_to_all.33.col_parts = f32[16,16,256]{2,1,0:T(8,128)S(1)} all-to-all(f32[16,16,256]{2,1,0:T(8,128)S(1)} %get-tuple-element.54), channel_id=1, replica_groups=mesh['z'=8,'x_high'=2,'x_low'=2,'tgt'=8] {'z','x_low'}, dimensions={0} | all-to-all | bytes 524288 | tf_op jit(solution)/shard_map/all_to_all | solution.py:373
  74.6 0.9 row_sums.1
  75.5 10.6 %all_to_all.34.row_parts = f32[8,8,256]{2,1,0:T(8,128)S(1)} all-to-all(f32[8,8,256]{2,1,0:T(8,128)S(1)} %row_sums.1), channel_id=1, replica_groups=mesh['z'=8,'x_high'=2,'x_low'=2,'tgt'=8] {'tgt'}, dimensions={0} | all-to-all | bytes 131072 | tf_op jit(solution)/shard_map/all_to_all | solution.py:373
  86.1 1.0 col_sums.3
  87.1 2.1 %collective-permute-start.2 = (f32[1,16,256]{2,1,0:T(8,128)S(1)}, f32[1,16,256]{2,1,0:T(8,128)S(1)}, u32[]{:S(2)}, u32[]{:S(2)}) collective-permute-start(f32[1,16,256]{2,1,0:T(8,128)S(1)} %get-tuple-element.55.own), channel_id=1, source_target_pairs={{0,24},{8,16},{16,8},{24,0},{1,25},{9,17},{17,9},{25,1},{2,26},{10... | collective-permute-start | bytes 49160 | tf_op jit(solution)/shard_map/ppermute | solution.py:395
  89.2 1.8 %collective-permute-done.2.other = f32[1,16,256]{2,1,0:T(8,128)S(1)} collective-permute-done((f32[1,16,256]{2,1,0:T(8,128)S(1)}, f32[1,16,256]{2,1,0:T(8,128)S(1)}, u32[]{:S(2)}, u32[]{:S(2)}) %collective-permute-start.2) | collective-permute-done | bytes 16416 | tf_op jit(solution)/shard_map/ppermute | solution.py:395
  91.0 12.3 %all_to_all.35.col_parts = f32[16,16,256]{2,1,0:T(8,128)S(1)} all-to-all(f32[16,16,256]{2,1,0:T(8,128)S(1)} %get-tuple-element.57), channel_id=1, replica_groups=mesh['z'=8,'x_high'=2,'x_low'=2,'tgt'=8] {'z','x_low'}, dimensions={0} | all-to-all | bytes 524288 | tf_op jit(solution)/shard_map/all_to_all | solution.py:373
  103.3 1.0 far.1
  104.3 3.5 %collective-permute-start.3 = (f32[2,264,384]{2,1,0:T(8,128)S(1)}, f32[2,264,384]{2,1,0:T(8,128)S(1)}, u32[]{:S(2)}, u32[]{:S(2)}) collective-permute-start(f32[2,264,384]{2,1,0:T(8,128)S(1)} %get-tuple-element.60), channel_id=1, source_target_pairs={{0,1},{1,0},{2,3},{3,2},{4,5},{5,4},{6,7},{7,6},{8,9},{9,8},{10,11... | collective-permute-start | bytes 2433032 | tf_op jit(solution)/shard_map/ppermute | solution.py:496
  107.8 1.0 side.3
  108.8 1.0 side.2
  109.8 0.1 far_sum.1
  110.0 0.4 collective-permute-start.4
  110.3 0.2 collective-permute-start.5
  110.6 0.3 collective-permute-start.9
  110.9 0.7 collective-permute-start.11
  111.6 0.8 collective-permute-done.4.other_first.other
  112.4 1.2 collective-permute-done.5.other_second.other
  113.5 0.1 near_sum.1
  113.6 0.4 collective-permute-start.6
  114.0 0.7 collective-permute-start.7
  114.7 1.0 end.1
  115.8 1.0 collective-permute-start.8
  116.8 5.7 %collective-permute-done.11.received = f32[264,384]{1,0:T(8,128)S(1)} collective-permute-done((f32[264,384]{1,0:T(8,128)S(1)}, f32[264,384]{1,0:T(8,128)S(1)}, u32[]{:S(2)}, u32[]{:S(2)}) %collective-permute-start.11) | collective-permute-done | bytes 405536 | tf_op jit(solution)/shard_map/ppermute | solution.py:496
  122.5 0.1 relay_sum.3
  122.5 0.1 collective-permute-start.12
  122.7 0.1 relay_sum.2
  122.7 0.9 collective-permute-start.10
  123.6 6.3 %collective-permute-done.6.low = f32[264,384]{1,0:T(8,128)S(1)} collective-permute-done((f32[264,384]{1,0:T(8,128)S(1)}, f32[264,384]{1,0:T(8,128)S(1)}, u32[]{:S(2)}, u32[]{:S(2)}) %collective-permute-start.6) | collective-permute-done | bytes 405536 | tf_op jit(solution)/shard_map/ppermute | solution.py:496
  129.9 1.2 collective-permute-done.7.high
  131.2 0.1 near.1
  131.2 0.6 copy.13
  131.9 0.7 multiply_reduce_fusion
  132.6 0.6 multiply_add_fusion
  133.2 5.5 %collective-permute-done.12.relay_high = f32[264,384]{1,0:T(8,128)S(1)} collective-permute-done((f32[264,384]{1,0:T(8,128)S(1)}, f32[264,384]{1,0:T(8,128)S(1)}, u32[]{:S(2)}, u32[]{:S(2)}) %collective-permute-start.12) | collective-permute-done | bytes 405536 | tf_op jit(solution)/shard_map/ppermute | solution.py:496
  138.6 1.2 collective-permute-done.10.relay_low
  139.8 1.1 finish.1
  (11 shorter events, 0.1 us)
Async XLA Ops:
  23.2 3.9 %collective-permute-start = (f32[1,16,256]{2,1,0:T(8,128)S(1)}, f32[1,16,256]{2,1,0:T(8,128)S(1)}, u32[]{:S(2)}, u32[]{:S(2)}) collective-permute-start(f32[1,16,256]{2,1,0:T(8,128)S(1)} %get-tuple-element.47.own), channel_id=1, source_target_pairs={{0,24},{8,16},{16,8},{24,0},{1,25},{9,17},{17,9},{25,1},{2,26},{10... | collective-permute-start | bytes 49160 | tf_op jit(solution)/shard_map/ppermute | solution.py:395
  58.4 3.9 %collective-permute-start.1 = (f32[1,16,256]{2,1,0:T(8,128)S(1)}, f32[1,16,256]{2,1,0:T(8,128)S(1)}, u32[]{:S(2)}, u32[]{:S(2)}) collective-permute-start(f32[1,16,256]{2,1,0:T(8,128)S(1)} %col_sums.2.own), channel_id=1, source_target_pairs={{0,24},{8,16},{16,8},{24,0},{1,25},{9,17},{17,9},{25,1},{2,26},{10... | collective-permute-start | bytes 49160 | tf_op jit(solution)/shard_map/ppermute | solution.py:395
  87.1 3.9 %collective-permute-start.2 = (f32[1,16,256]{2,1,0:T(8,128)S(1)}, f32[1,16,256]{2,1,0:T(8,128)S(1)}, u32[]{:S(2)}, u32[]{:S(2)}) collective-permute-start(f32[1,16,256]{2,1,0:T(8,128)S(1)} %get-tuple-element.55.own), channel_id=1, source_target_pairs={{0,24},{8,16},{16,8},{24,0},{1,25},{9,17},{17,9},{25,1},{2,26},{10... | collective-permute-start | bytes 49160 | tf_op jit(solution)/shard_map/ppermute | solution.py:395
  104.3 5.5 %collective-permute-start.3 = (f32[2,264,384]{2,1,0:T(8,128)S(1)}, f32[2,264,384]{2,1,0:T(8,128)S(1)}, u32[]{:S(2)}, u32[]{:S(2)}) collective-permute-start(f32[2,264,384]{2,1,0:T(8,128)S(1)} %get-tuple-element.60), channel_id=1, source_target_pairs={{0,1},{1,0},{2,3},{3,2},{4,5},{5,4},{6,7},{7,6},{8,9},{9,8},{10,11... | collective-permute-start | bytes 2433032 | tf_op jit(solution)/shard_map/ppermute | solution.py:496
  110.0 2.4 %collective-permute-start.4 = (f32[2,264,384]{2,1,0:T(8,128)S(1)}, f32[2,264,384]{2,1,0:T(8,128)S(1)}, u32[]{:S(2)}, u32[]{:S(2)}) collective-permute-start(f32[2,264,384]{2,1,0:T(8,128)S(1)} %get-tuple-element.69), channel_id=1, source_target_pairs={{0,1},{1,0},{2,3},{3,2},{4,5},{5,4},{6,7},{7,6},{8,9},{9,8},{10,11... | collective-permute-start | bytes 2433032 | tf_op jit(solution)/shard_map/ppermute | solution.py:496
  110.3 3.2 %collective-permute-start.5 = (f32[2,264,384]{2,1,0:T(8,128)S(1)}, f32[2,264,384]{2,1,0:T(8,128)S(1)}, u32[]{:S(2)}, u32[]{:S(2)}) collective-permute-start(f32[2,264,384]{2,1,0:T(8,128)S(1)} %get-tuple-element.71), channel_id=1, source_target_pairs={{0,1},{1,0},{2,3},{3,2},{4,5},{5,4},{6,7},{7,6},{8,9},{9,8},{10,11... | collective-permute-start | bytes 2433032 | tf_op jit(solution)/shard_map/ppermute | solution.py:496
  110.6 12.1 %collective-permute-start.9 = (f32[264,384]{1,0:T(8,128)S(1)}, f32[264,384]{1,0:T(8,128)S(1)}, u32[]{:S(2)}, u32[]{:S(2)}) collective-permute-start(f32[264,384]{1,0:T(8,128)S(1)} %get-tuple-element.77), channel_id=1, source_target_pairs={{0,2},{1,3},{2,0},{3,1},{4,6},{5,7},{6,4},{7,5},{8,10},{9,11},{10,... | collective-permute-start | bytes 1216520 | tf_op jit(solution)/shard_map/ppermute | solution.py:496
  110.9 11.6 %collective-permute-start.11 = (f32[264,384]{1,0:T(8,128)S(1)}, f32[264,384]{1,0:T(8,128)S(1)}, u32[]{:S(2)}, u32[]{:S(2)}) collective-permute-start(f32[264,384]{1,0:T(8,128)S(1)} %get-tuple-element.78), channel_id=1, source_target_pairs={{0,6},{1,7},{2,4},{3,5},{4,2},{5,3},{6,0},{7,1},{8,14},{9,15},{10,... | collective-permute-start | bytes 1216520 | tf_op jit(solution)/shard_map/ppermute | solution.py:496
  113.6 16.3 %collective-permute-start.6 = (f32[264,384]{1,0:T(8,128)S(1)}, f32[264,384]{1,0:T(8,128)S(1)}, u32[]{:S(2)}, u32[]{:S(2)}) collective-permute-start(f32[264,384]{1,0:T(8,128)S(1)} %get-tuple-element.72), channel_id=1, source_target_pairs={{0,2},{1,3},{2,0},{3,1},{4,6},{5,7},{6,4},{7,5},{8,10},{9,11},{10,... | collective-permute-start | bytes 1216520 | tf_op jit(solution)/shard_map/ppermute | solution.py:496
  114.0 17.1 %collective-permute-start.7 = (f32[264,384]{1,0:T(8,128)S(1)}, f32[264,384]{1,0:T(8,128)S(1)}, u32[]{:S(2)}, u32[]{:S(2)}) collective-permute-start(f32[264,384]{1,0:T(8,128)S(1)} %get-tuple-element.73), channel_id=1, source_target_pairs={{0,6},{1,7},{2,4},{3,5},{4,2},{5,3},{6,0},{7,1},{8,14},{9,15},{10,... | collective-permute-start | bytes 1216520 | tf_op jit(solution)/shard_map/ppermute | solution.py:496
  115.8 16.1 %copy-start = (bf16[2048,768]{1,0:T(8,128)(2,1)S(1)}, bf16[2048,768]{1,0:T(8,128)(2,1)}, u32[]{:S(2)}) copy-start(bf16[2048,768]{1,0:T(8,128)(2,1)} %param.4) | copy-start | bytes 9437188
  115.8 17.4 %collective-permute-start.8 = (f32[2,264,384]{2,1,0:T(8,128)S(1)}, f32[2,264,384]{2,1,0:T(8,128)S(1)}, u32[]{:S(2)}, u32[]{:S(2)}) collective-permute-start(f32[2,264,384]{2,1,0:T(8,128)S(1)} %get-tuple-element.76), channel_id=1, source_target_pairs={{0,1},{1,0},{2,3},{3,2},{4,5},{5,4},{6,7},{7,6},{8,9},{9,8},{10,11... | collective-permute-start | bytes 2433032 | tf_op jit(solution)/shard_map/ppermute | solution.py:496
  122.5 16.1 %collective-permute-start.12 = (f32[264,384]{1,0:T(8,128)S(1)}, f32[264,384]{1,0:T(8,128)S(1)}, u32[]{:S(2)}, u32[]{:S(2)}) collective-permute-start(f32[264,384]{1,0:T(8,128)S(1)} %relay_sum.3), channel_id=1, source_target_pairs={{0,2},{1,3},{2,0},{3,1},{4,6},{5,7},{6,4},{7,5},{8,10},{9,11},{10,... | collective-permute-start | bytes 1216520 | tf_op jit(solution)/shard_map/ppermute | solution.py:496
  122.7 17.1 %collective-permute-start.10 = (f32[264,384]{1,0:T(8,128)S(1)}, f32[264,384]{1,0:T(8,128)S(1)}, u32[]{:S(2)}, u32[]{:S(2)}) collective-permute-start(f32[264,384]{1,0:T(8,128)S(1)} %relay_sum.2), channel_id=1, source_target_pairs={{0,6},{1,7},{2,4},{3,5},{4,2},{5,3},{6,0},{7,1},{8,14},{9,15},{10,... | collective-permute-start | bytes 1216520 | tf_op jit(solution)/shard_map/ppermute | solution.py:496
